TPU v7x, 128 devices: a whole 4x4x4 slice. The times are simulated.
128 devices in a mesh: pt: 8 (over y, core), cl: 16 (over z, x).
Axes of the slice: x: 4, y: 4, z: 4, core: 2. Of those that a mesh axis runs over, the one named last changes fastest.
Arguments:
- cam_jac: float32 [2, 4, 2, 9, 32768], P(None, None, None, None, ('pt', 'cl')), may hold values from -160 to 160
- pt_jac: float32 [2, 4, 2, 3, 32768], P(None, None, None, None, ('pt', 'cl')), may hold values from -40 to 40
- residual: float32 [2, 4, 2, 32768], P(None, None, None, ('pt', 'cl')), may hold values from -48 to 48
- cam_ids: int32 [2, 4, 32768], P(None, None, ('pt', 'cl')), may hold values from 0 to 127, as said below
- obs_count: int32 [2, 32768], P(None, ('pt', 'cl')), may hold values from 1 to 4
- clusters: int32 [32768, 2], P(('pt', 'cl')), may hold values from 0 to 15, as said below
- owner_map: int32 [16], replicated, may hold values from 0 to 15, each once
- prev_step: float32 [16, 9, 128], replicated, may hold values from -6 to 6
- damping: float32 [1], replicated, may hold values from 0.5 to 2
Outputs:
- camera_step: float32 [16, 9, 128], P('cl')
- point_step: float32 [3, 32768], P(None, ('pt', 'cl'))
Inputs may be any that keep to these rules, and one draw needn't show every extreme that they name: Each point names two different clusters. Among the 256 points of one device no cluster is named by more than 64 points, and one cluster is named by exactly 64 points of every device. `cam_ids`: in each cluster, the 4 slots of a point name 4 consecutive cameras in slot order, counted cyclically modulo 128.
All inputs are finite; a program needn't handle non-finite values.
Results may differ from a plain program's by a relative error of at most 0.0003.
Values sent between devices are 32-bit elements; how exact they have to be, the bound alone decides.
No kernel may reach another device: no remote copies, remote signals or barrier semaphores. Data moves between devices by JAX's collectives and lax.ppermute only.
A program may use at most 128 MiB of HBM per device.

v0:
```python
import jax
import jax.numpy as jnp
from jax import lax
from jax.sharding import PartitionSpec as P

highest = lax.Precision.HIGHEST


def lower_solve(factor, first, second, third):
    diag_one, low_ba, low_ca, diag_two, low_cb, diag_three = factor
    out_one = first / diag_one
    out_two = (second - low_ba * out_one) / diag_two
    out_three = (third - low_ca * out_one - low_cb * out_two) / diag_three
    return (out_one, out_two, out_three)


def upper_solve(factor, first, second, third):
    diag_one, low_ba, low_ca, diag_two, low_cb, diag_three = factor
    out_three = third / diag_three
    out_two = (second - low_cb * out_three) / diag_two
    out_one = (first - low_ba * out_two - low_ca * out_three) / diag_one
    return (out_one, out_two, out_three)


def point_terms(cam_jac, pt_jac, residual, cam_ids, obs_count, clusters, prev_step, damping):
    slots = cam_jac.shape[1]
    params = prev_step.shape[1]
    cams = prev_step.shape[2]
    live = (jnp.arange(slots, dtype=jnp.int32)[None, :, None] < obs_count[:, None, :]).astype(
        jnp.float32
    )
    jac_cam = cam_jac * live[:, :, None, None, :]
    jac_point = pt_jac * live[:, :, None, None, :]
    resid = residual * live[:, :, None, :]
    normal = jnp.einsum("skmap,skmbp->abp", jac_point, jac_point, precision=highest)
    normal = normal + damping[0] * jnp.eye(3, dtype=jnp.float32)[:, :, None]
    diag_one = jnp.sqrt(normal[0, 0])
    low_ba = normal[1, 0] / diag_one
    low_ca = normal[2, 0] / diag_one
    diag_two = jnp.sqrt(normal[1, 1] - low_ba * low_ba)
    low_cb = (normal[2, 1] - low_ca * low_ba) / diag_two
    diag_three = jnp.sqrt(normal[2, 2] - low_ca * low_ca - low_cb * low_cb)
    factor = (diag_one, low_ba, low_ca, diag_two, low_cb, diag_three)
    coupling = jnp.einsum("skmip,skmap->skiap", jac_cam, jac_point, precision=highest)
    coeffs = jnp.stack(
        lower_solve(factor, coupling[:, :, :, 0], coupling[:, :, :, 1], coupling[:, :, :, 2]),
        axis=3,
    )
    grad_point = jnp.einsum("skmap,skmp->ap", jac_point, resid, precision=highest)
    reduced = jnp.stack(lower_solve(factor, grad_point[0], grad_point[1], grad_point[2]), axis=0)
    flat_prev = prev_step.transpose(1, 0, 2).reshape(params, -1)
    lookup = clusters.T[:, None, :] * cams + cam_ids
    prev_cols = jnp.moveaxis(flat_prev[:, lookup], 0, 2)
    carried = jnp.einsum("skiap,skip->sap", coeffs, prev_cols, precision=highest)
    mixed = reduced[None] + carried[::-1]
    rhs_terms = jnp.einsum("skiap,sap->skip", coeffs, mixed, precision=highest) - jnp.einsum(
        "skmip,skmp->skip", jac_cam, resid, precision=highest
    )
    return (jac_cam, coeffs, rhs_terms, factor, reduced)


def point_update(coeffs, factor, reduced, flat_steps, lookup):
    step_cols = jnp.moveaxis(flat_steps[:, lookup], 0, 2)
    total = reduced + jnp.einsum("skiap,skip->ap", coeffs, step_cols, precision=highest)
    solved = upper_solve(factor, total[0], total[1], total[2])
    return -jnp.stack(solved, axis=0)


def per_device(
    cam_jac, pt_jac, residual, cam_ids, obs_count, clusters, owner_map, prev_step, damping
):
    params = prev_step.shape[1]
    cams = prev_step.shape[2]
    order = params * cams
    slots = cam_jac.shape[1]
    npts = cam_jac.shape[-1]
    groups = lax.axis_size("cl")
    capacity = npts // 4
    jac_cam, coeffs, rhs_terms, factor, reduced = point_terms(
        cam_jac, pt_jac, residual, cam_ids, obs_count, clusters, prev_step, damping
    )
    packed = jnp.concatenate(
        [
            jac_cam.reshape(2, slots * 2 * params, npts),
            coeffs.reshape(2, slots * params * 3, npts),
            rhs_terms.reshape(2, slots * params, npts),
        ],
        axis=1,
    )
    packed = packed.transpose(1, 0, 2).reshape(-1, 2 * npts)
    cam_flat = cam_ids.transpose(1, 0, 2).reshape(slots, 2 * npts)
    target_dev = owner_map[clusters.T].reshape(2 * npts)
    onehot = (target_dev[:, None] == jnp.arange(groups, dtype=jnp.int32)[None, :]).astype(jnp.int32)
    earlier = jnp.cumsum(onehot, axis=0) - onehot
    position = jnp.sum(earlier * onehot, axis=1)
    target = target_dev * capacity + position
    send_float = (
        jnp.zeros((packed.shape[0], groups * capacity), jnp.float32).at[:, target].set(packed)
    )
    send_int = jnp.zeros((slots, groups * capacity), jnp.int32).at[:, target].set(cam_flat)
    recv_float, recv_int = (
        lax.all_to_all(send_float, "cl", split_axis=1, concat_axis=1, tiled=True),
        lax.all_to_all(send_int, "cl", split_axis=1, concat_axis=1, tiled=True),
    )
    seen = recv_float.shape[1]
    jac_recv = recv_float[: slots * 2 * params].reshape(slots, 2, params, seen)
    coef_recv = recv_float[slots * 2 * params : slots * 5 * params].reshape(slots, params, 3, seen)
    term_recv = recv_float[slots * 5 * params :].reshape(slots, params, seen)
    camera_hot = (recv_int[:, None, :] == jnp.arange(cams, dtype=jnp.int32)[None, :, None]).astype(
        jnp.float32
    )
    spread = jnp.einsum("kcs,kirs->rics", camera_hot, coef_recv, precision=highest)
    self_gram = jnp.einsum("kmis,kmjs->kijs", jac_recv, jac_recv, precision=highest)
    diag_vals = jnp.einsum("kcs,kijs->ijc", camera_hot, self_gram, precision=highest)
    rhs_part = jnp.einsum("kcs,kis->ic", camera_hot, term_recv, precision=highest)
    cam_eye = jnp.eye(cams, dtype=jnp.float32)
    blockdiag = (diag_vals.transpose(0, 2, 1)[:, :, :, None] * cam_eye[None, :, None, :]).reshape(
        order, order
    )
    flat_spread = spread.reshape(3, order, seen)
    partial_value = blockdiag - jnp.einsum(
        "ras,rbs->ab", flat_spread, flat_spread, precision=highest
    )
    total, right_side = lax.psum((partial_value, rhs_part), "pt")
    total = total + damping[0] * jnp.eye(order, dtype=jnp.float32)
    chol = jnp.linalg.cholesky(total)
    step = jax.scipy.linalg.cho_solve((chol, True), right_side.reshape(order)).reshape(params, cams)
    every_step = lax.all_gather(step[None], "cl", axis=0, tiled=True)
    flat_steps = every_step.transpose(1, 0, 2).reshape(params, -1)
    lookup = owner_map[clusters.T][:, None, :] * cams + cam_ids
    point_step = point_update(coeffs, factor, reduced, flat_steps, lookup)
    return (step[None], point_step)


def solution(mesh):
    in_specs = (
        P(None, None, None, None, ("pt", "cl")),
        P(None, None, None, None, ("pt", "cl")),
        P(None, None, None, ("pt", "cl")),
        P(None, None, ("pt", "cl")),
        P(None, ("pt", "cl")),
        P(("pt", "cl"), None),
        P(),
        P(),
        P(),
    )
    out_specs = (P("cl", None, None), P(None, ("pt", "cl")))
    return jax.shard_map(
        per_device, mesh=mesh, in_specs=in_specs, out_specs=out_specs, check_vma=False
    )
```

profile of v0, /device:TPU:0, one launch (start us, length us, event | category | flops | bytes accessed | tf_op | source)
XLA Modules:
  0.0 843.9 jit_solution(1181235680940530914)
XLA Ops:
  7.9 3.3 gather_fusion
  16.5 8.1 all-to-all-start.1
  28.2 2.3 copy.193
  30.8 2.3 copy.194
  34.0 4.0 fusion.8
  38.0 6.4 slice_reduce_fusion
  44.4 18.3 %fusion.170 = f32[2,4,256,3,9]{4,3,2,1,0:T(4,128)} fusion(f32[2,4,2,3,256]{3,2,4,1,0:T(2,128)S(1)} %copy-done.3, f32[2,4,2,9,256]{3,2,4,1,0:T(2,128)S(1)} %copy-done.4), kind=kOutput, calls=%fused_computation.392 | convolution fusion | flops 1327104 | bytes 417792 | tf_op jit(solution)/shard_map/skmip,skmap->skiap/dot_general | solution.py:44
  62.7 3.4 copy.195
  67.4 5.5 gather_fusion.1
  75.1 3.3 scatter_custom_fusion
  79.0 7.3 all-to-all-start
  90.6 12.6 %all-to-all-done = f32[216,16,64]{0,2,1:T(8,128)S(1)} async-done(((f32[216,16,64]{0,2,1:T(8,128)}), f32[216,16,64]{0,2,1:T(8,128)S(1)}, u32[]{:S(2)}, u32[]{:S(2)}) %all-to-all-start) | async-done | bytes 884768 | tf_op jit(solution)/shard_map/all_to_all | solution.py:102
  103.8 4.4 copy.202
  108.2 57.3 %convolution_bitcast_fusion = f32[4,9,9,1024]{1,2,3,0:T(8,128)} fusion(f32[4,2,9,1024]{2,1,3,0:T(2,128)} %copy.202), kind=kOutput, calls=%fused_computation.7 | convolution fusion | flops 7962624 | bytes 1622016 | tf_op jit(solution)/shard_map/kmis,kmjs->kijs/dot_general | solution.py:113
  165.5 19.5 %copy.207 = f32[4,9,9,1024]{3,2,0,1:T(8,128)S(1)} copy(f32[4,9,9,1024]{1,2,3,0:T(8,128)} %convolution_bitcast_fusion) | data formatting | bytes 2654208 | tf_op jit(solution)/shard_map/kmis,kmjs->kijs/transpose | solution.py:113
  185.1 2.8 convolution_bitcast_fusion.4
  189.0 2.9 broadcast_multiply_fusion
  191.9 4.9 copy.304
  196.9 6.9 copy.213
  204.8 5.2 copy.210
  210.0 25.2 %convolution_bitcast_fusion.2 = f32[3,9,128,1024]{2,1,0,3:T(8,128)} fusion(f32[4,9,3,1024]{1,0,2,3:T(4,128)} %copy.210, pred[4,128,1024,1]{1,0,3,2:T(4,128)(4,1)S(1)} %copy-done.5), kind=kOutput, calls=%fused_computation.10 | convolution fusion | flops 169869312 | bytes 15122432 | tf_op jit(solution)/shard_map/kcs,kirs->rics/dot_general | solution.py:112
  235.2 21.5 %copy.212 = f32[3,9,128,1024]{3,2,1,0:T(8,128)} copy(f32[3,9,128,1024]{2,1,0,3:T(8,128)} %convolution_bitcast_fusion.2) | data formatting | bytes 28311552 | tf_op jit(solution)/shard_map/kcs,kirs->rics/transpose | solution.py:112
  256.8 63.6 %fusion = f32[1152,1152]{0,1:T(8,128)} fusion(f32[1152,1152]{0,1:T(8,128)} %copy.213, f32[3,1152,1024]{2,1,0:T(8,128)} %bitcast.549), kind=kOutput, calls=%fused_computation.9 | convolution fusion | flops 48923688960 | bytes 24772608 | tf_op jit(solution)/shard_map/ras,rbs->ab/dot_general | solution.py:121
  322.2 13.0 %psum.15 = f32[9,128]{1,0:T(8,128)S(1)} all-reduce(f32[9,128]{1,0:T(8,128)S(1)} %fusion.21), channel_id=1, replica_groups=mesh['pt'=8,'cl'=16] {'pt'}, use_global_device_ids=true, to_apply=%region_24.25 | all-reduce | flops 1152 | bytes 9216 | tf_op jit(solution)/shard_map/psum | solution.py:124
  335.2 59.7 %all-reduce.3.cloned.1.call-done = f32[1152,1152]{0,1:T(8,128)} async-done(((f32[1152,1152]{0,1:T(8,128)}), f32[1152,1152]{0,1:T(8,128)}) %all-reduce.3.cloned.1.call-update) | async-done | bytes 5308432 | tf_op jit(solution)/shard_map/psum | solution.py:124
  394.9 5.2 select_add_fusion
  400.1 7.2 copy.215
  407.3 4.6 fusion.1
  412.0 2.3 copy-done.2
  414.3 11.7 %cholesky.253 = f32[128,128]{1,0:T(8,128)S(1)} custom-call(f32[128,128]{1,0:T(8,128)S(1)} %cholesky.661), custom_call_target="Cholesky" | custom-call | tf_op jit(solution)/shard_map/jit(cholesky)/cholesky | solution.py:126
  426.0 9.8 %custom-call.74 = f32[1,128,128]{1,2,0:T(8,128)S(1)} custom-call(f32[1,128,128]{2,1,0:T(8,128)S(1)} %get-tuple-element.92), custom_call_target="InvertDiagBlocksLowerTriangular" | custom-call | tf_op jit(solution)/shard_map/jit(cholesky)/cholesky | solution.py:126
  439.1 11.7 %cholesky.276 = f32[128,128]{1,0:T(8,128)S(1)} custom-call(f32[128,128]{1,0:T(8,128)S(1)} %cholesky.665), custom_call_target="Cholesky" | custom-call | tf_op jit(solution)/shard_map/jit(cholesky)/cholesky | solution.py:126
  451.2 2.9 cholesky.283
  454.1 9.8 %custom-call.75 = f32[1,128,128]{1,2,0:T(8,128)S(1)} custom-call(f32[1,128,128]{2,1,0:T(8,128)S(1)} %get-tuple-element.90), custom_call_target="InvertDiagBlocksLowerTriangular" | custom-call | tf_op jit(solution)/shard_map/jit(cholesky)/cholesky | solution.py:126
  466.8 3.0 convolution_subtract_fusion.1
  469.8 11.7 %cholesky.529 = f32[128,128]{1,0:T(8,128)S(1)} custom-call(f32[128,128]{1,0:T(8,128)S(1)} %cholesky.670), custom_call_target="Cholesky" | custom-call | tf_op jit(solution)/shard_map/jit(cholesky)/cholesky | solution.py:126
  482.3 9.8 %custom-call.76 = f32[1,128,128]{1,2,0:T(8,128)S(1)} custom-call(f32[1,128,128]{2,1,0:T(8,128)S(1)} %get-tuple-element.88), custom_call_target="InvertDiagBlocksLowerTriangular" | custom-call | tf_op jit(solution)/shard_map/jit(cholesky)/cholesky | solution.py:126
  493.4 3.8 convolution_subtract_fusion.2
  497.3 11.7 %cholesky.548 = f32[128,128]{1,0:T(8,128)S(1)} custom-call(f32[128,128]{1,0:T(8,128)S(1)} %cholesky.675), custom_call_target="Cholesky" | custom-call | tf_op jit(solution)/shard_map/jit(cholesky)/cholesky | solution.py:126
  509.7 9.8 %custom-call.77 = f32[1,128,128]{1,2,0:T(8,128)S(1)} custom-call(f32[1,128,128]{2,1,0:T(8,128)S(1)} %get-tuple-element.86), custom_call_target="InvertDiagBlocksLowerTriangular" | custom-call | tf_op jit(solution)/shard_map/jit(cholesky)/cholesky | solution.py:126
  520.8 3.7 fusion.9
  524.5 12.1 %cholesky.567 = f32[128,128]{1,0:T(8,128)S(1)} custom-call(f32[128,128]{1,0:T(8,128)S(1)} %cholesky.680), custom_call_target="Cholesky" | custom-call | tf_op jit(solution)/shard_map/jit(cholesky)/cholesky | solution.py:126
  537.4 9.8 %custom-call.78 = f32[1,128,128]{1,2,0:T(8,128)S(1)} custom-call(f32[1,128,128]{2,1,0:T(8,128)S(1)} %get-tuple-element.84), custom_call_target="InvertDiagBlocksLowerTriangular" | custom-call | tf_op jit(solution)/shard_map/jit(cholesky)/cholesky | solution.py:126
  548.3 3.7 fusion.15
  552.1 11.7 %cholesky.587 = f32[128,128]{1,0:T(8,128)S(1)} custom-call(f32[128,128]{1,0:T(8,128)S(1)} %cholesky.685), custom_call_target="Cholesky" | custom-call | tf_op jit(solution)/shard_map/jit(cholesky)/cholesky | solution.py:126
  564.6 9.8 %custom-call.79 = f32[1,128,128]{1,2,0:T(8,128)S(1)} custom-call(f32[1,128,128]{2,1,0:T(8,128)S(1)} %get-tuple-element.82), custom_call_target="InvertDiagBlocksLowerTriangular" | custom-call | tf_op jit(solution)/shard_map/jit(cholesky)/cholesky | solution.py:126
  575.7 3.5 fusion.18
  579.2 11.7 %cholesky.607 = f32[128,128]{1,0:T(8,128)S(1)} custom-call(f32[128,128]{1,0:T(8,128)S(1)} %cholesky.690), custom_call_target="Cholesky" | custom-call | tf_op jit(solution)/shard_map/jit(cholesky)/cholesky | solution.py:126
  591.7 9.8 %custom-call.80 = f32[1,128,128]{1,2,0:T(8,128)S(1)} custom-call(f32[1,128,128]{2,1,0:T(8,128)S(1)} %get-tuple-element.80), custom_call_target="InvertDiagBlocksLowerTriangular" | custom-call | tf_op jit(solution)/shard_map/jit(cholesky)/cholesky | solution.py:126
  602.5 3.0 convolution_subtract_fusion.3
  605.5 11.9 %cholesky.627 = f32[128,128]{1,0:T(8,128)S(1)} custom-call(f32[128,128]{1,0:T(8,128)S(1)} %cholesky.695), custom_call_target="Cholesky" | custom-call | tf_op jit(solution)/shard_map/jit(cholesky)/cholesky | solution.py:126
  618.2 9.8 %custom-call.81 = f32[1,128,128]{1,2,0:T(8,128)S(1)} custom-call(f32[1,128,128]{2,1,0:T(8,128)S(1)} %get-tuple-element.78), custom_call_target="InvertDiagBlocksLowerTriangular" | custom-call | tf_op jit(solution)/shard_map/jit(cholesky)/cholesky | solution.py:126
  628.9 2.2 convolution_subtract_fusion.4
  631.2 11.7 %cholesky.645 = f32[128,128]{1,0:T(8,128)S(1)} custom-call(f32[128,128]{1,0:T(8,128)S(1)} %convolution_subtract_fusion.4), custom_call_target="Cholesky" | custom-call | tf_op jit(solution)/shard_map/jit(cholesky)/cholesky | solution.py:126
  655.2 5.2 select_select_fusion
  660.4 31.5 %while.1 = (s32[]{:T(128)}, f32[1152,1152]{0,1:T(8,128)}, s32[9,2]{0,1:T(2,128)S(1)}, f32[9,128,128]{2,1,0:T(8,128)}, s32[]{:T(128)}) while((s32[]{:T(128)}, f32[1152,1152]{0,1:T(8,128)}, s32[9,2]{0,1:T(2,128)S(1)}, f32[9,128,128]{2,1,0:T(8,128)}, s32[]{:T(128)}) %tuple.99), condition=%wide.while_cond, body=%wide.while_body.sunk | while | flops 2 | bytes 393829 | solution.py:127
  661.0 2.2 dynamic-slice.7
  664.6 2.2 dynamic-slice.7
  668.1 2.2 dynamic-slice.7
  671.6 2.2 dynamic-slice.7
  675.1 2.2 dynamic-slice.7
  692.0 89.5 %custom-call.82 = f32[9,128,128]{1,2,0:T(8,128)S(1)} custom-call(f32[9,128,128]{2,1,0:T(8,128)} %get-tuple-element.9), custom_call_target="InvertDiagBlocksLowerTriangular" | custom-call | tf_op jit(solution)/shard_map/jit(_cho_solve)/triangular_solve | solution.py:127
  806.0 23.8 %all_gather.3 = f32[16,9,128]{2,1,0:T(8,128)S(1)} all-gather(f32[1,9,128]{2,1,0:T(8,128)S(1)} %bitcast.569), channel_id=1, replica_groups=mesh['pt'=8,'cl'=16] {'cl'}, dimensions={0}, use_global_device_ids=true | all-gather | bytes 78336 | tf_op jit(solution)/shard_map/all_gather | solution.py:128
  830.2 5.5 gather_fusion.2
  (293 shorter events, 93.9 us)
Async XLA Ops:
  7.2 0.8 copy-start
  7.2 23.4 %copy-start.12 = (f32[2,4,2,9,256]{4,2,3,1,0:T(2,128)S(1)}, f32[2,4,2,9,256]{4,2,3,1,0:T(2,128)}, u32[]{:S(2)}) copy-start(f32[2,4,2,9,256]{4,2,3,1,0:T(2,128)} %param.9) | copy-start | bytes 442372
  16.5 61.9 %all-to-all-start.1 = ((s32[16,1,256]{2,1,0:T(1,128)}), s32[16,1,256]{2,1,0:T(1,128)S(1)}, u32[]{:S(2)}, u32[]{:S(2)}) async-start(s32[16,1,256]{2,1,0:T(1,128)} %reshape.898), calls=%async_computation.1 | async-start | bytes 32768 | tf_op jit(solution)/shard_map/all_to_all | solution.py:103
  33.1 11.3 %copy-start.3 = (f32[2,4,2,3,256]{3,2,4,1,0:T(2,128)S(1)}, f32[2,4,2,3,256]{3,2,4,1,0:T(2,128)}, u32[]{:S(2)}) copy-start(f32[2,4,2,3,256]{3,2,4,1,0:T(2,128)} %copy.193) | copy-start | bytes 147460
  33.1 11.3 %copy-start.4 = (f32[2,4,2,9,256]{3,2,4,1,0:T(2,128)S(1)}, f32[2,4,2,9,256]{3,2,4,1,0:T(2,128)}, u32[]{:S(2)}) copy-start(f32[2,4,2,9,256]{3,2,4,1,0:T(2,128)} %copy.194) | copy-start | bytes 442372
  44.4 29.0 %copy-start.17 = (f32[256]{0:T(256)}, f32[256]{0:T(256)S(1)}, u32[]{:S(2)}) copy-start(f32[256]{0:T(256)S(1)} %get-tuple-element.44) | copy-start | bytes 3076
  44.4 22.0 %copy-start.16 = (s32[2,4,256]{2,1,0:T(4,128)S(1)}, s32[2,4,256]{2,1,0:T(4,128)}, u32[]{:S(2)}) copy-start(s32[2,4,256]{2,1,0:T(4,128)} %param.12) | copy-start | bytes 24580
  44.4 22.0 %copy-start.13 = (f32[16,9,128]{2,0,1:T(8,128)S(1)}, f32[16,9,128]{2,0,1:T(8,128)}, u32[]{:S(2)}) copy-start(f32[16,9,128]{2,0,1:T(8,128)} %param.16) | copy-start | bytes 221188
  66.1 22.5 %copy-start.6 = (f32[2,4,9,1,256]{4,1,3,2,0:T(4,128)}, f32[2,4,9,1,256]{4,1,3,2,0:T(4,128)S(1)}, u32[]{:S(2)}) copy-start(f32[2,4,9,1,256]{4,1,3,2,0:T(4,128)S(1)} %get-tuple-element.67) | copy-start | bytes 221188
  66.2 22.5 %copy-start.8 = (f32[2,4,9,1,256]{4,1,3,2,0:T(4,128)}, f32[2,4,9,1,256]{4,1,3,2,0:T(4,128)S(1)}, u32[]{:S(2)}) copy-start(f32[2,4,9,1,256]{4,1,3,2,0:T(4,128)S(1)} %get-tuple-element.68) | copy-start | bytes 221188
  73.3 13.0 %copy-start.19 = (f32[1,256]{1,0:T(1,128)}, f32[1,256]{1,0:T(1,128)S(1)}, u32[]{:S(2)}) copy-start(f32[1,256]{1,0:T(1,128)S(1)} %get-tuple-element.59) | copy-start | bytes 3076
  73.3 13.0 %copy-start.21 = (f32[1,256]{1,0:T(1,128)}, f32[1,256]{1,0:T(1,128)S(1)}, u32[]{:S(2)}) copy-start(f32[1,256]{1,0:T(1,128)S(1)} %get-tuple-element.58) | copy-start | bytes 3076
  73.9 0.6 copy-start.23
  73.9 0.6 copy-start.25
  78.4 0.6 copy-start.14
  79.0 24.2 %all-to-all-start = ((f32[216,16,64]{0,2,1:T(8,128)}), f32[216,16,64]{0,2,1:T(8,128)S(1)}, u32[]{:S(2)}, u32[]{:S(2)}) async-start(f32[216,16,64]{0,2,1:T(8,128)} %bitcast.36), calls=%async_computation | async-start | bytes 2097152 | tf_op jit(solution)/shard_map/all_to_all | solution.py:102
  86.3 308.6 %all-reduce.3.cloned.1.call-start = ((), (), s32[]{:S(2)}) async-start(), calls=%async_computation.2 | async-start | bytes 10616832 | tf_op jit(solution)/shard_map/psum | solution.py:124
  88.4 14.8 %copy-start.10 = (s32[4,1024]{1,0:T(4,128)}, s32[4,1024]{1,0:T(4,128)S(1)}, u32[]{:S(2)}) copy-start(s32[4,1024]{1,0:T(4,128)S(1)} %eq.64) | copy-start | bytes 49156
  203.7 6.3 copy-start.5
  320.4 0.7 copy-start.11
  411.9 2.3 copy-start.2
  660.4 169.8 %copy-start.15 = (s32[2048]{0:T(1024)S(1)}, s32[2048]{0:T(1024)}, u32[]{:S(2)}) copy-start(s32[2048]{0:T(1024)} %get-tuple-element.148) | copy-start | bytes 24580
  660.4 175.6 %copy-start.7 = (f32[2,4,9,1,256]{4,1,3,2,0:T(4,128)S(1)}, f32[2,4,9,1,256]{4,1,3,2,0:T(4,128)}, u32[]{:S(2)}) copy-start(f32[2,4,9,1,256]{4,1,3,2,0:T(4,128)} %copy-done.6) | copy-start | bytes 221188
  660.4 175.6 %copy-start.9 = (f32[2,4,9,1,256]{4,1,3,2,0:T(4,128)S(1)}, f32[2,4,9,1,256]{4,1,3,2,0:T(4,128)}, u32[]{:S(2)}) copy-start(f32[2,4,9,1,256]{4,1,3,2,0:T(4,128)} %copy-done.8) | copy-start | bytes 221188
  691.9 144.2 %copy-start.22 = (f32[1,256]{1,0:T(1,128)S(1)}, f32[1,256]{1,0:T(1,128)}, u32[]{:S(2)}) copy-start(f32[1,256]{1,0:T(1,128)} %copy-done.21) | copy-start | bytes 3076
  691.9 144.2 %copy-start.24 = (f32[1,256]{1,0:T(1,128)S(1)}, f32[1,256]{1,0:T(1,128)}, u32[]{:S(2)}) copy-start(f32[1,256]{1,0:T(1,128)} %copy-done.23) | copy-start | bytes 3076
  691.9 144.2 %copy-start.26 = (f32[1,256]{1,0:T(1,128)S(1)}, f32[1,256]{1,0:T(1,128)}, u32[]{:S(2)}) copy-start(f32[1,256]{1,0:T(1,128)} %copy-done.25) | copy-start | bytes 3076
  691.9 144.2 %copy-start.18 = (f32[256]{0:T(256)S(1)}, f32[256]{0:T(256)}, u32[]{:S(2)}) copy-start(f32[256]{0:T(256)} %copy-done.17) | copy-start | bytes 3076
  691.9 144.2 %copy-start.20 = (f32[1,256]{1,0:T(1,128)S(1)}, f32[1,256]{1,0:T(1,128)}, u32[]{:S(2)}) copy-start(f32[1,256]{1,0:T(1,128)} %copy-done.19) | copy-start | bytes 3076
  692.0 144.2 %copy-start.28 = (f32[1,256]{1,0:T(1,128)S(1)}, f32[1,256]{1,0:T(1,128)}, u32[]{:S(2)}) copy-start(f32[1,256]{1,0:T(1,128)} %get-tuple-element.61) | copy-start | bytes 3076
  692.0 144.2 %copy-start.29 = (f32[1,256]{1,0:T(1,128)S(1)}, f32[1,256]{1,0:T(1,128)}, u32[]{:S(2)}) copy-start(f32[1,256]{1,0:T(1,128)} %get-tuple-element.62) | copy-start | bytes 3076
  692.0 144.2 %copy-start.30 = (f32[1,256]{1,0:T(1,128)S(1)}, f32[1,256]{1,0:T(1,128)}, u32[]{:S(2)}) copy-start(f32[1,256]{1,0:T(1,128)} %get-tuple-element.63) | copy-start | bytes 3076
  692.0 144.8 %copy-start.1 = (s32[16]{0:T(128)S(1)}, s32[16]{0:T(128)}, u32[]{:S(2)}) copy-start(s32[16]{0:T(128)} %param.15) | copy-start | bytes 196
  805.9 30.9 %copy-start.27 = (f32[1152,1]{0,1:T(1,128)}, f32[1152,1]{0,1:T(1,128)S(1)}, u32[]{:S(2)}) copy-start(f32[1152,1]{0,1:T(1,128)S(1)} %constant_dynamic-update-slice_fusion.52) | copy-start | bytes 13828
Sparse Core Ops, SparseCore 0:
  320.6 74.2 all-reduce.2
where the time goes:
time: 849 us; the launch traced here: 844 us
  other arithmetic  307 us (36%)
  matrix products  231 us (27%)
  local copies, waits for them, and re-layouts  160 us (19%)
  waiting for transfers between devices  72.3 us (9%)
  blocking collectives  36.8 us (4%)
  between operations  21.7 us (3%)
  starting transfers between devices  15.5 us (2%)
    another operation x35, other arithmetic, per_device(): chol = jnp.linalg.cholesky(total)  191 us
    another operation x4, other arithmetic, per_device(): jax.scipy.linalg.cho_solve((chol, True), right_side.reshape(order))  94.7 us
    dot_general x1, matrix products, per_device(): jnp.einsum('ras,rbs->ab', flat_spread, flat_spread, precision=highest)  63.6 us
    psum x1, waiting for transfers between devices, per_device(): total, right_side = lax.psum((partial_value, rhs_part), 'pt')  59.7 us
    dot_general x1, matrix products, per_device(): jnp.einsum('kmis,kmjs->kijs', jac_recv, jac_recv, precision=highest)  57.3 us
    another operation x16, matrix products, per_device(): chol = jnp.linalg.cholesky(total)  34.4 us
    another operation x47, local copies, waits for them, and re-layouts  31.6 us
    dot_general x1, matrix products, per_device(): jnp.einsum('kcs,kirs->rics', camera_hot, coef_recv, precision=highest)  25.2 us
  transfers between devices with their start and end apart: 3, of which 2 were waited for; matrix products, arithmetic and copies ran while one was open for 7% of the time, Pallas kernels for 0%

commit v1 on v0

v1 whole, which is shorter than its diff:
```python
import jax
import jax.numpy as jnp
from jax import lax
from jax.experimental import pallas as pl
from jax.experimental.pallas import tpu as pltpu
from jax.sharding import PartitionSpec as P

f32 = jnp.float32
bf16 = jnp.bfloat16
LANES = 128
SLOTS = 4
PARAMS = 9
GROUPS = 32
UNK = 27
DIAG = 45
ROW_Q = 45
ROW_D = (0, 54, 135, 216)
BAND = 304
HALF = BAND // 2
PACK = 56
VMEM_LIMIT = 56 * 1024 * 1024


def split3(value):
    high = value.astype(bf16)
    rest = value - high.astype(f32)
    mid = rest.astype(bf16)
    low = (rest - mid.astype(f32)).astype(bf16)
    return high, mid, low


def dot_nt(left, right):
    return lax.dot_general(left, right, (((1,), (1,)), ((), ())), preferred_element_type=f32)


def iota(shape, dim):
    return lax.broadcasted_iota(jnp.int32, shape, dim)


def lanes_from(value, index):
    return jnp.take_along_axis(value, index, axis=1)


def spread_row(chunk, row):
    return jnp.broadcast_to(chunk[row : row + 1, :], (8, LANES))


def lookup_dot(table, masks, cam_ref, jac_ref, out_ref):
    for half in range(2):
        cols = slice(half * LANES, (half + 1) * LANES)
        for s in range(2):
            for k in range(SLOTS):
                index = jnp.broadcast_to(cam_ref[s, k : k + 1, cols], (16, LANES))
                sums = [None, None]
                for i in range(PARAMS):
                    got = jnp.concatenate(
                        [
                            lanes_from(table[i][0:8], index[0:8]),
                            lanes_from(table[i][8:16], index[8:16]),
                        ],
                        axis=0,
                    )
                    for m in range(2):
                        row = k * PARAMS + i
                        term = got * jac_ref[m, s, row : row + 1, cols]
                        sums[m] = term if sums[m] is None else sums[m] + term
                for m in range(2):
                    row = s * 8 + m * 4 + k
                    picked = jnp.sum(sums[m] * masks[s][half], axis=0, keepdims=True)
                    out_ref[row : row + 1, cols] = picked


def cluster_masks(cluster_rows):
    masks = []
    for s in range(2):
        per_half = []
        for half in range(2):
            row = cluster_rows[s : s + 1, half * LANES : (half + 1) * LANES]
            per_half.append((iota((16, LANES), 0) == row).astype(f32))
        masks.append(per_half)
    return masks


def points_kernel(
    owner_ref,
    damp_ref,
    jac_ref,
    jp_ref,
    res_ref,
    cam_ref,
    count_ref,
    clus_ref,
    prev_ref,
    send_ref,
    proj_ref,
    fact_ref,
    dots,
    packed,
):
    npts = 2 * LANES
    clus = clus_ref[...]
    dest = jnp.zeros_like(clus)
    for c in range(16):
        dest = jnp.where(clus == c, owner_ref[c], dest)
    slot_row = iota((8, npts), 0) % 4
    live = jnp.concatenate(
        [(slot_row < count_ref[s : s + 1, :]).astype(f32) for s in range(2)], axis=0
    )
    jp = [jp_ref[a] * live for a in range(3)]
    res = res_ref[...] * live

    def total(value):
        return jnp.sum(value, axis=0, keepdims=True)

    damp = damp_ref[0]
    inv1 = 1.0 / jnp.sqrt(total(jp[0] * jp[0]) + damp)
    l21 = total(jp[1] * jp[0]) * inv1
    l31 = total(jp[2] * jp[0]) * inv1
    inv2 = 1.0 / jnp.sqrt(total(jp[1] * jp[1]) + damp - l21 * l21)
    l32 = (total(jp[2] * jp[1]) - l31 * l21) * inv2
    inv3 = 1.0 / jnp.sqrt(total(jp[2] * jp[2]) + damp - l31 * l31 - l32 * l32)
    p1 = jp[0] * inv1
    p2 = (jp[1] - l21 * p1) * inv2
    p3 = (jp[2] - l31 * p1 - l32 * p2) * inv3
    proj = [p1, p2, p3]
    grad = [total(jp[a] * res) for a in range(3)]
    h1 = grad[0] * inv1
    h2 = (grad[1] - l21 * h1) * inv2
    h3 = (grad[2] - l31 * h1 - l32 * h2) * inv3
    h = [h1, h2, h3]
    for a in range(3):
        proj_ref[a] = proj[a]
    for n, row in enumerate([inv1, inv2, inv3, l21, l31, l32, h1, h2, h3]):
        fact_ref[n : n + 1, :] = row

    masks = cluster_masks(clus)
    table = [prev_ref[i] for i in range(PARAMS)]
    lookup_dot(table, masks, cam_ref, jac_ref, dots)
    dot_all = dots[...]
    wt = -res
    for a in range(3):
        terms = proj[a] * dot_all
        carried = [jnp.sum(terms[8 * s : 8 * s + 8], axis=0, keepdims=True) for s in range(2)]
        mixed = jnp.concatenate(
            [jnp.broadcast_to(h[a] + carried[1 - s], (8, npts)) for s in range(2)], axis=0
        )
        wt = wt + proj[a] * mixed

    for s in range(2):
        cols = slice(s * npts, (s + 1) * npts)
        for m in range(2):
            base = m * PACK
            for k in range(SLOTS):
                on = live[s * 8 + m * 4 + k : s * 8 + m * 4 + k + 1, :]
                packed[base + 9 * k : base + 9 * k + 9, cols] = (
                    jac_ref[m, s, 9 * k : 9 * k + 9, :] * on
                )
            rows = slice(s * 8 + m * 4, s * 8 + m * 4 + 4)
            for a in range(3):
                packed[base + 36 + 4 * a : base + 40 + 4 * a, cols] = proj[a][rows]
            packed[base + 48 : base + 52, cols] = wt[rows]
            packed[base + 52 : base + 53, cols] = cam_ref[s, 0:1, :].astype(f32)
            packed[base + 53 : base + 56, cols] = jnp.zeros((3, npts), f32)

    dest_row = jnp.concatenate([dest[0:1], dest[1:2]], axis=1)
    hot = (iota((16, 2 * npts), 0) == dest_row).astype(f32)
    before = (iota((2 * npts, 2 * npts), 1) < iota((2 * npts, 2 * npts), 0)).astype(bf16)
    earlier = dot_nt(hot.astype(bf16), before)
    place = jnp.sum(earlier * hot, axis=0, keepdims=True)
    slot = dest_row * 64 + place.astype(jnp.int32)
    parts = split3(packed[...])
    left = jnp.concatenate(parts, axis=0)
    low_half = iota((PACK, LANES), 1) < 64
    for pair in range(8):
        slots = iota((LANES, 2 * npts), 0) + pair * LANES
        pick = (slots == slot).astype(f32).astype(bf16)
        got = dot_nt(left, pick)
        full = got[0 : 2 * PACK] + got[2 * PACK : 4 * PACK] + got[4 * PACK : 6 * PACK]
        first = full[0:PACK]
        second = full[PACK : 2 * PACK]
        first_r = pltpu.roll(first, 64, 1)
        second_r = pltpu.roll(second, 64, 1)
        send_ref[2 * pair] = jnp.where(low_half, first, second_r)
        send_ref[2 * pair + 1] = jnp.where(low_half, first_r, second)


def band_kernel(core_ref, recv_ref, keep_ref, give_ref, rows, wide, hots):
    low_half = iota((8, LANES), 1) < 64
    quant = [[], []]
    for r in range(53):
        even = recv_ref[pl.ds(r, 8, stride=2 * PACK), :]
        odd = recv_ref[pl.ds(PACK + r, 8, stride=2 * PACK), :]
        even_r = pltpu.roll(even, 64, 1)
        odd_r = pltpu.roll(odd, 64, 1)
        quant[0].append(jnp.where(low_half, even, odd_r))
        quant[1].append(jnp.where(low_half, even_r, odd))

    def jac(k, m, i):
        return quant[m][9 * k + i]

    def proj(k, m, a):
        return quant[m][36 + 4 * a + k]

    def wt(k, m):
        return quant[m][48 + k]

    cam = quant[0][52].astype(jnp.int32)
    camera_of = 4 * (iota((LANES, LANES), 0) % GROUPS) + iota((LANES, LANES), 0) // GROUPS
    for b in range(8):
        cam_b = jnp.broadcast_to(cam[b : b + 1, :], (LANES, LANES))
        for k in range(SLOTS):
            hots[k, :, b * LANES : (b + 1) * LANES] = (
                (camera_of == (cam_b + k) % LANES).astype(f32).astype(bf16)
            )

    sizes = [304, 224, 144, 64]
    out = None
    for k in range(SLOTS):
        count = 0

        def put(row, value):
            rows[8 * row : 8 * row + 8, :] = value

        for dist in range(SLOTS - k):
            other = k + dist
            mix = [[None, None], [None, None]]
            for m in range(2):
                for n in range(2):
                    if dist == 0 and n < m:
                        mix[m][n] = mix[n][m]
                        continue
                    acc = proj(k, m, 0) * proj(other, n, 0)
                    acc = acc + proj(k, m, 1) * proj(other, n, 1)
                    acc = acc + proj(k, m, 2) * proj(other, n, 2)
                    same = dist == 0 and m == n
                    mix[m][n] = (1.0 - acc) if same else -acc
            for j in range(PARAMS):
                left = [
                    mix[m][0] * jac(other, 0, j) + mix[m][1] * jac(other, 1, j) for m in range(2)
                ]
                for i in range(PARAMS):
                    if dist == 0 and i > j:
                        continue
                    value = jac(k, 0, i) * left[0] + jac(k, 1, i) * left[1]
                    if dist == 0:
                        row = i * 9 - i * (i - 1) // 2 + (j - i)
                    else:
                        row = ROW_D[dist] + i * 9 + j
                    put(row, value)
                    count += 1
        for i in range(PARAMS):
            put(ROW_Q + i, jac(k, 0, i) * wt(k, 0) + jac(k, 1, i) * wt(k, 1))
            count += 1
        size = sizes[k]
        for row in range(count, size):
            put(row, jnp.zeros((8, LANES), f32))
        for b in range(8):
            piece = rows[pl.ds(b, size, stride=8), :]
            for n, part in enumerate(split3(piece)):
                wide[n, 0:size, b * LANES : (b + 1) * LANES] = part
        hot = hots[k]
        got = dot_nt(wide[0, 0:size, :], hot)
        got = got + dot_nt(wide[1, 0:size, :], hot)
        got = got + dot_nt(wide[2, 0:size, :], hot)
        if out is None:
            out = got
        else:
            out = jnp.concatenate([out[0:size] + got, out[size:]], axis=0)
    core = core_ref[0]
    low, high = out[0:HALF], out[HALF:BAND]
    keep_ref[...] = jnp.where(core == 0, low, high)
    give_ref[...] = jnp.where(core == 0, high, low)


def factor(size, diag, side, side_chunks):
    chunks = len(diag[0])
    inverse = []
    for k in range(size):
        pivot = spread_row(diag[k][k // 8], k % 8)
        root = lax.rsqrt(pivot)
        root = root * (1.5 - 0.5 * pivot * root * root)
        inverse.append(root)
        for v in range(k // 8, chunks):
            diag[k][v] = diag[k][v] * root
        for e in side_chunks:
            side[k][e] = side[k][e] * root
        for r in range(k + 1, size):
            coef = spread_row(diag[k][r // 8], r % 8)
            for v in range(r // 8, chunks):
                diag[r][v] = diag[r][v] - coef * diag[k][v]
            for e in side_chunks:
                side[r][e] = side[r][e] - coef * side[k][e]
    return inverse


def schur(size, side, lane):
    within = lane % GROUPS
    results = []
    for which in range(2):
        full = []
        for r in range(size):
            full.append(
                [
                    lanes_from(side[r][v % 2], within + GROUPS * (2 * which + v // 2))
                    for v in range(4)
                ]
            )
        per_a = []
        for a in range(UNK):
            acc = [None, None]
            for r in range(size):
                coef = spread_row(full[r][a // 8], a % 8)
                for e in range(2):
                    term = coef * side[r][e]
                    acc[e] = term if acc[e] is None else acc[e] + term
            per_a.append(acc)
        results.append(per_a)
    return results


def apply_schur(left, right, diag, side, lane, down, up, keep):
    within = lane % GROUPS
    part = lane // GROUPS
    from_down = (within - down + GROUPS) % GROUPS
    from_up = (within + up) % GROUPS
    pack_down = part * GROUPS + from_down
    pack_up = part * GROUPS + from_up
    is_left = part < 2
    is_rhs = jnp.logical_and(part == 1, iota((8, LANES), 0) == 3)
    for a in range(UNK):
        fresh = []
        for e in range(2):
            by_down = lanes_from(right[a][e], pack_down)
            by_up = lanes_from(left[a][e], pack_up)
            new = -jnp.where(is_left, by_down, by_up)
            if keep:
                new = new + side[a][e]
                if e == 1:
                    new = new - jnp.where(is_rhs, by_up, 0.0)
            elif e == 1:
                new = new + jnp.where(is_rhs, side[a][e] - by_up, 0.0)
            fresh.append(new)
        for v in range(a // 8, 4):
            own = lanes_from(right[a][v % 2], from_down + GROUPS * (2 + v // 2))
            other = lanes_from(left[a][v % 2], from_up + GROUPS * (v // 2))
            diag[a][v] = diag[a][v] - own - other
        side[a] = fresh


def solve_kernel(
    core_ref, damp_ref, mine_ref, other_ref, step_ref, cast_ref, rep, back, dmat, lmat, umat, smat, xrow, d0, l0, u0
):
    lane = iota((8, LANES), 1)
    within = lane % GROUPS
    part = lane // GROUPS
    core = core_ref[0]
    low = jnp.where(core == 0, mine_ref[...], other_ref[...])
    high = jnp.where(core == 0, other_ref[...], mine_ref[...])
    row = iota((HALF, LANES), 0)
    on_diag = row < 0
    for i in range(PARAMS):
        on_diag = jnp.logical_or(on_diag, row == i * 9 - i * (i - 1) // 2)
    low = low + jnp.where(on_diag, damp_ref[0], 0.0)
    first_rows = HALF // 8
    for n in range(BAND // 8):
        chunk = low[8 * n : 8 * n + 8] if n < first_rows else high[8 * n - HALF : 8 * n - HALF + 8]
        for r in range(4):
            rep[r, 8 * n : 8 * n + 8, :] = lanes_from(chunk, within + GROUPS * r)
            if r > 0:
                back[r - 1, 8 * n : 8 * n + 8, :] = lanes_from(
                    chunk, (within + GROUPS - 1) % GROUPS + GROUPS * r
                )
    zero = jnp.zeros((UNK, 32, LANES), f32)
    dmat[...] = zero
    lmat[...] = zero
    umat[...] = zero
    d0[...] = jnp.zeros_like(d0)
    l0[...] = jnp.zeros_like(l0)
    u0[...] = jnp.zeros_like(u0)

    def tri(i):
        return i * 9 - i * (i - 1) // 2

    for i in range(PARAMS):
        d0[i, i:9, :] = rep[0, tri(i) : tri(i) + 9 - i, :]
        for d in range(1, 4):
            u0[i, 9 * d - 9 : 9 * d, :] = rep[0, ROW_D[d] + 9 * i : ROW_D[d] + 9 * i + 9, :]
            l0[i, 27 - 9 * d : 36 - 9 * d, :] = back[3 - d, pl.ds(ROW_D[d] + i, 9, stride=9), :]
        l0[i, 27:28, :] = rep[0, ROW_Q + i : ROW_Q + i + 1, :]
        for r in range(1, 4):
            row = 9 * r - 9 + i
            dmat[row, row : 9 * r, :] = rep[r, tri(i) : tri(i) + 9 - i, :]
            for q in range(r + 1, 4):
                base = ROW_D[q - r] + 9 * i
                dmat[row, 9 * q - 9 : 9 * q, :] = rep[r, base : base + 9, :]
            for q in range(1, 4):
                if q < r:
                    base = ROW_D[4 + q - r] + 9 * i
                    umat[row, 9 * q - 9 : 9 * q, :] = rep[r, base : base + 9, :]
                if q > r:
                    base = ROW_D[4 + r - q] + i
                    lmat[row, 9 * q - 9 : 9 * q, :] = back[q - 1, pl.ds(base, 9, stride=9), :]
            lmat[row, 27:28, :] = rep[r, ROW_Q + i : ROW_Q + i + 1, :]

    def pack(lm, um):
        return [
            jnp.where(
                part == 0,
                lm[8 * e : 8 * e + 8],
                jnp.where(
                    part == 1,
                    lm[16 + 8 * e : 24 + 8 * e],
                    jnp.where(part == 2, um[8 * e : 8 * e + 8], um[16 + 8 * e : 24 + 8 * e]),
                ),
            )
            for e in range(2)
        ]

    def chunked(value, count):
        return [value[8 * v : 8 * v + 8] for v in range(count)]

    diag0 = [chunked(d0[i], 2) for i in range(PARAMS)]
    side0 = [pack(l0[i], u0[i]) for i in range(PARAMS)]
    inv0 = factor(PARAMS, diag0, side0, (0, 1))
    left, right = schur(PARAMS, side0, lane)
    diag = [chunked(dmat[a], 4) for a in range(UNK)]
    side = [pack(lmat[a], umat[a]) for a in range(UNK)]
    apply_schur(left, right, diag, side, lane, 0, 1, True)
    for a in range(UNK):
        for v in range(4):
            dmat[a, 8 * v : 8 * v + 8, :] = diag[a][v]
        for e in range(2):
            smat[a, 8 * e : 8 * e + 8, :] = side[a][e]

    def level(step, carry):
        stride = lax.shift_left(jnp.int32(1), step)
        diag_in = [chunked(dmat[a], 4) for a in range(UNK)]
        side_in = [chunked(smat[a], 2) for a in range(UNK)]
        diag = [list(row) for row in diag_in]
        side = [list(row) for row in side_in]
        factor(UNK, diag, side, (0, 1))
        left, right = schur(UNK, side, lane)
        diag = [list(row) for row in diag_in]
        side = [list(row) for row in side_in]
        apply_schur(left, right, diag, side, lane, stride, stride, False)
        for a in range(UNK):
            for v in range(4):
                dmat[a, 8 * v : 8 * v + 8, :] = diag[a][v]
            for e in range(2):
                smat[a, 8 * e : 8 * e + 8, :] = side[a][e]
        return carry

    lax.fori_loop(0, 5, level, jnp.int32(0))

    diag = [chunked(dmat[a], 4) for a in range(UNK)]
    side = [chunked(smat[a], 2) for a in range(UNK)]
    for a in range(UNK):
        for v in range(a // 8, 4):
            from_l = lanes_from(side[a][v % 2], within + GROUPS * (v // 2))
            from_u = lanes_from(side[a][v % 2], within + GROUPS * (2 + v // 2))
            diag[a][v] = diag[a][v] + from_l + from_u
    inverse = factor(UNK, diag, side, (1,))
    todo = [spread_row(lanes_from(side[a][1], within + GROUPS), 3) for a in range(UNK)]
    value = [None] * UNK
    for k in range(UNK - 1, -1, -1):
        value[k] = todo[k] * inverse[k]
        for r in range(k):
            todo[r] = todo[r] - spread_row(diag[r][k // 8], k % 8) * value[k]
    for a in range(UNK):
        xrow[a : a + 1, :] = value[a][0:1]
    xrow[UNK:32, :] = jnp.zeros((5, LANES), f32)
    own = chunked(xrow[...], 4)
    prev = [lanes_from(c, (lane + LANES - 1) % LANES) for c in own]
    both = pack(jnp.concatenate(prev, axis=0), jnp.concatenate(own, axis=0))
    todo0 = []
    for i in range(PARAMS):
        terms = side0[i][0] * both[0] + side0[i][1] * both[1]
        terms = terms + pltpu.roll(terms, 64, 1)
        terms = terms + pltpu.roll(terms, 32, 1)
        rhs = spread_row(lanes_from(side0[i][1], within + GROUPS), 3)
        summed = jnp.broadcast_to(jnp.sum(terms, axis=0, keepdims=True), (8, LANES))
        todo0.append(rhs - summed)
    value0 = [None] * PARAMS
    for k in range(PARAMS - 1, -1, -1):
        value0[k] = todo0[k] * inv0[k]
        for r in range(k):
            todo0[r] = todo0[r] - spread_row(diag0[r][k // 8], k % 8) * value0[k]
    camera = (lane % 4) * GROUPS + lane // 4
    for i in range(PARAMS):
        row = jnp.where(
            part == 0,
            value0[i],
            jnp.where(part == 1, value[i], jnp.where(part == 2, value[9 + i], value[18 + i])),
        )
        step_ref[i : i + 1, :] = lanes_from(row, camera)[0:1]
    for dest in range(16):
        cast_ref[dest, 0:PARAMS, :] = step_ref[...]
        cast_ref[dest, PARAMS:16, :] = jnp.zeros((16 - PARAMS, LANES), f32)


def update_kernel(owner_ref, all_ref, jac_ref, proj_ref, fact_ref, cam_ref, clus_ref, out_ref, dots):
    clus = clus_ref[...]
    dest = jnp.zeros_like(clus)
    for c in range(16):
        dest = jnp.where(clus == c, owner_ref[c], dest)
    masks = cluster_masks(dest)
    table = [all_ref[pl.ds(i, 16, stride=16), :] for i in range(PARAMS)]
    lookup_dot(table, masks, cam_ref, jac_ref, dots)
    dot_all = dots[...]

    def fact(n):
        return fact_ref[n : n + 1, :]

    tot = [fact(6 + a) + jnp.sum(proj_ref[a] * dot_all, axis=0, keepdims=True) for a in range(3)]
    x3 = tot[2] * fact(2)
    x2 = (tot[1] - fact(5) * x3) * fact(1)
    x1 = (tot[0] - fact(3) * x2 - fact(4) * x3) * fact(0)
    out_ref[0:1, :] = -x1
    out_ref[1:2, :] = -x2
    out_ref[2:3, :] = -x3


def smem():
    return pl.BlockSpec(memory_space=pltpu.SMEM)


def vmem():
    return pl.BlockSpec(memory_space=pltpu.VMEM)


def params():
    return pltpu.CompilerParams(vmem_limit_bytes=VMEM_LIMIT)


def run_points(owner_map, damping, jac, jp, res, cam_ids, obs_count, clus, prev):
    npts = 256
    return pl.pallas_call(
        points_kernel,
        out_shape=(
            jax.ShapeDtypeStruct((16, PACK, LANES), f32),
            jax.ShapeDtypeStruct((3, 16, npts), f32),
            jax.ShapeDtypeStruct((9, npts), f32),
        ),
        in_specs=[smem(), smem()] + [vmem()] * 7,
        out_specs=(vmem(), vmem(), vmem()),
        scratch_shapes=[pltpu.VMEM((16, npts), f32), pltpu.VMEM((2 * PACK, 2 * npts), f32)],
        compiler_params=params(),
        name="points",
    )(owner_map, damping, jac, jp, res, cam_ids, obs_count, clus, prev)


def run_band(core, recv):
    return pl.pallas_call(
        band_kernel,
        out_shape=(
            jax.ShapeDtypeStruct((HALF, LANES), f32),
            jax.ShapeDtypeStruct((HALF, LANES), f32),
        ),
        in_specs=[smem(), vmem()],
        out_specs=(vmem(), vmem()),
        scratch_shapes=[
            pltpu.VMEM((BAND * 8, LANES), f32),
            pltpu.VMEM((3, BAND, 1024), bf16),
            pltpu.VMEM((4, LANES, 1024), bf16),
        ],
        compiler_params=params(),
        name="band",
    )(core, recv)


def run_solve(core, damping, mine, other):
    return pl.pallas_call(
        solve_kernel,
        out_shape=(
            jax.ShapeDtypeStruct((PARAMS, LANES), f32),
            jax.ShapeDtypeStruct((16, 16, LANES), f32),
        ),
        in_specs=[smem(), smem(), vmem(), vmem()],
        out_specs=(vmem(), vmem()),
        scratch_shapes=[
            pltpu.VMEM((4, BAND, LANES), f32),
            pltpu.VMEM((3, BAND, LANES), f32),
            pltpu.VMEM((UNK, 32, LANES), f32),
            pltpu.VMEM((UNK, 32, LANES), f32),
            pltpu.VMEM((UNK, 32, LANES), f32),
            pltpu.VMEM((UNK, 16, LANES), f32),
            pltpu.VMEM((32, LANES), f32),
            pltpu.VMEM((PARAMS, 16, LANES), f32),
            pltpu.VMEM((PARAMS, 32, LANES), f32),
            pltpu.VMEM((PARAMS, 32, LANES), f32),
        ],
        compiler_params=params(),
        name="solve",
    )(core, damping, mine, other)


def run_update(owner_map, everything, jac, proj, fact, cam_ids, clus):
    return pl.pallas_call(
        update_kernel,
        out_shape=jax.ShapeDtypeStruct((3, 256), f32),
        in_specs=[smem()] + [vmem()] * 6,
        out_specs=vmem(),
        scratch_shapes=[pltpu.VMEM((16, 256), f32)],
        compiler_params=params(),
        name="update",
    )(owner_map, everything, jac, proj, fact, cam_ids, clus)


def sum_over_points(keep, give, ring):
    swap = [(i, i ^ 1) for i in range(ring)]
    half = keep + lax.ppermute(give, "pt", swap)
    moved = [
        lax.ppermute(half, "pt", [(i, (i + 2 * d) % ring) for i in range(ring)]) for d in range(1, 4)
    ]
    mine = (half + moved[1]) + (moved[0] + moved[2])
    return mine, lax.ppermute(mine, "pt", swap)


def per_device(
    cam_jac, pt_jac, residual, cam_ids, obs_count, clusters, owner_map, prev_step, damping
):
    npts = cam_jac.shape[-1]
    core = (lax.axis_index("pt") % 2).astype(jnp.int32).reshape(1)
    jac = cam_jac.transpose(2, 0, 1, 3, 4).reshape(2, 2, SLOTS * PARAMS, npts)
    jp = pt_jac.transpose(3, 0, 2, 1, 4).reshape(3, 16, npts)
    res = residual.transpose(0, 2, 1, 3).reshape(16, npts)
    clus = clusters.T
    send, proj, fact = run_points(
        owner_map, damping, jac, jp, res, cam_ids, obs_count, clus, prev_step.transpose(1, 0, 2)
    )
    recv = lax.all_to_all(send, "cl", split_axis=0, concat_axis=0, tiled=True)
    keep, give = run_band(core, recv.reshape(16 * PACK, LANES))
    mine, other = sum_over_points(keep, give, lax.axis_size("pt"))
    step, cast = run_solve(core, damping, mine, other)
    everything = lax.all_to_all(cast, "cl", split_axis=0, concat_axis=0, tiled=True)
    point_step = run_update(
        owner_map, everything.reshape(256, LANES), jac, proj, fact, cam_ids, clus
    )
    return (step[None], point_step)


def solution(mesh):
    in_specs = (
        P(None, None, None, None, ("pt", "cl")),
        P(None, None, None, None, ("pt", "cl")),
        P(None, None, None, ("pt", "cl")),
        P(None, None, ("pt", "cl")),
        P(None, ("pt", "cl")),
        P(("pt", "cl"), None),
        P(),
        P(),
        P(),
    )
    out_specs = (P("cl", None, None), P(None, ("pt", "cl")))
    return jax.shard_map(
        per_device, mesh=mesh, in_specs=in_specs, out_specs=out_specs, check_vma=False
    )
```

time: 849 us -> 76.5 us (0.09)
  other arithmetic: 307 us -> 0.92 us
  matrix products: 231 us -> 0 us
  local copies, waits for them, and re-layouts: 160 us -> 5.33 us
  waiting for transfers between devices: 72.3 us -> 25.7 us
  blocking collectives: 36.8 us -> 0 us
  Pallas kernels: 0 us -> 25.7 us
  between operations: 21.7 us -> 1.4 us
    another operation x43 -> x0, other arithmetic: 287 us -> none  [the longest x35 191 us: per_device(): chol = jnp.linalg.cholesky(total)]
    dot_general x7 -> x0, matrix products: 172 us -> none  [the longest x1 63.6 us: per_device(): jnp.einsum('ras,rbs->ab', flat_spread, flat_spread, precision=highest)]
    psum x1 -> x0, waiting for transfers between devices: 59.7 us -> none  [per_device(): total, right_side = lax.psum((partial_value, rhs_part), 'pt')]
    another operation x50 -> x0, matrix products: 58.3 us -> none  [the longest x16 34.4 us: per_device(): chol = jnp.linalg.cholesky(total)]
    transpose x5 -> x2, local copies, waits for them, and re-layouts: 42.9 us -> 0.74 us  [the longest x1 0.72 us: per_device(): res = residual.transpose(0, 2, 1, 3).reshape(16, npts)]
    another operation x82 -> x0, local copies, waits for them, and re-layouts: 41.8 us -> none
    pallas_call x0 -> x4, Pallas kernels: none -> 25.7 us  [the longest x1 14.8 us: run_solve(): pl.pallas_call(solve_kernel, out_shape=(jax.ShapeDtypeStruct((PARAMS, LAN...]
    all_gather x1 -> x0, blocking collectives: 23.8 us -> none  [per_device(): every_step = lax.all_gather(step[None], 'cl', axis=0, tiled=True)]
  transfers between devices with their start and end apart: 3 -> 7, of which waited for: 2 -> 5; matrix products, arithmetic and copies ran while one was open for 7% -> 1% of each run, Pallas kernels for 0% -> 0%
where the time goes in v1:
time: 76.5 us; the launch traced here: 76 us
  Pallas kernels  25.7 us (34%)
  waiting for transfers between devices  25.7 us (34%)
  starting transfers between devices  17 us (22%)
  local copies, waits for them, and re-layouts  5.33 us (7%)
  between operations  1.4 us (2%)
  other arithmetic  0.92 us (1%)
    pallas_call x1, Pallas kernels, run_solve(): pl.pallas_call(solve_kernel, out_shape=(jax.ShapeDtypeStruct((PARAMS, LAN...  14.8 us
    all_to_all x1, waiting for transfers between devices, per_device(): recv = lax.all_to_all(send, 'cl', split_axis=0, concat_axis=0, tiled=True)  10.8 us
    all_to_all x1, starting transfers between devices, per_device(): recv = lax.all_to_all(send, 'cl', split_axis=0, concat_axis=0, tiled=True)  7.96 us
    all_to_all x1, waiting for transfers between devices, per_device(): lax.all_to_all(cast, 'cl', split_axis=0, concat_axis=0, tiled=True)  7.34 us
    ppermute x3, starting transfers between devices, sum_over_points(): lax.ppermute(half, 'pt', [(i, (i + 2 * d) % ring) for i in range(ring)])  5.29 us
    pallas_call x1, Pallas kernels, run_band(): pl.pallas_call(band_kernel, out_shape=(jax.ShapeDtypeStruct((HALF, LANES)...  5.21 us
    ppermute x3, waiting for transfers between devices, sum_over_points(): lax.ppermute(half, 'pt', [(i, (i + 2 * d) % ring) for i in range(ring)])  4.81 us
    all_to_all x1, starting transfers between devices, per_device(): lax.all_to_all(cast, 'cl', split_axis=0, concat_axis=0, tiled=True)  3.64 us
  transfers between devices with their start and end apart: 7, of which 5 were waited for; matrix products, arithmetic and copies ran while one was open for 1% of the time, Pallas kernels for 0%

profile of v1, /device:TPU:0, one launch (start us, length us, event | category | flops | bytes accessed | tf_op | source)
XLA Modules:
  0.0 76.0 jit_solution(16673796974892905078)
XLA Ops:
  0.6 0.0 copy-start.5
  0.6 0.0 copy-start.3
  1.3 0.7 copy.17
  2.1 0.6 reshape.25.res_ref
  2.7 0.0 copy-done.5
  2.7 0.6 reshape.24.jp_ref
  3.3 0.0 copy-done.3
  3.3 0.7 copy.18.jac_ref
  4.0 3.5 %points.1 = (f32[16,56,128]{2,1,0:T(8,128)}, f32[3,16,256]{2,1,0:T(8,128)}, f32[9,256]{1,0:T(8,128)}) custom-call(s32[16]{0:T(128)} %owner_ref.3, f32[1]{0:T(128)S(6)} %copy.23.damp_ref, f32[2,2,36,256]{3,2,1,0:T(8,128)} %copy.18.jac_ref, f32[3,16,256]{2,1,0:T(8,128)} %reshape.24.jp_ref, f32[16,256]{1,0:T(8,128)} %reshape.25.res_ref, s32[2,4,256]{2,1,0:T(4,128)} %cam_ref.3, ...), custom_call_target="tpu_custom_call" | custom-call | tf_op jit(solution)/shard_map/points/pallas_call | solution.py:537
  7.6 8.0 %all-to-all-start = ((f32[16,56,128]{2,1,0:T(8,128)}), f32[16,56,128]{2,1,0:T(8,128)S(1)}, u32[]{:S(2)}, u32[]{:S(2)}) async-start(f32[16,56,128]{2,1,0:T(8,128)} %get-tuple-element.9), calls=%async_computation | async-start | bytes 917504 | tf_op jit(solution)/shard_map/all_to_all | solution.py:631
  15.5 10.8 %all-to-all-done = f32[16,56,128]{2,1,0:T(8,128)S(1)} async-done(((f32[16,56,128]{2,1,0:T(8,128)}), f32[16,56,128]{2,1,0:T(8,128)S(1)}, u32[]{:S(2)}, u32[]{:S(2)}) %all-to-all-start) | async-done | bytes 458784 | tf_op jit(solution)/shard_map/all_to_all | solution.py:631
  26.3 0.0 copy-start
  26.3 0.8 %copy-done = f32[16,56,128]{2,1,0:T(8,128)} copy-done((f32[16,56,128]{2,1,0:T(8,128)}, f32[16,56,128]{2,1,0:T(8,128)S(1)}, u32[]{:S(2)}) %copy-start) | copy-done | bytes 458776
  27.1 5.2 %band.1 = (f32[152,128]{1,0:T(8,128)}, f32[152,128]{1,0:T(8,128)}) custom-call(s32[1]{0:T(128)} %bitcast.core_ref, f32[896,128]{1,0:T(8,128)} %bitcast.11), custom_call_target="tpu_custom_call" | custom-call | tf_op jit(solution)/shard_map/band/pallas_call | solution.py:553
  32.3 0.0 collective-permute-start
  32.3 1.5 %collective-permute-done = f32[152,128]{1,0:T(8,128)S(1)} collective-permute-done((f32[152,128]{1,0:T(8,128)}, f32[152,128]{1,0:T(8,128)S(1)}, u32[]{:S(2)}, u32[]{:S(2)}) %collective-permute-start) | collective-permute-done | bytes 77856 | tf_op jit(solution)/shard_map/ppermute | solution.py:611
  33.8 0.9 %add.17 = f32[152,128]{1,0:T(8,128)S(1)} add(f32[152,128]{1,0:T(8,128)} %get-tuple-element.10, f32[152,128]{1,0:T(8,128)S(1)} %collective-permute-done) | non-fusion elementwise | flops 19456 | bytes 233472 | tf_op jit(solution)/shard_map/add | solution.py:611
  34.7 3.1 %collective-permute-start.3 = (f32[152,128]{1,0:T(8,128)S(1)}, f32[152,128]{1,0:T(8,128)S(1)}, u32[]{:S(2)}, u32[]{:S(2)}) collective-permute-start(f32[152,128]{1,0:T(8,128)S(1)} %add.17), channel_id=1, source_target_pairs={{0,96},{16,112},{32,0},{48,16},{64,32},{80,48},{96,64},{112,80},{1... | collective-permute-start | bytes 233480 | tf_op jit(solution)/shard_map/ppermute | solution.py:613
  37.8 0.0 collective-permute-start.2
  37.8 2.2 %collective-permute-start.1 = (f32[152,128]{1,0:T(8,128)S(1)}, f32[152,128]{1,0:T(8,128)S(1)}, u32[]{:S(2)}, u32[]{:S(2)}) collective-permute-start(f32[152,128]{1,0:T(8,128)S(1)} %add.17), channel_id=1, source_target_pairs={{0,64},{16,80},{32,96},{48,112},{64,0},{80,16},{96,32},{112,48},{1... | collective-permute-start | bytes 233480 | tf_op jit(solution)/shard_map/ppermute | solution.py:613
  40.0 0.0 collective-permute-done.3
  40.0 4.8 %collective-permute-done.2 = f32[152,128]{1,0:T(8,128)S(1)} collective-permute-done((f32[152,128]{1,0:T(8,128)S(1)}, f32[152,128]{1,0:T(8,128)S(1)}, u32[]{:S(2)}, u32[]{:S(2)}) %collective-permute-start.2) | collective-permute-done | bytes 77856 | tf_op jit(solution)/shard_map/ppermute | solution.py:613
  44.8 0.0 collective-permute-done.1
  44.8 0.0 copy-start.2
  44.8 0.1 collective-permute-start.4
  44.9 1.3 %collective-permute-done.4.other_ref = f32[152,128]{1,0:T(8,128)S(1)} collective-permute-done((f32[152,128]{1,0:T(8,128)S(1)}, f32[152,128]{1,0:T(8,128)S(1)}, u32[]{:S(2)}, u32[]{:S(2)}) %collective-permute-start.4) | collective-permute-done | bytes 77856 | tf_op jit(solution)/shard_map/ppermute | solution.py:616
  46.2 0.0 copy-done.2
  46.2 0.0 copy-start.4
  46.2 0.6 copy-done.4
  46.8 14.8 %solve.1 = (f32[9,128]{1,0:T(8,128)}, f32[16,16,128]{2,1,0:T(8,128)}) custom-call(s32[1]{0:T(128)} %bitcast.core_ref, f32[1]{0:T(128)S(6)} %copy.23.damp_ref, f32[152,128]{1,0:T(8,128)} %copy-done.2, f32[152,128]{1,0:T(8,128)} %copy-done.4), custom_call_target="tpu_custom_call" | custom-call | tf_op jit(solution)/shard_map/solve/pallas_call | solution.py:572
  61.6 0.0 copy-start.6
  61.6 3.6 %all-to-all-start.1 = ((f32[16,16,128]{2,1,0:T(8,128)}), f32[16,16,128]{2,1,0:T(8,128)S(1)}, u32[]{:S(2)}, u32[]{:S(2)}) async-start(f32[16,16,128]{2,1,0:T(8,128)} %get-tuple-element.13), calls=%async_computation.1 | async-start | bytes 262144 | tf_op jit(solution)/shard_map/all_to_all | solution.py:635
  65.3 0.0 copy-done.6
  65.3 0.6 copy.20
  65.9 7.3 %all-to-all-done.1 = f32[16,16,128]{2,1,0:T(8,128)S(1)} async-done(((f32[16,16,128]{2,1,0:T(8,128)}), f32[16,16,128]{2,1,0:T(8,128)S(1)}, u32[]{:S(2)}, u32[]{:S(2)}) %all-to-all-start.1) | async-done | bytes 131104 | tf_op jit(solution)/shard_map/all_to_all | solution.py:635
  73.2 0.0 copy-start.1
  73.2 0.7 copy-done.1
  73.9 2.1 %update.1 = f32[3,256]{1,0:T(4,128)} custom-call(s32[16]{0:T(128)} %owner_ref.3, f32[256,128]{1,0:T(8,128)} %bitcast.12, f32[2,2,36,256]{3,2,1,0:T(8,128)} %copy.18.jac_ref, f32[3,16,256]{2,1,0:T(8,128)} %get-tuple-element.14.proj_ref, f32[9,256]{1,0:T(8,128)} %get-tuple-element.15.fact_ref, s32[2,4,256]{2,1,0:T(4,128)} %cam_ref.3, s32[2,256]{1,0:T(2,128)} %bitcast.18), custom_call_target="tpu_custom_call" | custom-call | tf_op jit(solution)/shard_map/update/pallas_call | solution.py:598
  (2 shorter events, 0.0 us)
Async XLA Ops:
  0.6 2.0 %copy-start.5 = (f32[2,4,2,3,256]{4,2,3,1,0:T(2,128)S(1)}, f32[2,4,2,3,256]{4,2,3,1,0:T(2,128)}, u32[]{:S(2)}) copy-start(f32[2,4,2,3,256]{4,2,3,1,0:T(2,128)} %param.10) | copy-start | bytes 147460
  0.6 2.7 %copy-start.3 = (f32[2,4,2,9,256]{4,2,3,1,0:T(2,128)S(1)}, f32[2,4,2,9,256]{4,2,3,1,0:T(2,128)}, u32[]{:S(2)}) copy-start(f32[2,4,2,9,256]{4,2,3,1,0:T(2,128)} %param.9) | copy-start | bytes 442372
  7.6 18.8 %all-to-all-start = ((f32[16,56,128]{2,1,0:T(8,128)}), f32[16,56,128]{2,1,0:T(8,128)S(1)}, u32[]{:S(2)}, u32[]{:S(2)}) async-start(f32[16,56,128]{2,1,0:T(8,128)} %get-tuple-element.9), calls=%async_computation | async-start | bytes 917504 | tf_op jit(solution)/shard_map/all_to_all | solution.py:631
  26.3 0.8 %copy-start = (f32[16,56,128]{2,1,0:T(8,128)}, f32[16,56,128]{2,1,0:T(8,128)S(1)}, u32[]{:S(2)}) copy-start(f32[16,56,128]{2,1,0:T(8,128)S(1)} %all-to-all-done) | copy-start | bytes 1376260
  32.3 1.5 %collective-permute-start = (f32[152,128]{1,0:T(8,128)}, f32[152,128]{1,0:T(8,128)S(1)}, u32[]{:S(2)}, u32[]{:S(2)}) collective-permute-start(f32[152,128]{1,0:T(8,128)} %get-tuple-element.11), channel_id=1, source_target_pairs={{0,16},{16,0},{32,48},{48,32},{64,80},{80,64},{96,112},{112,96},{1... | collective-permute-start | bytes 233480 | tf_op jit(solution)/shard_map/ppermute | solution.py:611
  34.7 5.3 %collective-permute-start.3 = (f32[152,128]{1,0:T(8,128)S(1)}, f32[152,128]{1,0:T(8,128)S(1)}, u32[]{:S(2)}, u32[]{:S(2)}) collective-permute-start(f32[152,128]{1,0:T(8,128)S(1)} %add.17), channel_id=1, source_target_pairs={{0,96},{16,112},{32,0},{48,16},{64,32},{80,48},{96,64},{112,80},{1... | collective-permute-start | bytes 233480 | tf_op jit(solution)/shard_map/ppermute | solution.py:613
  37.8 7.0 %collective-permute-start.2 = (f32[152,128]{1,0:T(8,128)S(1)}, f32[152,128]{1,0:T(8,128)S(1)}, u32[]{:S(2)}, u32[]{:S(2)}) collective-permute-start(f32[152,128]{1,0:T(8,128)S(1)} %add.17), channel_id=1, source_target_pairs={{0,32},{16,48},{32,64},{48,80},{64,96},{80,112},{96,0},{112,16},{1... | collective-permute-start | bytes 233480 | tf_op jit(solution)/shard_map/ppermute | solution.py:613
  37.8 7.0 %collective-permute-start.1 = (f32[152,128]{1,0:T(8,128)S(1)}, f32[152,128]{1,0:T(8,128)S(1)}, u32[]{:S(2)}, u32[]{:S(2)}) collective-permute-start(f32[152,128]{1,0:T(8,128)S(1)} %add.17), channel_id=1, source_target_pairs={{0,64},{16,80},{32,96},{48,112},{64,0},{80,16},{96,32},{112,48},{1... | collective-permute-start | bytes 233480 | tf_op jit(solution)/shard_map/ppermute | solution.py:613
  44.8 1.4 %copy-start.2 = (f32[152,128]{1,0:T(8,128)}, f32[152,128]{1,0:T(8,128)S(1)}, u32[]{:S(2)}) copy-start(f32[152,128]{1,0:T(8,128)S(1)} %add_add_fusion.mine_ref) | copy-start | bytes 233476
  44.8 1.4 %collective-permute-start.4 = (f32[152,128]{1,0:T(8,128)S(1)}, f32[152,128]{1,0:T(8,128)S(1)}, u32[]{:S(2)}, u32[]{:S(2)}) collective-permute-start(f32[152,128]{1,0:T(8,128)S(1)} %add_add_fusion.mine_ref), channel_id=1, source_target_pairs={{0,16},{16,0},{32,48},{48,32},{64,80},{80,64},{96,112},{112,96},{1... | collective-permute-start | bytes 233480 | tf_op jit(solution)/shard_map/ppermute | solution.py:616
  46.2 0.6 copy-start.4
  61.6 3.7 %copy-start.6 = (f32[9,128]{1,0:T(8,128)S(1)}, f32[9,128]{1,0:T(8,128)}, u32[]{:S(2)}) copy-start(f32[9,128]{1,0:T(8,128)} %get-tuple-element.12) | copy-start | bytes 13828
  61.6 11.6 %all-to-all-start.1 = ((f32[16,16,128]{2,1,0:T(8,128)}), f32[16,16,128]{2,1,0:T(8,128)S(1)}, u32[]{:S(2)}, u32[]{:S(2)}) async-start(f32[16,16,128]{2,1,0:T(8,128)} %get-tuple-element.13), calls=%async_computation.1 | async-start | bytes 262144 | tf_op jit(solution)/shard_map/all_to_all | solution.py:635
  73.2 0.7 copy-start.1

commit v2 on v1

--- a/solution.py
+++ b/solution.py
@@ -18,7 +18,7 @@
 BAND = 304
 HALF = BAND // 2
 PACK = 56
-VMEM_LIMIT = 56 * 1024 * 1024
+MIB = 1024 * 1024
 
 
 def split3(value):
@@ -45,29 +45,23 @@
     return jnp.broadcast_to(chunk[row : row + 1, :], (8, LANES))
 
 
-def lookup_dot(table, masks, cam_ref, jac_ref, out_ref):
+def lookup_dot(table, last, masks, cam_ref, jac_ref, out_ref):
     for half in range(2):
         cols = slice(half * LANES, (half + 1) * LANES)
         for s in range(2):
+            rows, picks = masks[s][half]
             for k in range(SLOTS):
-                index = jnp.broadcast_to(cam_ref[s, k : k + 1, cols], (16, LANES))
-                sums = [None, None]
-                for i in range(PARAMS):
-                    got = jnp.concatenate(
-                        [
-                            lanes_from(table[i][0:8], index[0:8]),
-                            lanes_from(table[i][8:16], index[8:16]),
-                        ],
-                        axis=0,
-                    )
-                    for m in range(2):
-                        row = k * PARAMS + i
-                        term = got * jac_ref[m, s, row : row + 1, cols]
-                        sums[m] = term if sums[m] is None else sums[m] + term
+                index = jnp.broadcast_to(cam_ref[s, k : k + 1, cols], (8, LANES))
+                chosen = lanes_from(table[0], index)
+                for c in range(1, 16):
+                    chosen = jnp.where(picks[c], lanes_from(table[c], index), chosen)
+                ninth = lanes_from(last[0], index) * rows[0] + lanes_from(last[1], index) * rows[1]
                 for m in range(2):
+                    base = s * SLOTS * PARAMS + k * PARAMS
+                    terms = chosen * jac_ref[m, base : base + 8, cols]
+                    terms = terms + ninth * jac_ref[m, base + 8 : base + 9, cols]
                     row = s * 8 + m * 4 + k
-                    picked = jnp.sum(sums[m] * masks[s][half], axis=0, keepdims=True)
-                    out_ref[row : row + 1, cols] = picked
+                    out_ref[row : row + 1, cols] = jnp.sum(terms, axis=0, keepdims=True)
 
 
 def cluster_masks(cluster_rows):
@@ -76,7 +70,9 @@
         per_half = []
         for half in range(2):
             row = cluster_rows[s : s + 1, half * LANES : (half + 1) * LANES]
-            per_half.append((iota((16, LANES), 0) == row).astype(f32))
+            row = jnp.broadcast_to(row, (8, LANES))
+            rows = [(iota((8, LANES), 0) + 8 * n == row).astype(f32) for n in range(2)]
+            per_half.append((rows, [row == c for c in range(16)]))
         masks.append(per_half)
     return masks
 
@@ -84,6 +80,19 @@
 def points_kernel(
     owner_ref,
     damp_ref,
+    jac_hbm,
+    jp_hbm,
+    res_hbm,
+    cam_hbm,
+    count_hbm,
+    clus_hbm,
+    prev_hbm,
+    send_ref,
+    proj_ref,
+    fact_ref,
+    jm_ref,
+    dots,
+    packed,
     jac_ref,
     jp_ref,
     res_ref,
@@ -91,13 +100,28 @@
     count_ref,
     clus_ref,
     prev_ref,
-    send_ref,
-    proj_ref,
-    fact_ref,
-    dots,
-    packed,
+    arrived,
 ):
+    pairs = [
+        (clus_hbm, clus_ref),
+        (count_hbm, count_ref),
+        (jp_hbm, jp_ref),
+        (res_hbm, res_ref),
+        (cam_hbm, cam_ref),
+        (prev_hbm, prev_ref),
+        (jac_hbm, jac_ref),
+    ]
+    copies = [
+        pltpu.make_async_copy(source, target, arrived.at[n])
+        for n, (source, target) in enumerate(pairs)
+    ]
+    for copy in copies:
+        copy.start()
+    for copy in copies:
+        copy.wait()
     npts = 2 * LANES
+    for m in range(2):
+        jm_ref[m] = jac_ref[:, m, :]
     clus = clus_ref[...]
     dest = jnp.zeros_like(clus)
     for c in range(16):
@@ -106,8 +130,18 @@
     live = jnp.concatenate(
         [(slot_row < count_ref[s : s + 1, :]).astype(f32) for s in range(2)], axis=0
     )
-    jp = [jp_ref[a] * live for a in range(3)]
-    res = res_ref[...] * live
+
+    def by_slot(ref, step, first):
+        rows = [
+            ref[step * (4 * s + k) + first, m : m + 1, :]
+            for s in range(2)
+            for m in range(2)
+            for k in range(SLOTS)
+        ]
+        return jnp.concatenate(rows, axis=0) * live
+
+    jp = [by_slot(jp_ref, 3, a) for a in range(3)]
+    res = by_slot(res_ref, 1, 0)
 
     def total(value):
         return jnp.sum(value, axis=0, keepdims=True)
@@ -134,8 +168,9 @@
         fact_ref[n : n + 1, :] = row
 
     masks = cluster_masks(clus)
-    table = [prev_ref[i] for i in range(PARAMS)]
-    lookup_dot(table, masks, cam_ref, jac_ref, dots)
+    table = [prev_ref[pl.ds(c, 8, stride=16), :] for c in range(16)]
+    last = [prev_ref[128:136, :], prev_ref[136:144, :]]
+    lookup_dot(table, last, masks, cam_ref, jm_ref, dots)
     dot_all = dots[...]
     wt = -res
     for a in range(3):
@@ -153,7 +188,7 @@
             for k in range(SLOTS):
                 on = live[s * 8 + m * 4 + k : s * 8 + m * 4 + k + 1, :]
                 packed[base + 9 * k : base + 9 * k + 9, cols] = (
-                    jac_ref[m, s, 9 * k : 9 * k + 9, :] * on
+                    jm_ref[m, 36 * s + 9 * k : 36 * s + 9 * k + 9, :] * on
                 )
             rows = slice(s * 8 + m * 4, s * 8 + m * 4 + 4)
             for a in range(3):
@@ -214,12 +249,14 @@
             )
 
     sizes = [304, 224, 144, 64]
+    starts = [0, 304, 528, 672]
     out = None
     for k in range(SLOTS):
         count = 0
 
-        def put(row, value):
-            rows[8 * row : 8 * row + 8, :] = value
+        def put(row, value, k=k):
+            at = 8 * (starts[k] + row)
+            rows[at : at + 8, :] = value
 
         for dist in range(SLOTS - k):
             other = k + dist
@@ -255,13 +292,13 @@
         for row in range(count, size):
             put(row, jnp.zeros((8, LANES), f32))
         for b in range(8):
-            piece = rows[pl.ds(b, size, stride=8), :]
+            piece = rows[pl.ds(8 * starts[k] + b, size, stride=8), :]
             for n, part in enumerate(split3(piece)):
-                wide[n, 0:size, b * LANES : (b + 1) * LANES] = part
+                wide[n, starts[k] : starts[k] + size, b * LANES : (b + 1) * LANES] = part
         hot = hots[k]
-        got = dot_nt(wide[0, 0:size, :], hot)
-        got = got + dot_nt(wide[1, 0:size, :], hot)
-        got = got + dot_nt(wide[2, 0:size, :], hot)
+        got = dot_nt(wide[0, starts[k] : starts[k] + size, :], hot)
+        got = got + dot_nt(wide[1, starts[k] : starts[k] + size, :], hot)
+        got = got + dot_nt(wide[2, starts[k] : starts[k] + size, :], hot)
         if out is None:
             out = got
         else:
@@ -504,8 +541,9 @@
     for c in range(16):
         dest = jnp.where(clus == c, owner_ref[c], dest)
     masks = cluster_masks(dest)
-    table = [all_ref[pl.ds(i, 16, stride=16), :] for i in range(PARAMS)]
-    lookup_dot(table, masks, cam_ref, jac_ref, dots)
+    table = [all_ref[16 * c : 16 * c + 8, :] for c in range(16)]
+    last = [all_ref[pl.ds(8, 8, stride=16), :], all_ref[pl.ds(136, 8, stride=16), :]]
+    lookup_dot(table, last, masks, cam_ref, jac_ref, dots)
     dot_all = dots[...]
 
     def fact(n):
@@ -528,8 +566,8 @@
     return pl.BlockSpec(memory_space=pltpu.VMEM)
 
 
-def params():
-    return pltpu.CompilerParams(vmem_limit_bytes=VMEM_LIMIT)
+def params(mib):
+    return pltpu.CompilerParams(vmem_limit_bytes=mib * MIB)
 
 
 def run_points(owner_map, damping, jac, jp, res, cam_ids, obs_count, clus, prev):
@@ -540,11 +578,23 @@
             jax.ShapeDtypeStruct((16, PACK, LANES), f32),
             jax.ShapeDtypeStruct((3, 16, npts), f32),
             jax.ShapeDtypeStruct((9, npts), f32),
+            jax.ShapeDtypeStruct((2, 8 * PARAMS, npts), f32),
         ),
-        in_specs=[smem(), smem()] + [vmem()] * 7,
-        out_specs=(vmem(), vmem(), vmem()),
-        scratch_shapes=[pltpu.VMEM((16, npts), f32), pltpu.VMEM((2 * PACK, 2 * npts), f32)],
-        compiler_params=params(),
+        in_specs=[smem(), smem()] + [pl.BlockSpec(memory_space=pltpu.HBM)] * 7,
+        out_specs=(vmem(), vmem(), vmem(), vmem()),
+        scratch_shapes=[
+            pltpu.VMEM((16, npts), f32),
+            pltpu.VMEM((2 * PACK, 2 * npts), f32),
+            pltpu.VMEM(jac.shape, f32),
+            pltpu.VMEM(jp.shape, f32),
+            pltpu.VMEM(res.shape, f32),
+            pltpu.VMEM(cam_ids.shape, jnp.int32),
+            pltpu.VMEM(obs_count.shape, jnp.int32),
+            pltpu.VMEM(clus.shape, jnp.int32),
+            pltpu.VMEM(prev.shape, f32),
+            pltpu.SemaphoreType.DMA((7,)),
+        ],
+        compiler_params=params(58),
         name="points",
     )(owner_map, damping, jac, jp, res, cam_ids, obs_count, clus, prev)
 
@@ -559,11 +609,11 @@
         in_specs=[smem(), vmem()],
         out_specs=(vmem(), vmem()),
         scratch_shapes=[
-            pltpu.VMEM((BAND * 8, LANES), f32),
-            pltpu.VMEM((3, BAND, 1024), bf16),
+            pltpu.VMEM((736 * 8, LANES), f32),
+            pltpu.VMEM((3, 736, 1024), bf16),
             pltpu.VMEM((4, LANES, 1024), bf16),
         ],
-        compiler_params=params(),
+        compiler_params=params(20),
         name="band",
     )(core, recv)
 
@@ -589,7 +639,7 @@
             pltpu.VMEM((PARAMS, 32, LANES), f32),
             pltpu.VMEM((PARAMS, 32, LANES), f32),
         ],
-        compiler_params=params(),
+        compiler_params=params(12),
         name="solve",
     )(core, damping, mine, other)
 
@@ -601,7 +651,7 @@
         in_specs=[smem()] + [vmem()] * 6,
         out_specs=vmem(),
         scratch_shapes=[pltpu.VMEM((16, 256), f32)],
-        compiler_params=params(),
+        compiler_params=params(8),
         name="update",
     )(owner_map, everything, jac, proj, fact, cam_ids, clus)
 
@@ -609,10 +659,8 @@
 def sum_over_points(keep, give, ring):
     swap = [(i, i ^ 1) for i in range(ring)]
     half = keep + lax.ppermute(give, "pt", swap)
-    moved = [
-        lax.ppermute(half, "pt", [(i, (i + 2 * d) % ring) for i in range(ring)]) for d in range(1, 4)
-    ]
-    mine = (half + moved[1]) + (moved[0] + moved[2])
+    moved = [lax.ppermute(half, "pt", [(i, i ^ (2 * d)) for i in range(ring)]) for d in (1, 2, 3)]
+    mine = (half + moved[0]) + (moved[1] + moved[2])
     return mine, lax.ppermute(mine, "pt", swap)
 
 
@@ -621,12 +669,16 @@
 ):
     npts = cam_jac.shape[-1]
     core = (lax.axis_index("pt") % 2).astype(jnp.int32).reshape(1)
-    jac = cam_jac.transpose(2, 0, 1, 3, 4).reshape(2, 2, SLOTS * PARAMS, npts)
-    jp = pt_jac.transpose(3, 0, 2, 1, 4).reshape(3, 16, npts)
-    res = residual.transpose(0, 2, 1, 3).reshape(16, npts)
-    clus = clusters.T
-    send, proj, fact = run_points(
-        owner_map, damping, jac, jp, res, cam_ids, obs_count, clus, prev_step.transpose(1, 0, 2)
+    send, proj, fact, jac = run_points(
+        owner_map,
+        damping,
+        cam_jac.transpose(0, 1, 3, 2, 4).reshape(8 * PARAMS, 2, npts),
+        pt_jac.transpose(0, 1, 3, 2, 4).reshape(24, 2, npts),
+        residual.reshape(8, 2, npts),
+        cam_ids,
+        obs_count,
+        clusters.T,
+        prev_step.transpose(1, 0, 2).reshape(PARAMS * 16, LANES),
     )
     recv = lax.all_to_all(send, "cl", split_axis=0, concat_axis=0, tiled=True)
     keep, give = run_band(core, recv.reshape(16 * PACK, LANES))
@@ -634,7 +686,7 @@
     step, cast = run_solve(core, damping, mine, other)
     everything = lax.all_to_all(cast, "cl", split_axis=0, concat_axis=0, tiled=True)
     point_step = run_update(
-        owner_map, everything.reshape(256, LANES), jac, proj, fact, cam_ids, clus
+        owner_map, everything.reshape(256, LANES), jac, proj, fact, cam_ids, clusters.T
     )
     return (step[None], point_step)
 

time: 76.5 us -> 67.8 us (0.89)
  local copies, waits for them, and re-layouts: 5.33 us -> 1.27 us
  Pallas kernels: 25.7 us -> 22.8 us
  starting transfers between devices: 17 us -> 16 us
  other arithmetic: 0.92 us -> 0.03 us
    pallas_call x1, Pallas kernels: 5.21 us -> 2.96 us  [run_band(): pl.pallas_call(band_kernel, out_shape=(jax.ShapeDtypeStruct((HALF, LANES)...]
    reshape x3 -> x0, local copies, waits for them, and re-layouts: 1.93 us -> none  [the longest x1 0.68 us: per_device(): jac = cam_jac.transpose(2, 0, 1, 3, 4).reshape(2, 2, SLOTS * PARAMS, npts)]
    unnamed x15 -> x13, local copies, waits for them, and re-layouts: 2.66 us -> 1.27 us
    ppermute x3, starting transfers between devices: 5.29 us -> 4.17 us  [sum_over_points(): lax.ppermute(half, 'pt', [(i, i ^ 2 * d) for i in range(ring)])]
    pallas_call x1, Pallas kernels: 14.8 us -> 13.9 us  [run_solve(): pl.pallas_call(solve_kernel, out_shape=(jax.ShapeDtypeStruct((PARAMS, LAN...]
    add x1, other arithmetic: 0.9 us -> 0.01 us  [sum_over_points(): half = keep + lax.ppermute(give, 'pt', swap)]
    pallas_call x1, Pallas kernels: 3.55 us -> 4.34 us  [run_points(): pl.pallas_call(points_kernel, out_shape=(jax.ShapeDtypeStruct((16, PACK,...]
  transfers between devices with their start and end apart: 7 -> 7, of which waited for: 5 -> 6; matrix products, arithmetic and copies ran while one was open for 1% -> 1% of each run, Pallas kernels for 0% -> 0%
where the time goes in v2:
time: 67.8 us; the launch traced here: 67.4 us
  waiting for transfers between devices  26 us (38%)
  Pallas kernels  22.8 us (34%)
  starting transfers between devices  16 us (24%)
  between operations  1.38 us (2%)
  local copies, waits for them, and re-layouts  1.27 us (2%)
    pallas_call x1, Pallas kernels, run_solve(): pl.pallas_call(solve_kernel, out_shape=(jax.ShapeDtypeStruct((PARAMS, LAN...  13.9 us
    all_to_all x1, waiting for transfers between devices, per_device(): recv = lax.all_to_all(send, 'cl', split_axis=0, concat_axis=0, tiled=True)  10.8 us
    all_to_all x1, starting transfers between devices, per_device(): recv = lax.all_to_all(send, 'cl', split_axis=0, concat_axis=0, tiled=True)  7.97 us
    all_to_all x1, waiting for transfers between devices, per_device(): lax.all_to_all(cast, 'cl', split_axis=0, concat_axis=0, tiled=True)  7.34 us
    ppermute x3, waiting for transfers between devices, sum_over_points(): lax.ppermute(half, 'pt', [(i, i ^ 2 * d) for i in range(ring)])  5.4 us
    pallas_call x1, Pallas kernels, run_points(): pl.pallas_call(points_kernel, out_shape=(jax.ShapeDtypeStruct((16, PACK,...  4.34 us
    ppermute x3, starting transfers between devices, sum_over_points(): lax.ppermute(half, 'pt', [(i, i ^ 2 * d) for i in range(ring)])  4.17 us
    all_to_all x1, starting transfers between devices, per_device(): lax.all_to_all(cast, 'cl', split_axis=0, concat_axis=0, tiled=True)  3.64 us
  transfers between devices with their start and end apart: 7, of which 6 were waited for; matrix products, arithmetic and copies ran while one was open for 1% of the time, Pallas kernels for 0%

profile of v2, /device:TPU:0, one launch (start us, length us, event | category | flops | bytes accessed | tf_op | source)
XLA Modules:
  0.0 67.4 jit_solution(5846002315563242404)
XLA Ops:
  1.3 4.3 %points.1 = (f32[16,56,128]{2,1,0:T(8,128)}, f32[3,16,256]{2,1,0:T(8,128)}, f32[9,256]{1,0:T(8,128)}, f32[2,72,256]{2,1,0:T(8,128)}) custom-call(s32[16]{0:T(128)} %owner_ref.3, f32[1]{0:T(128)S(6)} %copy.12.damp_ref, f32[72,2,256]{2,1,0:T(2,128)} %bitcast.20, f32[24,2,256]{2,1,0:T(2,128)} %bitcast.22, f32[8,2,256]{2,1,0:T(2,128)} %bitcast.23, ...), custom_call_target="tpu_custom_call" | custom-call | tf_op jit(solution)/shard_map/points/pallas_call | solution.py:575
  5.6 8.0 %all-to-all-start = ((f32[16,56,128]{2,1,0:T(8,128)}), f32[16,56,128]{2,1,0:T(8,128)S(1)}, u32[]{:S(2)}, u32[]{:S(2)}) async-start(f32[16,56,128]{2,1,0:T(8,128)} %get-tuple-element.10), calls=%async_computation | async-start | bytes 917504 | tf_op jit(solution)/shard_map/all_to_all | solution.py:683
  13.6 10.8 %all-to-all-done = f32[16,56,128]{2,1,0:T(8,128)S(1)} async-done(((f32[16,56,128]{2,1,0:T(8,128)}), f32[16,56,128]{2,1,0:T(8,128)S(1)}, u32[]{:S(2)}, u32[]{:S(2)}) %all-to-all-start) | async-done | bytes 458784 | tf_op jit(solution)/shard_map/all_to_all | solution.py:683
  24.4 3.0 %band.1 = (f32[152,128]{1,0:T(8,128)S(1)}, f32[152,128]{1,0:T(8,128)S(1)}) custom-call(s32[1]{0:T(128)} %bitcast.core_ref, f32[896,128]{1,0:T(8,128)S(1)} %bitcast.15), custom_call_target="tpu_custom_call" | custom-call | tf_op jit(solution)/shard_map/band/pallas_call | solution.py:603
  27.4 0.1 collective-permute-start
  27.5 1.3 %collective-permute-done = f32[152,128]{1,0:T(8,128)S(1)} collective-permute-done((f32[152,128]{1,0:T(8,128)S(1)}, f32[152,128]{1,0:T(8,128)S(1)}, u32[]{:S(2)}, u32[]{:S(2)}) %collective-permute-start) | collective-permute-done | bytes 77856 | tf_op jit(solution)/shard_map/ppermute | solution.py:661
  28.7 3.1 %collective-permute-start.3 = (f32[152,128]{1,0:T(8,128)S(1)}, f32[152,128]{1,0:T(8,128)S(1)}, u32[]{:S(2)}, u32[]{:S(2)}) collective-permute-start(f32[152,128]{1,0:T(8,128)S(1)} %add.17), channel_id=1, source_target_pairs={{0,96},{16,112},{32,64},{48,80},{64,32},{80,48},{96,0},{112,16},{1... | collective-permute-start | bytes 233480 | tf_op jit(solution)/shard_map/ppermute | solution.py:662
  31.8 0.6 collective-permute-start.2
  32.5 0.4 collective-permute-start.1
  32.9 2.6 %collective-permute-done.3 = f32[152,128]{1,0:T(8,128)S(1)} collective-permute-done((f32[152,128]{1,0:T(8,128)S(1)}, f32[152,128]{1,0:T(8,128)S(1)}, u32[]{:S(2)}, u32[]{:S(2)}) %collective-permute-start.3) | collective-permute-done | bytes 77856 | tf_op jit(solution)/shard_map/ppermute | solution.py:662
  35.5 2.8 %collective-permute-done.2 = f32[152,128]{1,0:T(8,128)S(1)} collective-permute-done((f32[152,128]{1,0:T(8,128)S(1)}, f32[152,128]{1,0:T(8,128)S(1)}, u32[]{:S(2)}, u32[]{:S(2)}) %collective-permute-start.2) | collective-permute-done | bytes 77856 | tf_op jit(solution)/shard_map/ppermute | solution.py:662
  38.3 0.0 collective-permute-done.1
  38.3 0.1 collective-permute-start.4
  38.4 1.3 %collective-permute-done.4.other_ref = f32[152,128]{1,0:T(8,128)S(1)} collective-permute-done((f32[152,128]{1,0:T(8,128)S(1)}, f32[152,128]{1,0:T(8,128)S(1)}, u32[]{:S(2)}, u32[]{:S(2)}) %collective-permute-start.4) | collective-permute-done | bytes 77856 | tf_op jit(solution)/shard_map/ppermute | solution.py:664
  39.7 13.9 %solve.1 = (f32[9,128]{1,0:T(8,128)S(1)}, f32[16,16,128]{2,1,0:T(8,128)}) custom-call(s32[1]{0:T(128)} %bitcast.core_ref, f32[1]{0:T(128)S(6)} %copy.12.damp_ref, f32[152,128]{1,0:T(8,128)S(1)} %add_add_fusion.mine_ref, f32[152,128]{1,0:T(8,128)S(1)} %collective-permute-done.4.other_ref), custom_call_target="tpu_custom_call" | custom-call | tf_op jit(solution)/shard_map/solve/pallas_call | solution.py:622
  53.6 0.0 copy-start
  53.6 0.0 copy-start.1
  53.6 0.0 copy-start.3
  53.6 3.6 %all-to-all-start.1 = ((f32[16,16,128]{2,1,0:T(8,128)}), f32[16,16,128]{2,1,0:T(8,128)S(1)}, u32[]{:S(2)}, u32[]{:S(2)}) async-start(f32[16,16,128]{2,1,0:T(8,128)} %get-tuple-element.14), calls=%async_computation.1 | async-start | bytes 262144 | tf_op jit(solution)/shard_map/all_to_all | solution.py:687
  57.2 0.0 copy-start.2
  57.2 0.6 copy.11
  57.8 7.3 %all-to-all-done.1 = f32[16,16,128]{2,1,0:T(8,128)S(1)} async-done(((f32[16,16,128]{2,1,0:T(8,128)}), f32[16,16,128]{2,1,0:T(8,128)S(1)}, u32[]{:S(2)}, u32[]{:S(2)}) %all-to-all-start.1) | async-done | bytes 131104 | tf_op jit(solution)/shard_map/all_to_all | solution.py:687
  65.2 0.0 copy-start.4
  65.2 0.0 copy-start.5
  65.2 0.0 copy-done
  65.2 0.0 copy-done.1
  65.2 0.0 copy-done.3
  65.2 0.0 copy-done.2
  65.2 0.6 copy-done.4
  65.8 0.0 copy-done.5
  65.8 1.6 %update.1 = f32[3,256]{1,0:T(4,128)} custom-call(s32[16]{0:T(128)S(1)} %copy-done.5, f32[256,128]{1,0:T(8,128)S(1)} %bitcast.16, f32[2,72,256]{2,1,0:T(8,128)S(1)} %copy-done, f32[3,16,256]{2,1,0:T(8,128)S(1)} %copy-done.1, f32[9,256]{1,0:T(8,128)S(1)} %copy-done.3, s32[2,4,256]{2,1,0:T(4,128)S(1)} %copy-done.2, s32[2,256]{1,0:T(2,128)S(1)} %bitcast.18), custom_call_target="tpu_custom_call" | custom-call | tf_op jit(solution)/shard_map/update/pallas_call | solution.py:648
  (2 shorter events, 0.0 us)
Async XLA Ops:
  5.6 18.8 %all-to-all-start = ((f32[16,56,128]{2,1,0:T(8,128)}), f32[16,56,128]{2,1,0:T(8,128)S(1)}, u32[]{:S(2)}, u32[]{:S(2)}) async-start(f32[16,56,128]{2,1,0:T(8,128)} %get-tuple-element.10), calls=%async_computation | async-start | bytes 917504 | tf_op jit(solution)/shard_map/all_to_all | solution.py:683
  27.4 1.4 %collective-permute-start = (f32[152,128]{1,0:T(8,128)S(1)}, f32[152,128]{1,0:T(8,128)S(1)}, u32[]{:S(2)}, u32[]{:S(2)}) collective-permute-start(f32[152,128]{1,0:T(8,128)S(1)} %get-tuple-element.12), channel_id=1, source_target_pairs={{0,16},{16,0},{32,48},{48,32},{64,80},{80,64},{96,112},{112,96},{1... | collective-permute-start | bytes 233480 | tf_op jit(solution)/shard_map/ppermute | solution.py:661
  28.7 6.7 %collective-permute-start.3 = (f32[152,128]{1,0:T(8,128)S(1)}, f32[152,128]{1,0:T(8,128)S(1)}, u32[]{:S(2)}, u32[]{:S(2)}) collective-permute-start(f32[152,128]{1,0:T(8,128)S(1)} %add.17), channel_id=1, source_target_pairs={{0,96},{16,112},{32,64},{48,80},{64,32},{80,48},{96,0},{112,16},{1... | collective-permute-start | bytes 233480 | tf_op jit(solution)/shard_map/ppermute | solution.py:662
  31.8 6.5 %collective-permute-start.2 = (f32[152,128]{1,0:T(8,128)S(1)}, f32[152,128]{1,0:T(8,128)S(1)}, u32[]{:S(2)}, u32[]{:S(2)}) collective-permute-start(f32[152,128]{1,0:T(8,128)S(1)} %add.17), channel_id=1, source_target_pairs={{0,64},{16,80},{32,96},{48,112},{64,0},{80,16},{96,32},{112,48},{1... | collective-permute-start | bytes 233480 | tf_op jit(solution)/shard_map/ppermute | solution.py:662
  32.5 5.8 %collective-permute-start.1 = (f32[152,128]{1,0:T(8,128)S(1)}, f32[152,128]{1,0:T(8,128)S(1)}, u32[]{:S(2)}, u32[]{:S(2)}) collective-permute-start(f32[152,128]{1,0:T(8,128)S(1)} %add.17), channel_id=1, source_target_pairs={{0,32},{16,48},{32,0},{48,16},{64,96},{80,112},{96,64},{112,80},{1... | collective-permute-start | bytes 233480 | tf_op jit(solution)/shard_map/ppermute | solution.py:662
  38.3 1.4 %collective-permute-start.4 = (f32[152,128]{1,0:T(8,128)S(1)}, f32[152,128]{1,0:T(8,128)S(1)}, u32[]{:S(2)}, u32[]{:S(2)}) collective-permute-start(f32[152,128]{1,0:T(8,128)S(1)} %add_add_fusion.mine_ref), channel_id=1, source_target_pairs={{0,16},{16,0},{32,48},{48,32},{64,80},{80,64},{96,112},{112,96},{1... | collective-permute-start | bytes 233480 | tf_op jit(solution)/shard_map/ppermute | solution.py:664
  53.6 11.6 %copy-start = (f32[2,72,256]{2,1,0:T(8,128)S(1)}, f32[2,72,256]{2,1,0:T(8,128)}, u32[]{:S(2)}) copy-start(f32[2,72,256]{2,1,0:T(8,128)} %get-tuple-element.15.jac_ref) | copy-start | bytes 442372
  53.6 11.6 %copy-start.1 = (f32[3,16,256]{2,1,0:T(8,128)S(1)}, f32[3,16,256]{2,1,0:T(8,128)}, u32[]{:S(2)}) copy-start(f32[3,16,256]{2,1,0:T(8,128)} %get-tuple-element.16.proj_ref) | copy-start | bytes 147460
  53.6 11.6 %copy-start.3 = (f32[9,256]{1,0:T(8,128)S(1)}, f32[9,256]{1,0:T(8,128)}, u32[]{:S(2)}) copy-start(f32[9,256]{1,0:T(8,128)} %get-tuple-element.17.fact_ref) | copy-start | bytes 27652
  53.6 11.6 %all-to-all-start.1 = ((f32[16,16,128]{2,1,0:T(8,128)}), f32[16,16,128]{2,1,0:T(8,128)S(1)}, u32[]{:S(2)}, u32[]{:S(2)}) async-start(f32[16,16,128]{2,1,0:T(8,128)} %get-tuple-element.14), calls=%async_computation.1 | async-start | bytes 262144 | tf_op jit(solution)/shard_map/all_to_all | solution.py:687
  57.2 8.0 %copy-start.2 = (s32[2,4,256]{2,1,0:T(4,128)S(1)}, s32[2,4,256]{2,1,0:T(4,128)}, u32[]{:S(2)}) copy-start(s32[2,4,256]{2,1,0:T(4,128)} %cam_ref.1) | copy-start | bytes 24580
  65.2 0.7 %copy-start.4 = (s32[256,2]{0,1:T(2,128)S(1)}, s32[256,2]{0,1:T(2,128)}, u32[]{:S(2)}) copy-start(s32[256,2]{0,1:T(2,128)} %param.14) | copy-start | bytes 6148
  65.2 0.7 %copy-start.5 = (s32[16]{0:T(128)S(1)}, s32[16]{0:T(128)}, u32[]{:S(2)}) copy-start(s32[16]{0:T(128)} %owner_ref.3) | copy-start | bytes 196

commit v3 on v2

--- a/solution.py
+++ b/solution.py
@@ -11,10 +11,12 @@
 SLOTS = 4
 PARAMS = 9
 GROUPS = 32
+BLOCK = 9
 UNK = 27
-DIAG = 45
 ROW_Q = 45
 ROW_D = (0, 54, 135, 216)
+ROW_END = (54, 135, 216, 297)
+NEEDED = ({0, 1, 2, 3}, {0, 1, 2}, {0, 1, 3}, {0, 2, 3})
 BAND = 304
 HALF = BAND // 2
 PACK = 56
@@ -91,6 +93,8 @@
     proj_ref,
     fact_ref,
     jm_ref,
+    where_ref,
+    dest_ref,
     dots,
     packed,
     jac_ref,
@@ -126,6 +130,8 @@
     dest = jnp.zeros_like(clus)
     for c in range(16):
         dest = jnp.where(clus == c, owner_ref[c], dest)
+    dest_ref[...] = dest
+    where_ref[...] = cam_ref[...]
     slot_row = iota((8, npts), 0) % 4
     live = jnp.concatenate(
         [(slot_row < count_ref[s : s + 1, :]).astype(f32) for s in range(2)], axis=0
@@ -206,17 +212,19 @@
     parts = split3(packed[...])
     left = jnp.concatenate(parts, axis=0)
     low_half = iota((PACK, LANES), 1) < 64
-    for pair in range(8):
-        slots = iota((LANES, 2 * npts), 0) + pair * LANES
+    for quad in range(4):
+        slots = iota((2 * LANES, 2 * npts), 0) + quad * 2 * LANES
         pick = (slots == slot).astype(f32).astype(bf16)
         got = dot_nt(left, pick)
         full = got[0 : 2 * PACK] + got[2 * PACK : 4 * PACK] + got[4 * PACK : 6 * PACK]
-        first = full[0:PACK]
-        second = full[PACK : 2 * PACK]
-        first_r = pltpu.roll(first, 64, 1)
-        second_r = pltpu.roll(second, 64, 1)
-        send_ref[2 * pair] = jnp.where(low_half, first, second_r)
-        send_ref[2 * pair + 1] = jnp.where(low_half, first_r, second)
+        for pair in range(2):
+            cols = slice(pair * LANES, (pair + 1) * LANES)
+            first = full[0:PACK, cols]
+            second = full[PACK : 2 * PACK, cols]
+            first_r = pltpu.roll(first, 64, 1)
+            second_r = pltpu.roll(second, 64, 1)
+            send_ref[4 * quad + 2 * pair] = jnp.where(low_half, first, second_r)
+            send_ref[4 * quad + 2 * pair + 1] = jnp.where(low_half, first_r, second)
 
 
 def band_kernel(core_ref, recv_ref, keep_ref, give_ref, rows, wide, hots):
@@ -330,27 +338,25 @@
     return inverse
 
 
-def schur(size, side, lane):
+def schur(size, side, lane, whole):
     within = lane % GROUPS
     results = []
     for which in range(2):
-        full = []
         for r in range(size):
-            full.append(
-                [
-                    lanes_from(side[r][v % 2], within + GROUPS * (2 * which + v // 2))
-                    for v in range(4)
-                ]
-            )
-        per_a = []
-        for a in range(UNK):
-            acc = [None, None]
+            for v in range(4):
+                at = 32 * (which * UNK + r) + 8 * v
+                whole[at : at + 8, :] = lanes_from(
+                    side[r][v % 2], within + GROUPS * (2 * which + v // 2)
+                )
+        per_a = [[None, None] for a in range(UNK)]
+        for first in range(0, UNK, BLOCK):
             for r in range(size):
-                coef = spread_row(full[r][a // 8], a % 8)
-                for e in range(2):
-                    term = coef * side[r][e]
-                    acc[e] = term if acc[e] is None else acc[e] + term
-            per_a.append(acc)
+                for a in range(first, min(first + BLOCK, UNK)):
+                    at = 32 * (which * UNK + r) + a
+                    coef = jnp.broadcast_to(whole[at : at + 1, :], (8, LANES))
+                    for e in range(2):
+                        term = coef * side[r][e]
+                        per_a[a][e] = term if r == 0 else per_a[a][e] + term
         results.append(per_a)
     return results
 
@@ -385,9 +391,10 @@
 
 
 def solve_kernel(
-    core_ref, damp_ref, mine_ref, other_ref, step_ref, cast_ref, rep, back, dmat, lmat, umat, smat, xrow, d0, l0, u0
+    core_ref, damp_ref, mine_ref, other_ref, step_ref, cast_ref, rep, back, dmat, smat, xrow, whole
 ):
     lane = iota((8, LANES), 1)
+    sub = iota((8, LANES), 0)
     within = lane % GROUPS
     part = lane // GROUPS
     core = core_ref[0]
@@ -401,103 +408,139 @@
     first_rows = HALF // 8
     for n in range(BAND // 8):
         chunk = low[8 * n : 8 * n + 8] if n < first_rows else high[8 * n - HALF : 8 * n - HALF + 8]
+        at = slice(8 * n, 8 * n + 8)
+        kinds = {d for d in range(4) if ROW_D[d] < 8 * n + 8 and 8 * n < ROW_END[d]}
         for r in range(4):
-            rep[r, 8 * n : 8 * n + 8, :] = lanes_from(chunk, within + GROUPS * r)
-            if r > 0:
-                back[r - 1, 8 * n : 8 * n + 8, :] = lanes_from(
+            if kinds & NEEDED[r]:
+                rep[r, at, :] = lanes_from(chunk, within + GROUPS * r)
+            if r > 0 and kinds & set(range(4 - r, 4)):
+                back[r - 1, at, :] = lanes_from(
                     chunk, (within + GROUPS - 1) % GROUPS + GROUPS * r
                 )
-    zero = jnp.zeros((UNK, 32, LANES), f32)
-    dmat[...] = zero
-    lmat[...] = zero
-    umat[...] = zero
-    d0[...] = jnp.zeros_like(d0)
-    l0[...] = jnp.zeros_like(l0)
-    u0[...] = jnp.zeros_like(u0)
 
     def tri(i):
         return i * 9 - i * (i - 1) // 2
 
-    for i in range(PARAMS):
-        d0[i, i:9, :] = rep[0, tri(i) : tri(i) + 9 - i, :]
-        for d in range(1, 4):
-            u0[i, 9 * d - 9 : 9 * d, :] = rep[0, ROW_D[d] + 9 * i : ROW_D[d] + 9 * i + 9, :]
-            l0[i, 27 - 9 * d : 36 - 9 * d, :] = back[3 - d, pl.ds(ROW_D[d] + i, 9, stride=9), :]
-        l0[i, 27:28, :] = rep[0, ROW_Q + i : ROW_Q + i + 1, :]
-        for r in range(1, 4):
-            row = 9 * r - 9 + i
-            dmat[row, row : 9 * r, :] = rep[r, tri(i) : tri(i) + 9 - i, :]
-            for q in range(r + 1, 4):
-                base = ROW_D[q - r] + 9 * i
-                dmat[row, 9 * q - 9 : 9 * q, :] = rep[r, base : base + 9, :]
-            for q in range(1, 4):
-                if q < r:
-                    base = ROW_D[4 + q - r] + 9 * i
-                    umat[row, 9 * q - 9 : 9 * q, :] = rep[r, base : base + 9, :]
-                if q > r:
-                    base = ROW_D[4 + r - q] + i
-                    lmat[row, 9 * q - 9 : 9 * q, :] = back[q - 1, pl.ds(base, 9, stride=9), :]
-            lmat[row, 27:28, :] = rep[r, ROW_Q + i : ROW_Q + i + 1, :]
+    def line(ref, r, start):
+        return jnp.broadcast_to(ref[r, start : start + 1, :], (8, LANES))
+
+    def tail(values):
+        out = jnp.zeros((8, LANES), f32)
+        for n, value in values:
+            out = jnp.where(sub == n, value, out)
+        return out
+
+    def forward(r, d, i):
+        start = tri(i) - i if d == 0 else ROW_D[d] + 9 * i
+        return rep[r, start : start + 8, :], line(rep, r, start + 8)
+
+    def backward(r, d, i):
+        start = ROW_D[d] + i
+        return back[r - 1, pl.ds(start, 8, stride=9), :], line(back, r - 1, start + 72)
 
     def pack(lm, um):
         return [
             jnp.where(
                 part == 0,
-                lm[8 * e : 8 * e + 8],
-                jnp.where(
-                    part == 1,
-                    lm[16 + 8 * e : 24 + 8 * e],
-                    jnp.where(part == 2, um[8 * e : 8 * e + 8], um[16 + 8 * e : 24 + 8 * e]),
-                ),
+                lm[e],
+                jnp.where(part == 1, lm[2 + e], jnp.where(part == 2, um[e], um[2 + e])),
             )
             for e in range(2)
         ]
 
+    def rhs(r, i):
+        return line(rep, r, ROW_Q + i)
+
     def chunked(value, count):
         return [value[8 * v : 8 * v + 8] for v in range(count)]
 
-    diag0 = [chunked(d0[i], 2) for i in range(PARAMS)]
-    side0 = [pack(l0[i], u0[i]) for i in range(PARAMS)]
+    zero = jnp.zeros((8, LANES), f32)
+
+    diag0, side0 = [], []
+    for i in range(PARAMS):
+        diag0.append(list(forward(0, 0, i)))
+        after = [forward(0, d, i) for d in (1, 2, 3)]
+        before = [backward(4 - d, d, i) for d in (3, 2, 1)]
+        lm = [p[0] for p in before]
+        lm.append(tail([(n, p[1]) for n, p in enumerate(before)] + [(3, rhs(0, i))]))
+        um = [p[0] for p in after]
+        um.append(tail([(n, p[1]) for n, p in enumerate(after)]))
+        side0.append(pack(lm, um))
     inv0 = factor(PARAMS, diag0, side0, (0, 1))
-    left, right = schur(PARAMS, side0, lane)
-    diag = [chunked(dmat[a], 4) for a in range(UNK)]
-    side = [pack(lmat[a], umat[a]) for a in range(UNK)]
+    left, right = schur(PARAMS, side0, lane, whole)
+
+    diag, side = [], []
+    for a in range(UNK):
+        r, i = (a // 8 + 1, a % 8) if a < 24 else (a - 23, 8)
+        own = {q: forward(r, q - r, i) for q in range(r, 4)}
+        ahead = {q: forward(r, 4 + q - r, i) for q in range(1, r)}
+        behind = {q: backward(q, 4 + r - q, i) for q in range(r + 1, 4)}
+        diag.append([own[q][0] if q in own else zero for q in (1, 2, 3)])
+        ninths = [(q - 1, p[1]) for q, p in own.items()]
+        ninths += [(q - 1, line(rep, q, ROW_D[r - q] + 72 + i)) for q in range(1, r)]
+        diag[a].append(tail(ninths))
+        um = [ahead[q][0] if q in ahead else zero for q in (1, 2, 3)]
+        um.append(tail([(q - 1, p[1]) for q, p in ahead.items()]))
+        lm = [behind[q][0] if q in behind else zero for q in (1, 2, 3)]
+        lm.append(tail([(q - 1, p[1]) for q, p in behind.items()] + [(3, rhs(r, i))]))
+        side.append(pack(lm, um))
     apply_schur(left, right, diag, side, lane, 0, 1, True)
-    for a in range(UNK):
-        for v in range(4):
-            dmat[a, 8 * v : 8 * v + 8, :] = diag[a][v]
-        for e in range(2):
-            smat[a, 8 * e : 8 * e + 8, :] = side[a][e]
-
-    def level(step, carry):
-        stride = lax.shift_left(jnp.int32(1), step)
-        diag_in = [chunked(dmat[a], 4) for a in range(UNK)]
-        side_in = [chunked(smat[a], 2) for a in range(UNK)]
-        diag = [list(row) for row in diag_in]
-        side = [list(row) for row in side_in]
-        factor(UNK, diag, side, (0, 1))
-        left, right = schur(UNK, side, lane)
-        diag = [list(row) for row in diag_in]
-        side = [list(row) for row in side_in]
-        apply_schur(left, right, diag, side, lane, stride, stride, False)
+
+    def store(diag, side):
         for a in range(UNK):
-            for v in range(4):
+            for v in range(a // 8, 4):
                 dmat[a, 8 * v : 8 * v + 8, :] = diag[a][v]
             for e in range(2):
                 smat[a, 8 * e : 8 * e + 8, :] = side[a][e]
+
+    def load():
+        diag = [
+            [dmat[a, 8 * v : 8 * v + 8, :] if v >= a // 8 else None for v in range(4)]
+            for a in range(UNK)
+        ]
+        return diag, [chunked(smat[a], 2) for a in range(UNK)]
+
+    store(diag, side)
+
+    def level(step, carry):
+        stride = lax.shift_left(jnp.int32(1), step)
+        diag, side = load()
+        factor(UNK, diag, side, (0, 1))
+        left, right = schur(UNK, side, lane, whole)
+        diag, side = load()
+        apply_schur(left, right, diag, side, lane, stride, stride, False)
+        store(diag, side)
         return carry
 
-    lax.fori_loop(0, 5, level, jnp.int32(0))
-
-    diag = [chunked(dmat[a], 4) for a in range(UNK)]
-    side = [chunked(smat[a], 2) for a in range(UNK)]
+    lax.fori_loop(0, 4, level, jnp.int32(0))
+
+    diag, side = load()
+    both = []
     for a in range(UNK):
+        halves = []
+        for base in (0, 2 * GROUPS):
+            index = within + GROUPS * (part // 2) + base
+            halves.append(
+                jnp.where(
+                    part % 2 == 0, lanes_from(side[a][0], index), lanes_from(side[a][1], index)
+                )
+            )
+        both.append([halves[0] + halves[1]])
+        right_side = lanes_from(side[a][1], within + GROUPS)
+        diag[a][3] = jnp.where(sub == 3, right_side, diag[a][3])
+    work = [list(line_of) for line_of in diag]
+    factor(UNK, work, both, (0,))
+    full = [[lanes_from(both[r][0], within + GROUPS * v) for v in range(4)] for r in range(UNK)]
+    for a in range(UNK):
+        acc = None
+        for r in range(UNK):
+            term = spread_row(full[r][a // 8], a % 8) * both[r][0]
+            acc = term if acc is None else acc + term
         for v in range(a // 8, 4):
-            from_l = lanes_from(side[a][v % 2], within + GROUPS * (v // 2))
-            from_u = lanes_from(side[a][v % 2], within + GROUPS * (2 + v // 2))
-            diag[a][v] = diag[a][v] + from_l + from_u
-    inverse = factor(UNK, diag, side, (1,))
-    todo = [spread_row(lanes_from(side[a][1], within + GROUPS), 3) for a in range(UNK)]
+            moved = lanes_from(acc, (within + 16) % GROUPS + GROUPS * v)
+            diag[a][v] = diag[a][v] - moved
+    inverse = factor(UNK, diag, both, ())
+    todo = [spread_row(diag[a][3], 3) for a in range(UNK)]
     value = [None] * UNK
     for k in range(UNK - 1, -1, -1):
         value[k] = todo[k] * inverse[k]
@@ -508,15 +551,15 @@
     xrow[UNK:32, :] = jnp.zeros((5, LANES), f32)
     own = chunked(xrow[...], 4)
     prev = [lanes_from(c, (lane + LANES - 1) % LANES) for c in own]
-    both = pack(jnp.concatenate(prev, axis=0), jnp.concatenate(own, axis=0))
+    packed = pack(prev, own)
     todo0 = []
     for i in range(PARAMS):
-        terms = side0[i][0] * both[0] + side0[i][1] * both[1]
+        terms = side0[i][0] * packed[0] + side0[i][1] * packed[1]
         terms = terms + pltpu.roll(terms, 64, 1)
         terms = terms + pltpu.roll(terms, 32, 1)
-        rhs = spread_row(lanes_from(side0[i][1], within + GROUPS), 3)
+        right_side = spread_row(lanes_from(side0[i][1], within + GROUPS), 3)
         summed = jnp.broadcast_to(jnp.sum(terms, axis=0, keepdims=True), (8, LANES))
-        todo0.append(rhs - summed)
+        todo0.append(right_side - summed)
     value0 = [None] * PARAMS
     for k in range(PARAMS - 1, -1, -1):
         value0[k] = todo0[k] * inv0[k]
@@ -524,23 +567,20 @@
             todo0[r] = todo0[r] - spread_row(diag0[r][k // 8], k % 8) * value0[k]
     camera = (lane % 4) * GROUPS + lane // 4
     for i in range(PARAMS):
-        row = jnp.where(
+        near = [value[8 * r + i] if i < 8 else value[24 + r] for r in range(3)]
+        mixed = jnp.where(
             part == 0,
             value0[i],
-            jnp.where(part == 1, value[i], jnp.where(part == 2, value[9 + i], value[18 + i])),
+            jnp.where(part == 1, near[0], jnp.where(part == 2, near[1], near[2])),
         )
-        step_ref[i : i + 1, :] = lanes_from(row, camera)[0:1]
+        step_ref[i : i + 1, :] = lanes_from(mixed, camera)[0:1]
     for dest in range(16):
         cast_ref[dest, 0:PARAMS, :] = step_ref[...]
         cast_ref[dest, PARAMS:16, :] = jnp.zeros((16 - PARAMS, LANES), f32)
 
 
-def update_kernel(owner_ref, all_ref, jac_ref, proj_ref, fact_ref, cam_ref, clus_ref, out_ref, dots):
-    clus = clus_ref[...]
-    dest = jnp.zeros_like(clus)
-    for c in range(16):
-        dest = jnp.where(clus == c, owner_ref[c], dest)
-    masks = cluster_masks(dest)
+def update_kernel(all_ref, jac_ref, proj_ref, fact_ref, cam_ref, dest_ref, out_ref, dots):
+    masks = cluster_masks(dest_ref[...])
     table = [all_ref[16 * c : 16 * c + 8, :] for c in range(16)]
     last = [all_ref[pl.ds(8, 8, stride=16), :], all_ref[pl.ds(136, 8, stride=16), :]]
     lookup_dot(table, last, masks, cam_ref, jac_ref, dots)
@@ -579,9 +619,11 @@
             jax.ShapeDtypeStruct((3, 16, npts), f32),
             jax.ShapeDtypeStruct((9, npts), f32),
             jax.ShapeDtypeStruct((2, 8 * PARAMS, npts), f32),
+            jax.ShapeDtypeStruct(cam_ids.shape, jnp.int32),
+            jax.ShapeDtypeStruct(clus.shape, jnp.int32),
         ),
         in_specs=[smem(), smem()] + [pl.BlockSpec(memory_space=pltpu.HBM)] * 7,
-        out_specs=(vmem(), vmem(), vmem(), vmem()),
+        out_specs=(vmem(),) * 6,
         scratch_shapes=[
             pltpu.VMEM((16, npts), f32),
             pltpu.VMEM((2 * PACK, 2 * npts), f32),
@@ -631,29 +673,25 @@
             pltpu.VMEM((4, BAND, LANES), f32),
             pltpu.VMEM((3, BAND, LANES), f32),
             pltpu.VMEM((UNK, 32, LANES), f32),
-            pltpu.VMEM((UNK, 32, LANES), f32),
-            pltpu.VMEM((UNK, 32, LANES), f32),
             pltpu.VMEM((UNK, 16, LANES), f32),
             pltpu.VMEM((32, LANES), f32),
-            pltpu.VMEM((PARAMS, 16, LANES), f32),
-            pltpu.VMEM((PARAMS, 32, LANES), f32),
-            pltpu.VMEM((PARAMS, 32, LANES), f32),
+            pltpu.VMEM((2 * UNK * 32, LANES), f32),
         ],
         compiler_params=params(12),
         name="solve",
     )(core, damping, mine, other)
 
 
-def run_update(owner_map, everything, jac, proj, fact, cam_ids, clus):
+def run_update(everything, jac, proj, fact, where, dest):
     return pl.pallas_call(
         update_kernel,
         out_shape=jax.ShapeDtypeStruct((3, 256), f32),
-        in_specs=[smem()] + [vmem()] * 6,
+        in_specs=[vmem()] * 6,
         out_specs=vmem(),
         scratch_shapes=[pltpu.VMEM((16, 256), f32)],
         compiler_params=params(8),
         name="update",
-    )(owner_map, everything, jac, proj, fact, cam_ids, clus)
+    )(everything, jac, proj, fact, where, dest)
 
 
 def sum_over_points(keep, give, ring):
@@ -669,7 +707,7 @@
 ):
     npts = cam_jac.shape[-1]
     core = (lax.axis_index("pt") % 2).astype(jnp.int32).reshape(1)
-    send, proj, fact, jac = run_points(
+    send, proj, fact, jac, where, dest = run_points(
         owner_map,
         damping,
         cam_jac.transpose(0, 1, 3, 2, 4).reshape(8 * PARAMS, 2, npts),
@@ -685,9 +723,7 @@
     mine, other = sum_over_points(keep, give, lax.axis_size("pt"))
     step, cast = run_solve(core, damping, mine, other)
     everything = lax.all_to_all(cast, "cl", split_axis=0, concat_axis=0, tiled=True)
-    point_step = run_update(
-        owner_map, everything.reshape(256, LANES), jac, proj, fact, cam_ids, clusters.T
-    )
+    point_step = run_update(everything.reshape(256, LANES), jac, proj, fact, where, dest)
     return (step[None], point_step)
 
 

time: 67.8 us -> 63.9 us (0.942)
  Pallas kernels: 22.8 us -> 18.8 us
    pallas_call x1, Pallas kernels: 13.9 us -> 10.9 us  [run_solve(): pl.pallas_call(solve_kernel, out_shape=(jax.ShapeDtypeStruct((PARAMS, LAN...]
where the time goes in v3:
time: 63.9 us; the launch traced here: 63.5 us
  waiting for transfers between devices  26 us (41%)
  Pallas kernels  18.8 us (29%)
  starting transfers between devices  16 us (25%)
  between operations  1.37 us (2%)
  local copies, waits for them, and re-layouts  1.27 us (2%)
    pallas_call x1, Pallas kernels, run_solve(): pl.pallas_call(solve_kernel, out_shape=(jax.ShapeDtypeStruct((PARAMS, LAN...  10.9 us
    all_to_all x1, waiting for transfers between devices, per_device(): recv = lax.all_to_all(send, 'cl', split_axis=0, concat_axis=0, tiled=True)  10.8 us
    all_to_all x1, starting transfers between devices, per_device(): recv = lax.all_to_all(send, 'cl', split_axis=0, concat_axis=0, tiled=True)  7.97 us
    all_to_all x1, waiting for transfers between devices, per_device(): lax.all_to_all(cast, 'cl', split_axis=0, concat_axis=0, tiled=True)  7.34 us
    ppermute x3, waiting for transfers between devices, sum_over_points(): lax.ppermute(half, 'pt', [(i, i ^ 2 * d) for i in range(ring)])  5.39 us
    ppermute x3, starting transfers between devices, sum_over_points(): lax.ppermute(half, 'pt', [(i, i ^ 2 * d) for i in range(ring)])  4.17 us
    pallas_call x1, Pallas kernels, run_points(): pl.pallas_call(points_kernel, out_shape=(jax.ShapeDtypeStruct((16, PACK,...  3.91 us
    all_to_all x1, starting transfers between devices, per_device(): lax.all_to_all(cast, 'cl', split_axis=0, concat_axis=0, tiled=True)  3.64 us
  transfers between devices with their start and end apart: 7, of which 6 were waited for; matrix products, arithmetic and copies ran while one was open for 1% of the time, Pallas kernels for 0%

profile of v3, /device:TPU:0, one launch (start us, length us, event | category | flops | bytes accessed | tf_op | source)
XLA Modules:
  0.0 63.5 jit_solution(4679915360332385487)
XLA Ops:
  1.3 3.9 %points.1 = (f32[16,56,128]{2,1,0:T(8,128)}, f32[3,16,256]{2,1,0:T(8,128)}, f32[9,256]{1,0:T(8,128)}, f32[2,72,256]{2,1,0:T(8,128)}, s32[2,4,256]{2,1,0:T(4,128)}, /*index=5*/s32[2,256]{1,0:T(2,128)}) custom-call(s32[16]{0:T(128)} %owner_ref.1, f32[1]{0:T(128)S(6)} %copy.12.damp_ref, f32[72,2,256]{2,1,0:T(2,128)} %bitcast.18, f32[24,2,256]{2,1,0:T(2,128)} %bitcast.20, ...), custom_call_target="tpu_custom_call" | custom-call | tf_op jit(solution)/shard_map/points/pallas_call | solution.py:615
  5.2 8.0 %all-to-all-start = ((f32[16,56,128]{2,1,0:T(8,128)}), f32[16,56,128]{2,1,0:T(8,128)S(1)}, u32[]{:S(2)}, u32[]{:S(2)}) async-start(f32[16,56,128]{2,1,0:T(8,128)} %get-tuple-element.12), calls=%async_computation | async-start | bytes 917504 | tf_op jit(solution)/shard_map/all_to_all | solution.py:721
  13.2 10.8 %all-to-all-done = f32[16,56,128]{2,1,0:T(8,128)S(1)} async-done(((f32[16,56,128]{2,1,0:T(8,128)}), f32[16,56,128]{2,1,0:T(8,128)S(1)}, u32[]{:S(2)}, u32[]{:S(2)}) %all-to-all-start) | async-done | bytes 458784 | tf_op jit(solution)/shard_map/all_to_all | solution.py:721
  24.0 3.0 %band.1 = (f32[152,128]{1,0:T(8,128)S(1)}, f32[152,128]{1,0:T(8,128)S(1)}) custom-call(s32[1]{0:T(128)} %bitcast.core_ref, f32[896,128]{1,0:T(8,128)S(1)} %bitcast.15), custom_call_target="tpu_custom_call" | custom-call | tf_op jit(solution)/shard_map/band/pallas_call | solution.py:645
  26.9 0.1 collective-permute-start
  27.0 1.3 %collective-permute-done = f32[152,128]{1,0:T(8,128)S(1)} collective-permute-done((f32[152,128]{1,0:T(8,128)S(1)}, f32[152,128]{1,0:T(8,128)S(1)}, u32[]{:S(2)}, u32[]{:S(2)}) %collective-permute-start) | collective-permute-done | bytes 77856 | tf_op jit(solution)/shard_map/ppermute | solution.py:699
  28.3 3.1 %collective-permute-start.3 = (f32[152,128]{1,0:T(8,128)S(1)}, f32[152,128]{1,0:T(8,128)S(1)}, u32[]{:S(2)}, u32[]{:S(2)}) collective-permute-start(f32[152,128]{1,0:T(8,128)S(1)} %add.17), channel_id=1, source_target_pairs={{0,96},{16,112},{32,64},{48,80},{64,32},{80,48},{96,0},{112,16},{1... | collective-permute-start | bytes 233480 | tf_op jit(solution)/shard_map/ppermute | solution.py:700
  31.4 0.6 %collective-permute-start.2 = (f32[152,128]{1,0:T(8,128)S(1)}, f32[152,128]{1,0:T(8,128)S(1)}, u32[]{:S(2)}, u32[]{:S(2)}) collective-permute-start(f32[152,128]{1,0:T(8,128)S(1)} %add.17), channel_id=1, source_target_pairs={{0,64},{16,80},{32,96},{48,112},{64,0},{80,16},{96,32},{112,48},{1... | collective-permute-start | bytes 233480 | tf_op jit(solution)/shard_map/ppermute | solution.py:700
  32.0 0.4 collective-permute-start.1
  32.5 2.5 %collective-permute-done.3 = f32[152,128]{1,0:T(8,128)S(1)} collective-permute-done((f32[152,128]{1,0:T(8,128)S(1)}, f32[152,128]{1,0:T(8,128)S(1)}, u32[]{:S(2)}, u32[]{:S(2)}) %collective-permute-start.3) | collective-permute-done | bytes 77856 | tf_op jit(solution)/shard_map/ppermute | solution.py:700
  35.0 2.8 %collective-permute-done.2 = f32[152,128]{1,0:T(8,128)S(1)} collective-permute-done((f32[152,128]{1,0:T(8,128)S(1)}, f32[152,128]{1,0:T(8,128)S(1)}, u32[]{:S(2)}, u32[]{:S(2)}) %collective-permute-start.2) | collective-permute-done | bytes 77856 | tf_op jit(solution)/shard_map/ppermute | solution.py:700
  37.9 0.0 collective-permute-done.1
  37.9 0.1 collective-permute-start.4
  38.0 1.3 %collective-permute-done.4.other_ref = f32[152,128]{1,0:T(8,128)S(1)} collective-permute-done((f32[152,128]{1,0:T(8,128)S(1)}, f32[152,128]{1,0:T(8,128)S(1)}, u32[]{:S(2)}, u32[]{:S(2)}) %collective-permute-start.4) | collective-permute-done | bytes 77856 | tf_op jit(solution)/shard_map/ppermute | solution.py:702
  39.3 10.9 %solve.1 = (f32[9,128]{1,0:T(8,128)S(1)}, f32[16,16,128]{2,1,0:T(8,128)}) custom-call(s32[1]{0:T(128)} %bitcast.core_ref, f32[1]{0:T(128)S(6)} %copy.12.damp_ref, f32[152,128]{1,0:T(8,128)S(1)} %add_add_fusion.mine_ref, f32[152,128]{1,0:T(8,128)S(1)} %collective-permute-done.4.other_ref), custom_call_target="tpu_custom_call" | custom-call | tf_op jit(solution)/shard_map/solve/pallas_call | solution.py:664
  50.1 0.0 copy-start
  50.2 0.0 copy-start.1
  50.2 3.6 %all-to-all-start.1 = ((f32[16,16,128]{2,1,0:T(8,128)}), f32[16,16,128]{2,1,0:T(8,128)S(1)}, u32[]{:S(2)}, u32[]{:S(2)}) async-start(f32[16,16,128]{2,1,0:T(8,128)} %get-tuple-element.16), calls=%async_computation.1 | async-start | bytes 262144 | tf_op jit(solution)/shard_map/all_to_all | solution.py:725
  53.8 0.0 copy-start.2
  53.8 0.6 copy.11
  54.4 0.0 copy-start.3
  54.4 7.3 %all-to-all-done.1 = f32[16,16,128]{2,1,0:T(8,128)S(1)} async-done(((f32[16,16,128]{2,1,0:T(8,128)}), f32[16,16,128]{2,1,0:T(8,128)S(1)}, u32[]{:S(2)}, u32[]{:S(2)}) %all-to-all-start.1) | async-done | bytes 131104 | tf_op jit(solution)/shard_map/all_to_all | solution.py:725
  61.8 0.0 copy-start.4
  61.8 0.0 copy-done
  61.8 0.0 copy-done.1
  61.8 0.0 copy-done.2
  61.8 0.0 copy-done.3
  61.8 0.7 %copy-done.4 = s32[2,256]{1,0:T(2,128)S(1)} copy-done((s32[2,256]{1,0:T(2,128)S(1)}, s32[2,256]{1,0:T(2,128)}, u32[]{:S(2)}) %copy-start.4) | copy-done | bytes 2072
  62.4 1.1 %update.1 = f32[3,256]{1,0:T(4,128)} custom-call(f32[256,128]{1,0:T(8,128)S(1)} %bitcast.16, f32[2,72,256]{2,1,0:T(8,128)S(1)} %copy-done, f32[3,16,256]{2,1,0:T(8,128)S(1)} %copy-done.1, f32[9,256]{1,0:T(8,128)S(1)} %copy-done.2, s32[2,4,256]{2,1,0:T(4,128)S(1)} %copy-done.3, s32[2,256]{1,0:T(2,128)S(1)} %copy-done.4), custom_call_target="tpu_custom_call" | custom-call | tf_op jit(solution)/shard_map/update/pallas_call | solution.py:686
  (2 shorter events, 0.0 us)
Async XLA Ops:
  5.2 18.8 %all-to-all-start = ((f32[16,56,128]{2,1,0:T(8,128)}), f32[16,56,128]{2,1,0:T(8,128)S(1)}, u32[]{:S(2)}, u32[]{:S(2)}) async-start(f32[16,56,128]{2,1,0:T(8,128)} %get-tuple-element.12), calls=%async_computation | async-start | bytes 917504 | tf_op jit(solution)/shard_map/all_to_all | solution.py:721
  26.9 1.4 %collective-permute-start = (f32[152,128]{1,0:T(8,128)S(1)}, f32[152,128]{1,0:T(8,128)S(1)}, u32[]{:S(2)}, u32[]{:S(2)}) collective-permute-start(f32[152,128]{1,0:T(8,128)S(1)} %get-tuple-element.14), channel_id=1, source_target_pairs={{0,16},{16,0},{32,48},{48,32},{64,80},{80,64},{96,112},{112,96},{1... | collective-permute-start | bytes 233480 | tf_op jit(solution)/shard_map/ppermute | solution.py:699
  28.3 6.7 %collective-permute-start.3 = (f32[152,128]{1,0:T(8,128)S(1)}, f32[152,128]{1,0:T(8,128)S(1)}, u32[]{:S(2)}, u32[]{:S(2)}) collective-permute-start(f32[152,128]{1,0:T(8,128)S(1)} %add.17), channel_id=1, source_target_pairs={{0,96},{16,112},{32,64},{48,80},{64,32},{80,48},{96,0},{112,16},{1... | collective-permute-start | bytes 233480 | tf_op jit(solution)/shard_map/ppermute | solution.py:700
  31.4 6.5 %collective-permute-start.2 = (f32[152,128]{1,0:T(8,128)S(1)}, f32[152,128]{1,0:T(8,128)S(1)}, u32[]{:S(2)}, u32[]{:S(2)}) collective-permute-start(f32[152,128]{1,0:T(8,128)S(1)} %add.17), channel_id=1, source_target_pairs={{0,64},{16,80},{32,96},{48,112},{64,0},{80,16},{96,32},{112,48},{1... | collective-permute-start | bytes 233480 | tf_op jit(solution)/shard_map/ppermute | solution.py:700
  32.0 5.8 %collective-permute-start.1 = (f32[152,128]{1,0:T(8,128)S(1)}, f32[152,128]{1,0:T(8,128)S(1)}, u32[]{:S(2)}, u32[]{:S(2)}) collective-permute-start(f32[152,128]{1,0:T(8,128)S(1)} %add.17), channel_id=1, source_target_pairs={{0,32},{16,48},{32,0},{48,16},{64,96},{80,112},{96,64},{112,80},{1... | collective-permute-start | bytes 233480 | tf_op jit(solution)/shard_map/ppermute | solution.py:700
  37.9 1.4 %collective-permute-start.4 = (f32[152,128]{1,0:T(8,128)S(1)}, f32[152,128]{1,0:T(8,128)S(1)}, u32[]{:S(2)}, u32[]{:S(2)}) collective-permute-start(f32[152,128]{1,0:T(8,128)S(1)} %add_add_fusion.mine_ref), channel_id=1, source_target_pairs={{0,16},{16,0},{32,48},{48,32},{64,80},{80,64},{96,112},{112,96},{1... | collective-permute-start | bytes 233480 | tf_op jit(solution)/shard_map/ppermute | solution.py:702
  50.1 11.6 %copy-start = (f32[2,72,256]{2,1,0:T(8,128)S(1)}, f32[2,72,256]{2,1,0:T(8,128)}, u32[]{:S(2)}) copy-start(f32[2,72,256]{2,1,0:T(8,128)} %get-tuple-element.17.jac_ref) | copy-start | bytes 442372
  50.2 11.6 %copy-start.1 = (f32[3,16,256]{2,1,0:T(8,128)S(1)}, f32[3,16,256]{2,1,0:T(8,128)}, u32[]{:S(2)}) copy-start(f32[3,16,256]{2,1,0:T(8,128)} %get-tuple-element.18.proj_ref) | copy-start | bytes 147460
  50.2 11.6 %all-to-all-start.1 = ((f32[16,16,128]{2,1,0:T(8,128)}), f32[16,16,128]{2,1,0:T(8,128)S(1)}, u32[]{:S(2)}, u32[]{:S(2)}) async-start(f32[16,16,128]{2,1,0:T(8,128)} %get-tuple-element.16), calls=%async_computation.1 | async-start | bytes 262144 | tf_op jit(solution)/shard_map/all_to_all | solution.py:725
  53.8 8.0 %copy-start.2 = (f32[9,256]{1,0:T(8,128)S(1)}, f32[9,256]{1,0:T(8,128)}, u32[]{:S(2)}) copy-start(f32[9,256]{1,0:T(8,128)} %get-tuple-element.19.fact_ref) | copy-start | bytes 27652
  54.4 7.4 %copy-start.3 = (s32[2,4,256]{2,1,0:T(4,128)S(1)}, s32[2,4,256]{2,1,0:T(4,128)}, u32[]{:S(2)}) copy-start(s32[2,4,256]{2,1,0:T(4,128)} %get-tuple-element.20.cam_ref) | copy-start | bytes 24580
  61.8 0.7 %copy-start.4 = (s32[2,256]{1,0:T(2,128)S(1)}, s32[2,256]{1,0:T(2,128)}, u32[]{:S(2)}) copy-start(s32[2,256]{1,0:T(2,128)} %get-tuple-element.21.dest_ref) | copy-start | bytes 6148

commit v4 on v3

--- a/solution.py
+++ b/solution.py
@@ -12,6 +12,7 @@
 PARAMS = 9
 GROUPS = 32
 BLOCK = 9
+NODES = 16
 UNK = 27
 ROW_Q = 45
 ROW_D = (0, 54, 135, 216)
@@ -53,7 +54,8 @@
         for s in range(2):
             rows, picks = masks[s][half]
             for k in range(SLOTS):
-                index = jnp.broadcast_to(cam_ref[s, k : k + 1, cols], (8, LANES))
+                at = 4 * s + k
+                index = jnp.broadcast_to(cam_ref[at : at + 1, cols], (8, LANES))
                 chosen = lanes_from(table[0], index)
                 for c in range(1, 16):
                     chosen = jnp.where(picks[c], lanes_from(table[c], index), chosen)
@@ -90,11 +92,9 @@
     clus_hbm,
     prev_hbm,
     send_ref,
-    proj_ref,
-    fact_ref,
+    real_ref,
     jm_ref,
     where_ref,
-    dest_ref,
     dots,
     packed,
     jac_ref,
@@ -130,8 +130,9 @@
     dest = jnp.zeros_like(clus)
     for c in range(16):
         dest = jnp.where(clus == c, owner_ref[c], dest)
-    dest_ref[...] = dest
-    where_ref[...] = cam_ref[...]
+    where_ref[0:4, :] = cam_ref[0]
+    where_ref[4:8, :] = cam_ref[1]
+    where_ref[8:10, :] = dest
     slot_row = iota((8, npts), 0) % 4
     live = jnp.concatenate(
         [(slot_row < count_ref[s : s + 1, :]).astype(f32) for s in range(2)], axis=0
@@ -169,14 +170,14 @@
     h3 = (grad[2] - l31 * h1 - l32 * h2) * inv3
     h = [h1, h2, h3]
     for a in range(3):
-        proj_ref[a] = proj[a]
+        real_ref[16 * a : 16 * a + 16, :] = proj[a]
     for n, row in enumerate([inv1, inv2, inv3, l21, l31, l32, h1, h2, h3]):
-        fact_ref[n : n + 1, :] = row
+        real_ref[48 + n : 49 + n, :] = row
 
     masks = cluster_masks(clus)
     table = [prev_ref[pl.ds(c, 8, stride=16), :] for c in range(16)]
     last = [prev_ref[128:136, :], prev_ref[136:144, :]]
-    lookup_dot(table, last, masks, cam_ref, jm_ref, dots)
+    lookup_dot(table, last, masks, where_ref, jm_ref, dots)
     dot_all = dots[...]
     wt = -res
     for a in range(3):
@@ -338,56 +339,91 @@
     return inverse
 
 
-def schur(size, side, lane, whole):
+def advance(size, work, diag, side, lane, whole):
     within = lane % GROUPS
-    results = []
+    part = lane // GROUPS
+    from_up = (within + 1) % GROUPS
+    pack_up = part * GROUPS + from_up
+    is_left = part < 2
+    is_rhs = jnp.logical_and(part == 1, iota((8, LANES), 0) == 3)
     for which in range(2):
-        for r in range(size):
-            for v in range(4):
+        for v in range(4):
+            for r in range(size):
                 at = 32 * (which * UNK + r) + 8 * v
                 whole[at : at + 8, :] = lanes_from(
-                    side[r][v % 2], within + GROUPS * (2 * which + v // 2)
+                    work[r][v % 2], within + GROUPS * (2 * which + v // 2)
                 )
-        per_a = [[None, None] for a in range(UNK)]
-        for first in range(0, UNK, BLOCK):
+    for first in range(0, UNK, BLOCK):
+        block = range(first, min(first + BLOCK, UNK))
+        sums = []
+        for which in range(2):
+            acc = {}
             for r in range(size):
-                for a in range(first, min(first + BLOCK, UNK)):
+                for a in block:
                     at = 32 * (which * UNK + r) + a
                     coef = jnp.broadcast_to(whole[at : at + 1, :], (8, LANES))
                     for e in range(2):
-                        term = coef * side[r][e]
-                        per_a[a][e] = term if r == 0 else per_a[a][e] + term
-        results.append(per_a)
-    return results
-
-
-def apply_schur(left, right, diag, side, lane, down, up, keep):
-    within = lane % GROUPS
-    part = lane // GROUPS
-    from_down = (within - down + GROUPS) % GROUPS
-    from_up = (within + up) % GROUPS
-    pack_down = part * GROUPS + from_down
-    pack_up = part * GROUPS + from_up
-    is_left = part < 2
-    is_rhs = jnp.logical_and(part == 1, iota((8, LANES), 0) == 3)
-    for a in range(UNK):
-        fresh = []
-        for e in range(2):
-            by_down = lanes_from(right[a][e], pack_down)
-            by_up = lanes_from(left[a][e], pack_up)
-            new = -jnp.where(is_left, by_down, by_up)
-            if keep:
-                new = new + side[a][e]
+                        term = coef * work[r][e]
+                        acc[a, e] = term if r == 0 else acc[a, e] + term
+            sums.append(acc)
+        left, right = sums
+        for a in block:
+            for e in range(2):
+                by_up = lanes_from(left[a, e], pack_up)
+                new = side[a][e] - jnp.where(is_left, right[a, e], by_up)
                 if e == 1:
                     new = new - jnp.where(is_rhs, by_up, 0.0)
-            elif e == 1:
-                new = new + jnp.where(is_rhs, side[a][e] - by_up, 0.0)
-            fresh.append(new)
-        for v in range(a // 8, 4):
-            own = lanes_from(right[a][v % 2], from_down + GROUPS * (2 + v // 2))
-            other = lanes_from(left[a][v % 2], from_up + GROUPS * (v // 2))
-            diag[a][v] = diag[a][v] - own - other
-        side[a] = fresh
+                side[a][e] = new
+        for v in range(first // 8, 4):
+            for a in block:
+                if v >= a // 8:
+                    own = lanes_from(right[a, v % 2], within + GROUPS * (2 + v // 2))
+                    diag[a][v] = diag[a][v] - own
+            for a in block:
+                if v >= a // 8:
+                    other = lanes_from(left[a, v % 2], from_up + GROUPS * (v // 2))
+                    diag[a][v] = diag[a][v] - other
+
+
+def advance_wide(work, diag, side, lane, whole, down, up):
+    within = lane % NODES
+    part = lane // NODES
+    from_down = (within - down + NODES) % NODES
+    from_up = (within + up) % NODES
+    pack_down = part * NODES + from_down
+    pack_up = part * NODES + from_up
+    is_left = part < 4
+    is_rhs = jnp.logical_and(part == 3, iota((8, LANES), 0) == 3)
+    for v in range(8):
+        for r in range(UNK):
+            at = 64 * r + 8 * v
+            whole[at : at + 8, :] = lanes_from(work[r][0], within + NODES * v)
+    for first in range(0, UNK, BLOCK):
+        block = range(first, min(first + BLOCK, UNK))
+        sums = []
+        for which in range(2):
+            acc = {}
+            for r in range(UNK):
+                for a in block:
+                    at = 64 * r + 32 * which + a
+                    term = jnp.broadcast_to(whole[at : at + 1, :], (8, LANES)) * work[r][0]
+                    acc[a] = term if r == 0 else acc[a] + term
+            sums.append(acc)
+        left, right = sums
+        for a in block:
+            by_down = lanes_from(right[a], pack_down)
+            by_up = lanes_from(left[a], pack_up)
+            new = -jnp.where(is_left, by_down, by_up)
+            side[a] = [new + jnp.where(is_rhs, side[a][0] - by_up, 0.0)]
+        for v in range(first // 8, 4):
+            for a in block:
+                if v >= a // 8:
+                    own = lanes_from(right[a], from_down + NODES * (4 + v))
+                    diag[a][v] = diag[a][v] - own
+            for a in block:
+                if v >= a // 8:
+                    other = lanes_from(left[a], from_up + NODES * v)
+                    diag[a][v] = diag[a][v] - other
 
 
 def solve_kernel(
@@ -406,17 +442,19 @@
         on_diag = jnp.logical_or(on_diag, row == i * 9 - i * (i - 1) // 2)
     low = low + jnp.where(on_diag, damp_ref[0], 0.0)
     first_rows = HALF // 8
-    for n in range(BAND // 8):
-        chunk = low[8 * n : 8 * n + 8] if n < first_rows else high[8 * n - HALF : 8 * n - HALF + 8]
-        at = slice(8 * n, 8 * n + 8)
-        kinds = {d for d in range(4) if ROW_D[d] < 8 * n + 8 and 8 * n < ROW_END[d]}
-        for r in range(4):
-            if kinds & NEEDED[r]:
-                rep[r, at, :] = lanes_from(chunk, within + GROUPS * r)
-            if r > 0 and kinds & set(range(4 - r, 4)):
-                back[r - 1, at, :] = lanes_from(
-                    chunk, (within + GROUPS - 1) % GROUPS + GROUPS * r
-                )
+    for r in range(4):
+        for shift, wanted in ((0, NEEDED[r]), (1, set(range(4 - r, 4)))):
+            index = (within + GROUPS - shift) % GROUPS + GROUPS * r
+            for n in range(BAND // 8):
+                kinds = {d for d in range(4) if ROW_D[d] < 8 * n + 8 and 8 * n < ROW_END[d]}
+                if not kinds & wanted:
+                    continue
+                at = slice(8 * n, 8 * n + 8)
+                chunk = low[at] if n < first_rows else high[8 * n - HALF : 8 * n - HALF + 8]
+                if shift:
+                    back[r - 1, at, :] = lanes_from(chunk, index)
+                else:
+                    rep[r, at, :] = lanes_from(chunk, index)
 
     def tri(i):
         return i * 9 - i * (i - 1) // 2
@@ -467,7 +505,6 @@
         um.append(tail([(n, p[1]) for n, p in enumerate(after)]))
         side0.append(pack(lm, um))
     inv0 = factor(PARAMS, diag0, side0, (0, 1))
-    left, right = schur(PARAMS, side0, lane, whole)
 
     diag, side = [], []
     for a in range(UNK):
@@ -484,72 +521,120 @@
         lm = [behind[q][0] if q in behind else zero for q in (1, 2, 3)]
         lm.append(tail([(q - 1, p[1]) for q, p in behind.items()] + [(3, rhs(r, i))]))
         side.append(pack(lm, um))
-    apply_schur(left, right, diag, side, lane, 0, 1, True)
+    advance(PARAMS, side0, diag, side, lane, whole)
+
+    few = lane % NODES
+    which = lane // NODES
+    odd_diag = [[None] * 4 for a in range(UNK)]
+    even_diag = [[None] * 4 for a in range(UNK)]
+    for n, target in enumerate((even_diag, odd_diag)):
+        for a in range(UNK):
+            for v in range(a // 8, 4):
+                target[a][v] = lanes_from(diag[a][v], 2 * few + n)
+    base = 2 * few + GROUPS * (2 * (which // 4) + (which % 4) // 2)
+    split = []
+    for n in range(2):
+        first = [lanes_from(side[a][0], base + n) for a in range(UNK)]
+        second = [lanes_from(side[a][1], base + n) for a in range(UNK)]
+        split.append([[jnp.where(which % 2 == 0, p, q)] for p, q in zip(first, second)])
+    diag, (side, odd_side) = even_diag, split
+    odd_inverse = factor(UNK, odd_diag, odd_side, (0,))
+    advance_wide(odd_side, diag, side, lane, whole, 1, 0)
 
     def store(diag, side):
         for a in range(UNK):
             for v in range(a // 8, 4):
                 dmat[a, 8 * v : 8 * v + 8, :] = diag[a][v]
-            for e in range(2):
-                smat[a, 8 * e : 8 * e + 8, :] = side[a][e]
+            smat[a] = side[a][0]
 
     def load():
         diag = [
             [dmat[a, 8 * v : 8 * v + 8, :] if v >= a // 8 else None for v in range(4)]
             for a in range(UNK)
         ]
-        return diag, [chunked(smat[a], 2) for a in range(UNK)]
+        return diag, [[smat[a]] for a in range(UNK)]
 
     store(diag, side)
 
     def level(step, carry):
         stride = lax.shift_left(jnp.int32(1), step)
         diag, side = load()
-        factor(UNK, diag, side, (0, 1))
-        left, right = schur(UNK, side, lane, whole)
+        factor(UNK, diag, side, (0,))
+        work = side
         diag, side = load()
-        apply_schur(left, right, diag, side, lane, stride, stride, False)
+        advance_wide(work, diag, side, lane, whole, stride, stride)
         store(diag, side)
         return carry
 
-    lax.fori_loop(0, 4, level, jnp.int32(0))
+    lax.fori_loop(0, 3, level, jnp.int32(0))
 
     diag, side = load()
-    both = []
+    from_left = [lanes_from(side[a][0], few + NODES * (which % 4)) for a in range(UNK)]
+    from_right = [lanes_from(side[a][0], few + NODES * (4 + which % 4)) for a in range(UNK)]
+    both = [[p + q] for p, q in zip(from_left, from_right)]
     for a in range(UNK):
-        halves = []
-        for base in (0, 2 * GROUPS):
-            index = within + GROUPS * (part // 2) + base
-            halves.append(
-                jnp.where(
-                    part % 2 == 0, lanes_from(side[a][0], index), lanes_from(side[a][1], index)
-                )
-            )
-        both.append([halves[0] + halves[1]])
-        right_side = lanes_from(side[a][1], within + GROUPS)
+        right_side = lanes_from(side[a][0], few + 3 * NODES)
         diag[a][3] = jnp.where(sub == 3, right_side, diag[a][3])
     work = [list(line_of) for line_of in diag]
     factor(UNK, work, both, (0,))
-    full = [[lanes_from(both[r][0], within + GROUPS * v) for v in range(4)] for r in range(UNK)]
+    for v in range(4):
+        for r in range(UNK):
+            at = 64 * r + 8 * v
+            whole[at : at + 8, :] = lanes_from(both[r][0], few + NODES * v)
+    for first in range(0, UNK, BLOCK):
+        block = range(first, min(first + BLOCK, UNK))
+        acc = {}
+        for r in range(UNK):
+            for a in block:
+                at = 64 * r + a
+                term = jnp.broadcast_to(whole[at : at + 1, :], (8, LANES)) * both[r][0]
+                acc[a] = term if r == 0 else acc[a] + term
+        for v in range(first // 8, 4):
+            for a in block:
+                if v >= a // 8:
+                    moved = lanes_from(acc[a], (few + NODES // 2) % NODES + NODES * v)
+                    diag[a][v] = diag[a][v] - moved
+    inverse = factor(UNK, diag, both, ())
+
+    def back_solve(size, diag, inverse, todo):
+        value = [None] * size
+        for k in range(size - 1, -1, -1):
+            value[k] = todo[k] * inverse[k]
+            for r in range(k):
+                todo[r] = todo[r] - spread_row(diag[r][k // 8], k % 8) * value[k]
+        return value
+
+    def as_chunks(value):
+        for a in range(UNK):
+            xrow[a : a + 1, :] = value[a][0:1]
+        xrow[UNK:32, :] = jnp.zeros((5, LANES), f32)
+        return chunked(xrow[...], 4)
+
+    even_steps = as_chunks(
+        back_solve(UNK, diag, inverse, [spread_row(diag[a][3], 3) for a in range(UNK)])
+    )
+    packed = jnp.zeros((8, LANES), f32)
+    for v in range(4):
+        packed = jnp.where(which == v, even_steps[v], packed)
+        after = lanes_from(even_steps[v], (few + 1) % NODES)
+        packed = jnp.where(which == 4 + v, after, packed)
+    right_sides = [lanes_from(odd_side[a][0], few + 3 * NODES) for a in range(UNK)]
+    todo = []
     for a in range(UNK):
-        acc = None
-        for r in range(UNK):
-            term = spread_row(full[r][a // 8], a % 8) * both[r][0]
-            acc = term if acc is None else acc + term
-        for v in range(a // 8, 4):
-            moved = lanes_from(acc, (within + 16) % GROUPS + GROUPS * v)
-            diag[a][v] = diag[a][v] - moved
-    inverse = factor(UNK, diag, both, ())
-    todo = [spread_row(diag[a][3], 3) for a in range(UNK)]
-    value = [None] * UNK
-    for k in range(UNK - 1, -1, -1):
-        value[k] = todo[k] * inverse[k]
-        for r in range(k):
-            todo[r] = todo[r] - spread_row(diag[r][k // 8], k % 8) * value[k]
-    for a in range(UNK):
-        xrow[a : a + 1, :] = value[a][0:1]
-    xrow[UNK:32, :] = jnp.zeros((5, LANES), f32)
-    own = chunked(xrow[...], 4)
+        terms = odd_side[a][0] * packed
+        for shift in (64, 32, 16):
+            terms = terms + pltpu.roll(terms, shift, 1)
+        summed = jnp.broadcast_to(jnp.sum(terms, axis=0, keepdims=True), (8, LANES))
+        todo.append(spread_row(right_sides[a], 3) - summed)
+    odd_steps = as_chunks(back_solve(UNK, odd_diag, odd_inverse, todo))
+    own = [
+        jnp.where(
+            lane % 2 == 0,
+            lanes_from(even_steps[v], within // 2),
+            lanes_from(odd_steps[v], within // 2),
+        )
+        for v in range(4)
+    ]
     prev = [lanes_from(c, (lane + LANES - 1) % LANES) for c in own]
     packed = pack(prev, own)
     todo0 = []
@@ -560,14 +645,10 @@
         right_side = spread_row(lanes_from(side0[i][1], within + GROUPS), 3)
         summed = jnp.broadcast_to(jnp.sum(terms, axis=0, keepdims=True), (8, LANES))
         todo0.append(right_side - summed)
-    value0 = [None] * PARAMS
-    for k in range(PARAMS - 1, -1, -1):
-        value0[k] = todo0[k] * inv0[k]
-        for r in range(k):
-            todo0[r] = todo0[r] - spread_row(diag0[r][k // 8], k % 8) * value0[k]
+    value0 = back_solve(PARAMS, diag0, inv0, todo0)
     camera = (lane % 4) * GROUPS + lane // 4
     for i in range(PARAMS):
-        near = [value[8 * r + i] if i < 8 else value[24 + r] for r in range(3)]
+        near = [spread_row(own[r], i) if i < 8 else spread_row(own[3], r) for r in range(3)]
         mixed = jnp.where(
             part == 0,
             value0[i],
@@ -579,17 +660,20 @@
         cast_ref[dest, PARAMS:16, :] = jnp.zeros((16 - PARAMS, LANES), f32)
 
 
-def update_kernel(all_ref, jac_ref, proj_ref, fact_ref, cam_ref, dest_ref, out_ref, dots):
-    masks = cluster_masks(dest_ref[...])
+def update_kernel(all_ref, jac_ref, real_ref, where_ref, out_ref, dots):
+    masks = cluster_masks(where_ref[8:10, :])
     table = [all_ref[16 * c : 16 * c + 8, :] for c in range(16)]
     last = [all_ref[pl.ds(8, 8, stride=16), :], all_ref[pl.ds(136, 8, stride=16), :]]
-    lookup_dot(table, last, masks, cam_ref, jac_ref, dots)
+    lookup_dot(table, last, masks, where_ref, jac_ref, dots)
     dot_all = dots[...]
 
     def fact(n):
-        return fact_ref[n : n + 1, :]
-
-    tot = [fact(6 + a) + jnp.sum(proj_ref[a] * dot_all, axis=0, keepdims=True) for a in range(3)]
+        return real_ref[48 + n : 49 + n, :]
+
+    tot = []
+    for a in range(3):
+        terms = real_ref[16 * a : 16 * a + 16, :] * dot_all
+        tot.append(fact(6 + a) + jnp.sum(terms, axis=0, keepdims=True))
     x3 = tot[2] * fact(2)
     x2 = (tot[1] - fact(5) * x3) * fact(1)
     x1 = (tot[0] - fact(3) * x2 - fact(4) * x3) * fact(0)
@@ -616,14 +700,12 @@
         points_kernel,
         out_shape=(
             jax.ShapeDtypeStruct((16, PACK, LANES), f32),
-            jax.ShapeDtypeStruct((3, 16, npts), f32),
-            jax.ShapeDtypeStruct((9, npts), f32),
+            jax.ShapeDtypeStruct((57, npts), f32),
             jax.ShapeDtypeStruct((2, 8 * PARAMS, npts), f32),
-            jax.ShapeDtypeStruct(cam_ids.shape, jnp.int32),
-            jax.ShapeDtypeStruct(clus.shape, jnp.int32),
+            jax.ShapeDtypeStruct((10, npts), jnp.int32),
         ),
         in_specs=[smem(), smem()] + [pl.BlockSpec(memory_space=pltpu.HBM)] * 7,
-        out_specs=(vmem(),) * 6,
+        out_specs=(vmem(),) * 4,
         scratch_shapes=[
             pltpu.VMEM((16, npts), f32),
             pltpu.VMEM((2 * PACK, 2 * npts), f32),
@@ -673,7 +755,7 @@
             pltpu.VMEM((4, BAND, LANES), f32),
             pltpu.VMEM((3, BAND, LANES), f32),
             pltpu.VMEM((UNK, 32, LANES), f32),
-            pltpu.VMEM((UNK, 16, LANES), f32),
+            pltpu.VMEM((UNK, 8, LANES), f32),
             pltpu.VMEM((32, LANES), f32),
             pltpu.VMEM((2 * UNK * 32, LANES), f32),
         ],
@@ -682,16 +764,16 @@
     )(core, damping, mine, other)
 
 
-def run_update(everything, jac, proj, fact, where, dest):
+def run_update(everything, jac, real, where):
     return pl.pallas_call(
         update_kernel,
         out_shape=jax.ShapeDtypeStruct((3, 256), f32),
-        in_specs=[vmem()] * 6,
+        in_specs=[vmem()] * 4,
         out_specs=vmem(),
         scratch_shapes=[pltpu.VMEM((16, 256), f32)],
         compiler_params=params(8),
         name="update",
-    )(everything, jac, proj, fact, where, dest)
+    )(everything, jac, real, where)
 
 
 def sum_over_points(keep, give, ring):
@@ -707,7 +789,7 @@
 ):
     npts = cam_jac.shape[-1]
     core = (lax.axis_index("pt") % 2).astype(jnp.int32).reshape(1)
-    send, proj, fact, jac, where, dest = run_points(
+    send, real, jac, where = run_points(
         owner_map,
         damping,
         cam_jac.transpose(0, 1, 3, 2, 4).reshape(8 * PARAMS, 2, npts),
@@ -723,7 +805,7 @@
     mine, other = sum_over_points(keep, give, lax.axis_size("pt"))
     step, cast = run_solve(core, damping, mine, other)
     everything = lax.all_to_all(cast, "cl", split_axis=0, concat_axis=0, tiled=True)
-    point_step = run_update(everything.reshape(256, LANES), jac, proj, fact, where, dest)
+    point_step = run_update(everything.reshape(256, LANES), jac, real, where)
     return (step[None], point_step)
 
 

time: 63.9 us -> 60.8 us (0.951)
  Pallas kernels: 18.8 us -> 16.5 us
  local copies, waits for them, and re-layouts: 1.27 us -> 0.61 us
    pallas_call x1, Pallas kernels: 10.9 us -> 8.55 us  [run_solve(): pl.pallas_call(solve_kernel, out_shape=(jax.ShapeDtypeStruct((PARAMS, LAN...]
    unnamed x11 -> x7, local copies, waits for them, and re-layouts: 1.27 us -> 0.61 us
where the time goes in v4:
time: 60.8 us; the launch traced here: 60.5 us
  waiting for transfers between devices  26 us (43%)
  Pallas kernels  16.5 us (27%)
  starting transfers between devices  16 us (26%)
  between operations  1.36 us (2%)
  local copies, waits for them, and re-layouts  0.61 us (1%)
    all_to_all x1, waiting for transfers between devices, per_device(): recv = lax.all_to_all(send, 'cl', split_axis=0, concat_axis=0, tiled=True)  10.8 us
    pallas_call x1, Pallas kernels, run_solve(): pl.pallas_call(solve_kernel, out_shape=(jax.ShapeDtypeStruct((PARAMS, LAN...  8.55 us
    all_to_all x1, starting transfers between devices, per_device(): recv = lax.all_to_all(send, 'cl', split_axis=0, concat_axis=0, tiled=True)  7.97 us
    all_to_all x1, waiting for transfers between devices, per_device(): lax.all_to_all(cast, 'cl', split_axis=0, concat_axis=0, tiled=True)  7.34 us
    ppermute x3, waiting for transfers between devices, sum_over_points(): lax.ppermute(half, 'pt', [(i, i ^ 2 * d) for i in range(ring)])  5.4 us
    ppermute x3, starting transfers between devices, sum_over_points(): lax.ppermute(half, 'pt', [(i, i ^ 2 * d) for i in range(ring)])  4.17 us
    pallas_call x1, Pallas kernels, run_points(): pl.pallas_call(points_kernel, out_shape=(jax.ShapeDtypeStruct((16, PACK,...  3.93 us
    all_to_all x1, starting transfers between devices, per_device(): lax.all_to_all(cast, 'cl', split_axis=0, concat_axis=0, tiled=True)  3.64 us
  transfers between devices with their start and end apart: 7, of which 6 were waited for; matrix products, arithmetic and copies ran while one was open for 1% of the time, Pallas kernels for 0%

profile of v4, /device:TPU:0, one launch (start us, length us, event | category | flops | bytes accessed | tf_op | source)
XLA Modules:
  0.0 60.5 jit_solution(17910721523751019214)
XLA Ops:
  1.3 3.9 %points.1 = (f32[16,56,128]{2,1,0:T(8,128)}, f32[57,256]{1,0:T(8,128)}, f32[2,72,256]{2,1,0:T(8,128)}, s32[10,256]{1,0:T(8,128)}) custom-call(s32[16]{0:T(128)} %owner_ref.1, f32[1]{0:T(128)S(6)} %copy.12.damp_ref, f32[72,2,256]{2,1,0:T(2,128)} %bitcast.18, f32[24,2,256]{2,1,0:T(2,128)} %bitcast.20, f32[8,2,256]{2,1,0:T(2,128)} %bitcast.21, ...), custom_call_target="tpu_custom_call" | custom-call | tf_op jit(solution)/shard_map/points/pallas_call | solution.py:699
  5.2 8.0 %all-to-all-start = ((f32[16,56,128]{2,1,0:T(8,128)}), f32[16,56,128]{2,1,0:T(8,128)S(1)}, u32[]{:S(2)}, u32[]{:S(2)}) async-start(f32[16,56,128]{2,1,0:T(8,128)} %get-tuple-element.10), calls=%async_computation | async-start | bytes 917504 | tf_op jit(solution)/shard_map/all_to_all | solution.py:803
  13.2 10.8 %all-to-all-done = f32[16,56,128]{2,1,0:T(8,128)S(1)} async-done(((f32[16,56,128]{2,1,0:T(8,128)}), f32[16,56,128]{2,1,0:T(8,128)S(1)}, u32[]{:S(2)}, u32[]{:S(2)}) %all-to-all-start) | async-done | bytes 458784 | tf_op jit(solution)/shard_map/all_to_all | solution.py:803
  24.0 3.0 %band.1 = (f32[152,128]{1,0:T(8,128)S(1)}, f32[152,128]{1,0:T(8,128)S(1)}) custom-call(s32[1]{0:T(128)} %bitcast.core_ref, f32[896,128]{1,0:T(8,128)S(1)} %bitcast.15), custom_call_target="tpu_custom_call" | custom-call | tf_op jit(solution)/shard_map/band/pallas_call | solution.py:727
  27.0 0.1 collective-permute-start
  27.1 1.3 %collective-permute-done = f32[152,128]{1,0:T(8,128)S(1)} collective-permute-done((f32[152,128]{1,0:T(8,128)S(1)}, f32[152,128]{1,0:T(8,128)S(1)}, u32[]{:S(2)}, u32[]{:S(2)}) %collective-permute-start) | collective-permute-done | bytes 77856 | tf_op jit(solution)/shard_map/ppermute | solution.py:781
  28.3 3.1 %collective-permute-start.3 = (f32[152,128]{1,0:T(8,128)S(1)}, f32[152,128]{1,0:T(8,128)S(1)}, u32[]{:S(2)}, u32[]{:S(2)}) collective-permute-start(f32[152,128]{1,0:T(8,128)S(1)} %add.17), channel_id=1, source_target_pairs={{0,96},{16,112},{32,64},{48,80},{64,32},{80,48},{96,0},{112,16},{1... | collective-permute-start | bytes 233480 | tf_op jit(solution)/shard_map/ppermute | solution.py:782
  31.4 0.6 %collective-permute-start.2 = (f32[152,128]{1,0:T(8,128)S(1)}, f32[152,128]{1,0:T(8,128)S(1)}, u32[]{:S(2)}, u32[]{:S(2)}) collective-permute-start(f32[152,128]{1,0:T(8,128)S(1)} %add.17), channel_id=1, source_target_pairs={{0,64},{16,80},{32,96},{48,112},{64,0},{80,16},{96,32},{112,48},{1... | collective-permute-start | bytes 233480 | tf_op jit(solution)/shard_map/ppermute | solution.py:782
  32.1 0.4 collective-permute-start.1
  32.5 2.6 %collective-permute-done.3 = f32[152,128]{1,0:T(8,128)S(1)} collective-permute-done((f32[152,128]{1,0:T(8,128)S(1)}, f32[152,128]{1,0:T(8,128)S(1)}, u32[]{:S(2)}, u32[]{:S(2)}) %collective-permute-start.3) | collective-permute-done | bytes 77856 | tf_op jit(solution)/shard_map/ppermute | solution.py:782
  35.1 2.8 %collective-permute-done.2 = f32[152,128]{1,0:T(8,128)S(1)} collective-permute-done((f32[152,128]{1,0:T(8,128)S(1)}, f32[152,128]{1,0:T(8,128)S(1)}, u32[]{:S(2)}, u32[]{:S(2)}) %collective-permute-start.2) | collective-permute-done | bytes 77856 | tf_op jit(solution)/shard_map/ppermute | solution.py:782
  37.9 0.0 collective-permute-done.1
  37.9 0.1 collective-permute-start.4
  38.0 1.3 %collective-permute-done.4.other_ref = f32[152,128]{1,0:T(8,128)S(1)} collective-permute-done((f32[152,128]{1,0:T(8,128)S(1)}, f32[152,128]{1,0:T(8,128)S(1)}, u32[]{:S(2)}, u32[]{:S(2)}) %collective-permute-start.4) | collective-permute-done | bytes 77856 | tf_op jit(solution)/shard_map/ppermute | solution.py:784
  39.3 8.6 %solve.1 = (f32[9,128]{1,0:T(8,128)S(1)}, f32[16,16,128]{2,1,0:T(8,128)}) custom-call(s32[1]{0:T(128)} %bitcast.core_ref, f32[1]{0:T(128)S(6)} %copy.12.damp_ref, f32[152,128]{1,0:T(8,128)S(1)} %add_add_fusion.mine_ref, f32[152,128]{1,0:T(8,128)S(1)} %collective-permute-done.4.other_ref), custom_call_target="tpu_custom_call" | custom-call | tf_op jit(solution)/shard_map/solve/pallas_call | solution.py:746
  47.8 0.0 copy-start
  47.8 0.0 copy-start.1
  47.8 3.6 %all-to-all-start.1 = ((f32[16,16,128]{2,1,0:T(8,128)}), f32[16,16,128]{2,1,0:T(8,128)S(1)}, u32[]{:S(2)}, u32[]{:S(2)}) async-start(f32[16,16,128]{2,1,0:T(8,128)} %get-tuple-element.14), calls=%async_computation.1 | async-start | bytes 262144 | tf_op jit(solution)/shard_map/all_to_all | solution.py:807
  51.5 0.0 copy-start.2
  51.5 0.6 copy.11
  52.1 7.3 %all-to-all-done.1 = f32[16,16,128]{2,1,0:T(8,128)S(1)} async-done(((f32[16,16,128]{2,1,0:T(8,128)}), f32[16,16,128]{2,1,0:T(8,128)S(1)}, u32[]{:S(2)}, u32[]{:S(2)}) %all-to-all-start.1) | async-done | bytes 131104 | tf_op jit(solution)/shard_map/all_to_all | solution.py:807
  59.4 0.0 copy-done
  59.4 0.0 copy-done.1
  59.4 0.0 copy-done.2
  59.5 1.1 %update.1 = f32[3,256]{1,0:T(4,128)} custom-call(f32[256,128]{1,0:T(8,128)S(1)} %bitcast.16, f32[2,72,256]{2,1,0:T(8,128)S(1)} %copy-done, f32[57,256]{1,0:T(8,128)S(1)} %copy-done.1, s32[10,256]{1,0:T(8,128)S(1)} %copy-done.2), custom_call_target="tpu_custom_call" | custom-call | tf_op jit(solution)/shard_map/update/pallas_call | solution.py:768
  (2 shorter events, 0.0 us)
Async XLA Ops:
  5.2 18.8 %all-to-all-start = ((f32[16,56,128]{2,1,0:T(8,128)}), f32[16,56,128]{2,1,0:T(8,128)S(1)}, u32[]{:S(2)}, u32[]{:S(2)}) async-start(f32[16,56,128]{2,1,0:T(8,128)} %get-tuple-element.10), calls=%async_computation | async-start | bytes 917504 | tf_op jit(solution)/shard_map/all_to_all | solution.py:803
  27.0 1.4 %collective-permute-start = (f32[152,128]{1,0:T(8,128)S(1)}, f32[152,128]{1,0:T(8,128)S(1)}, u32[]{:S(2)}, u32[]{:S(2)}) collective-permute-start(f32[152,128]{1,0:T(8,128)S(1)} %get-tuple-element.12), channel_id=1, source_target_pairs={{0,16},{16,0},{32,48},{48,32},{64,80},{80,64},{96,112},{112,96},{1... | collective-permute-start | bytes 233480 | tf_op jit(solution)/shard_map/ppermute | solution.py:781
  28.3 6.7 %collective-permute-start.3 = (f32[152,128]{1,0:T(8,128)S(1)}, f32[152,128]{1,0:T(8,128)S(1)}, u32[]{:S(2)}, u32[]{:S(2)}) collective-permute-start(f32[152,128]{1,0:T(8,128)S(1)} %add.17), channel_id=1, source_target_pairs={{0,96},{16,112},{32,64},{48,80},{64,32},{80,48},{96,0},{112,16},{1... | collective-permute-start | bytes 233480 | tf_op jit(solution)/shard_map/ppermute | solution.py:782
  31.4 6.5 %collective-permute-start.2 = (f32[152,128]{1,0:T(8,128)S(1)}, f32[152,128]{1,0:T(8,128)S(1)}, u32[]{:S(2)}, u32[]{:S(2)}) collective-permute-start(f32[152,128]{1,0:T(8,128)S(1)} %add.17), channel_id=1, source_target_pairs={{0,64},{16,80},{32,96},{48,112},{64,0},{80,16},{96,32},{112,48},{1... | collective-permute-start | bytes 233480 | tf_op jit(solution)/shard_map/ppermute | solution.py:782
  32.1 5.8 %collective-permute-start.1 = (f32[152,128]{1,0:T(8,128)S(1)}, f32[152,128]{1,0:T(8,128)S(1)}, u32[]{:S(2)}, u32[]{:S(2)}) collective-permute-start(f32[152,128]{1,0:T(8,128)S(1)} %add.17), channel_id=1, source_target_pairs={{0,32},{16,48},{32,0},{48,16},{64,96},{80,112},{96,64},{112,80},{1... | collective-permute-start | bytes 233480 | tf_op jit(solution)/shard_map/ppermute | solution.py:782
  37.9 1.4 %collective-permute-start.4 = (f32[152,128]{1,0:T(8,128)S(1)}, f32[152,128]{1,0:T(8,128)S(1)}, u32[]{:S(2)}, u32[]{:S(2)}) collective-permute-start(f32[152,128]{1,0:T(8,128)S(1)} %add_add_fusion.mine_ref), channel_id=1, source_target_pairs={{0,16},{16,0},{32,48},{48,32},{64,80},{80,64},{96,112},{112,96},{1... | collective-permute-start | bytes 233480 | tf_op jit(solution)/shard_map/ppermute | solution.py:784
  47.8 11.6 %copy-start = (f32[2,72,256]{2,1,0:T(8,128)S(1)}, f32[2,72,256]{2,1,0:T(8,128)}, u32[]{:S(2)}) copy-start(f32[2,72,256]{2,1,0:T(8,128)} %get-tuple-element.15.jac_ref) | copy-start | bytes 442372
  47.8 11.6 %copy-start.1 = (f32[57,256]{1,0:T(8,128)S(1)}, f32[57,256]{1,0:T(8,128)}, u32[]{:S(2)}) copy-start(f32[57,256]{1,0:T(8,128)} %get-tuple-element.16.real_ref) | copy-start | bytes 175108
  47.8 11.6 %all-to-all-start.1 = ((f32[16,16,128]{2,1,0:T(8,128)}), f32[16,16,128]{2,1,0:T(8,128)S(1)}, u32[]{:S(2)}, u32[]{:S(2)}) async-start(f32[16,16,128]{2,1,0:T(8,128)} %get-tuple-element.14), calls=%async_computation.1 | async-start | bytes 262144 | tf_op jit(solution)/shard_map/all_to_all | solution.py:807
  51.5 8.0 %copy-start.2 = (s32[10,256]{1,0:T(8,128)S(1)}, s32[10,256]{1,0:T(8,128)}, u32[]{:S(2)}) copy-start(s32[10,256]{1,0:T(8,128)} %get-tuple-element.17.where_ref) | copy-start | bytes 30724

commit v5 on v4

--- a/solution.py
+++ b/solution.py
@@ -20,6 +20,7 @@
 NEEDED = ({0, 1, 2, 3}, {0, 1, 2}, {0, 1, 3}, {0, 2, 3})
 BAND = 304
 HALF = BAND // 2
+DIAG = 45
 PACK = 56
 MIB = 1024 * 1024
 
@@ -228,7 +229,7 @@
             send_ref[4 * quad + 2 * pair + 1] = jnp.where(low_half, first_r, second)
 
 
-def band_kernel(core_ref, recv_ref, keep_ref, give_ref, rows, wide, hots):
+def band_kernel(half_ref, recv_ref, out_ref, rows, wide, hots):
     low_half = iota((8, LANES), 1) < 64
     quant = [[], []]
     for r in range(53):
@@ -250,72 +251,90 @@
 
     cam = quant[0][52].astype(jnp.int32)
     camera_of = 4 * (iota((LANES, LANES), 0) % GROUPS) + iota((LANES, LANES), 0) // GROUPS
-    for b in range(8):
-        cam_b = jnp.broadcast_to(cam[b : b + 1, :], (LANES, LANES))
-        for k in range(SLOTS):
-            hots[k, :, b * LANES : (b + 1) * LANES] = (
-                (camera_of == (cam_b + k) % LANES).astype(f32).astype(bf16)
-            )
-
-    sizes = [304, 224, 144, 64]
-    starts = [0, 304, 528, 672]
-    out = None
-    for k in range(SLOTS):
-        count = 0
-
-        def put(row, value, k=k):
-            at = 8 * (starts[k] + row)
-            rows[at : at + 8, :] = value
-
-        for dist in range(SLOTS - k):
-            other = k + dist
-            mix = [[None, None], [None, None]]
-            for m in range(2):
-                for n in range(2):
-                    if dist == 0 and n < m:
-                        mix[m][n] = mix[n][m]
-                        continue
-                    acc = proj(k, m, 0) * proj(other, n, 0)
-                    acc = acc + proj(k, m, 1) * proj(other, n, 1)
-                    acc = acc + proj(k, m, 2) * proj(other, n, 2)
-                    same = dist == 0 and m == n
-                    mix[m][n] = (1.0 - acc) if same else -acc
-            for j in range(PARAMS):
-                left = [
-                    mix[m][0] * jac(other, 0, j) + mix[m][1] * jac(other, 1, j) for m in range(2)
-                ]
-                for i in range(PARAMS):
-                    if dist == 0 and i > j:
-                        continue
-                    value = jac(k, 0, i) * left[0] + jac(k, 1, i) * left[1]
-                    if dist == 0:
-                        row = i * 9 - i * (i - 1) // 2 + (j - i)
-                    else:
-                        row = ROW_D[dist] + i * 9 + j
-                    put(row, value)
-                    count += 1
-        for i in range(PARAMS):
-            put(ROW_Q + i, jac(k, 0, i) * wt(k, 0) + jac(k, 1, i) * wt(k, 1))
-            count += 1
-        size = sizes[k]
-        for row in range(count, size):
-            put(row, jnp.zeros((8, LANES), f32))
+
+    def part_of_band(half, sizes):
+        starts = [sum(sizes[:k]) for k in range(len(sizes))]
         for b in range(8):
-            piece = rows[pl.ds(8 * starts[k] + b, size, stride=8), :]
-            for n, part in enumerate(split3(piece)):
-                wide[n, starts[k] : starts[k] + size, b * LANES : (b + 1) * LANES] = part
-        hot = hots[k]
-        got = dot_nt(wide[0, starts[k] : starts[k] + size, :], hot)
-        got = got + dot_nt(wide[1, starts[k] : starts[k] + size, :], hot)
-        got = got + dot_nt(wide[2, starts[k] : starts[k] + size, :], hot)
-        if out is None:
-            out = got
-        else:
-            out = jnp.concatenate([out[0:size] + got, out[size:]], axis=0)
-    core = core_ref[0]
-    low, high = out[0:HALF], out[HALF:BAND]
-    keep_ref[...] = jnp.where(core == 0, low, high)
-    give_ref[...] = jnp.where(core == 0, high, low)
+            cam_b = jnp.broadcast_to(cam[b : b + 1, :], (LANES, LANES))
+            for k in range(len(sizes)):
+                hots[k, :, b * LANES : (b + 1) * LANES] = (
+                    (camera_of == (cam_b + k) % LANES).astype(f32).astype(bf16)
+                )
+        out = None
+        for k, size in enumerate(sizes):
+            seen = set()
+
+            def wanted(row):
+                return 0 <= row - HALF * half < HALF
+
+            def put(row, value, k=k, seen=seen):
+                local = row - HALF * half
+                seen.add(local)
+                at = 8 * (starts[k] + local)
+                rows[at : at + 8, :] = value
+
+            for dist in range(SLOTS - k):
+                other = k + dist
+                last = DIAG if dist == 0 else ROW_D[dist] + 81
+                start = 0 if dist == 0 else ROW_D[dist]
+                if not any(wanted(row) for row in range(start, last)):
+                    continue
+                mix = [[None, None], [None, None]]
+                for m in range(2):
+                    for n in range(2):
+                        if dist == 0 and n < m:
+                            mix[m][n] = mix[n][m]
+                            continue
+                        acc = proj(k, m, 0) * proj(other, n, 0)
+                        acc = acc + proj(k, m, 1) * proj(other, n, 1)
+                        acc = acc + proj(k, m, 2) * proj(other, n, 2)
+                        same = dist == 0 and m == n
+                        mix[m][n] = (1.0 - acc) if same else -acc
+                for j in range(PARAMS):
+                    left = [
+                        mix[m][0] * jac(other, 0, j) + mix[m][1] * jac(other, 1, j)
+                        for m in range(2)
+                    ]
+                    for i in range(PARAMS):
+                        if dist == 0:
+                            row = i * 9 - i * (i - 1) // 2 + (j - i)
+                        else:
+                            row = ROW_D[dist] + i * 9 + j
+                        if (dist == 0 and i > j) or not wanted(row):
+                            continue
+                        put(row, jac(k, 0, i) * left[0] + jac(k, 1, i) * left[1])
+            for i in range(PARAMS):
+                if wanted(ROW_Q + i):
+                    put(ROW_Q + i, jac(k, 0, i) * wt(k, 0) + jac(k, 1, i) * wt(k, 1))
+            for local in range(size):
+                if local not in seen:
+                    rows[8 * (starts[k] + local) : 8 * (starts[k] + local) + 8, :] = jnp.zeros(
+                        (8, LANES), f32
+                    )
+            at = slice(starts[k], starts[k] + size)
+            for b in range(8):
+                piece = rows[pl.ds(8 * starts[k] + b, size, stride=8), :]
+                for n, part in enumerate(split3(piece)):
+                    wide[n, at, b * LANES : (b + 1) * LANES] = part
+            hot = hots[k]
+            got = dot_nt(wide[0, at, :], hot)
+            got = got + dot_nt(wide[1, at, :], hot)
+            got = got + dot_nt(wide[2, at, :], hot)
+            if out is None:
+                out = got
+            elif size == out.shape[0]:
+                out = out + got
+            else:
+                out = jnp.concatenate([out[:size] + got, out[size:]], axis=0)
+        out_ref[...] = out[0:HALF]
+
+    @pl.when(half_ref[0] == 0)
+    def _():
+        part_of_band(0, [160, 160, 144, 64])
+
+    @pl.when(half_ref[0] == 1)
+    def _():
+        part_of_band(1, [160, 64])
 
 
 def factor(size, diag, side, side_chunks):
@@ -723,23 +742,21 @@
     )(owner_map, damping, jac, jp, res, cam_ids, obs_count, clus, prev)
 
 
-def run_band(core, recv):
+def run_band(half, recv, name):
     return pl.pallas_call(
         band_kernel,
-        out_shape=(
-            jax.ShapeDtypeStruct((HALF, LANES), f32),
-            jax.ShapeDtypeStruct((HALF, LANES), f32),
-        ),
+        out_shape=jax.ShapeDtypeStruct((HALF, LANES), f32),
         in_specs=[smem(), vmem()],
-        out_specs=(vmem(), vmem()),
+        out_specs=vmem(),
         scratch_shapes=[
-            pltpu.VMEM((736 * 8, LANES), f32),
-            pltpu.VMEM((3, 736, 1024), bf16),
+            pltpu.VMEM((528 * 8, LANES), f32),
+            pltpu.VMEM((3, 528, 1024), bf16),
             pltpu.VMEM((4, LANES, 1024), bf16),
         ],
         compiler_params=params(20),
-        name="band",
-    )(core, recv)
+        cost_estimate=pl.CostEstimate(flops=4 * 10**8, bytes_accessed=10**7, transcendentals=0),
+        name=name,
+    )(half, recv)
 
 
 def run_solve(core, damping, mine, other):
@@ -776,9 +793,9 @@
     )(everything, jac, real, where)
 
 
-def sum_over_points(keep, give, ring):
+def sum_over_points(keep, given, ring):
     swap = [(i, i ^ 1) for i in range(ring)]
-    half = keep + lax.ppermute(give, "pt", swap)
+    half = keep + given
     moved = [lax.ppermute(half, "pt", [(i, i ^ (2 * d)) for i in range(ring)]) for d in (1, 2, 3)]
     mine = (half + moved[0]) + (moved[1] + moved[2])
     return mine, lax.ppermute(mine, "pt", swap)
@@ -801,8 +818,12 @@
         prev_step.transpose(1, 0, 2).reshape(PARAMS * 16, LANES),
     )
     recv = lax.all_to_all(send, "cl", split_axis=0, concat_axis=0, tiled=True)
-    keep, give = run_band(core, recv.reshape(16 * PACK, LANES))
-    mine, other = sum_over_points(keep, give, lax.axis_size("pt"))
+    recv = recv.reshape(16 * PACK, LANES)
+    ring = lax.axis_size("pt")
+    given = lax.ppermute(
+        run_band(1 - core, recv, "band_give"), "pt", [(i, i ^ 1) for i in range(ring)]
+    )
+    mine, other = sum_over_points(run_band(core, recv, "band_keep"), given, ring)
     step, cast = run_solve(core, damping, mine, other)
     everything = lax.all_to_all(cast, "cl", split_axis=0, concat_axis=0, tiled=True)
     point_step = run_update(everything.reshape(256, LANES), jac, real, where)

time: 60.8 us -> 59.8 us (0.984)
  waiting for transfers between devices: 26 us -> 23.9 us
  Pallas kernels: 16.5 us -> 17.3 us
    ppermute x1, waiting for transfers between devices: 1.26 us -> 0.01 us  [per_device(): lax.ppermute(run_band(1 - core, recv, 'band_give'), 'pt', [(i, i ^ 1) for...]
    ppermute x3, waiting for transfers between devices: 5.4 us -> 4.55 us  [sum_over_points(): lax.ppermute(half, 'pt', [(i, i ^ 2 * d) for i in range(ring)])]
    pallas_call x1 -> x2, Pallas kernels: 2.96 us -> 3.72 us  [run_band(): pl.pallas_call(band_kernel, out_shape=jax.ShapeDtypeStruct((HALF, LANES),...]
  transfers between devices with their start and end apart: 7 -> 7, of which waited for: 6 -> 5; matrix products, arithmetic and copies ran while one was open for 1% -> 1% of each run, Pallas kernels for 0% -> 4%
where the time goes in v5:
time: 59.8 us; the launch traced here: 59.5 us
  waiting for transfers between devices  23.9 us (40%)
  Pallas kernels  17.3 us (29%)
  starting transfers between devices  16.3 us (27%)
  between operations  1.39 us (2%)
  local copies, waits for them, and re-layouts  0.61 us (1%)
    all_to_all x1, waiting for transfers between devices, per_device(): recv = lax.all_to_all(send, 'cl', split_axis=0, concat_axis=0, tiled=True)  10.8 us
    pallas_call x1, Pallas kernels, run_solve(): pl.pallas_call(solve_kernel, out_shape=(jax.ShapeDtypeStruct((PARAMS, LAN...  8.55 us
    all_to_all x1, starting transfers between devices, per_device(): recv = lax.all_to_all(send, 'cl', split_axis=0, concat_axis=0, tiled=True)  7.97 us
    all_to_all x1, waiting for transfers between devices, per_device(): lax.all_to_all(cast, 'cl', split_axis=0, concat_axis=0, tiled=True)  7.34 us
    ppermute x3, waiting for transfers between devices, sum_over_points(): lax.ppermute(half, 'pt', [(i, i ^ 2 * d) for i in range(ring)])  4.55 us
    ppermute x3, starting transfers between devices, sum_over_points(): lax.ppermute(half, 'pt', [(i, i ^ 2 * d) for i in range(ring)])  4.33 us
    pallas_call x1, Pallas kernels, run_points(): pl.pallas_call(points_kernel, out_shape=(jax.ShapeDtypeStruct((16, PACK,...  3.93 us
    pallas_call x2, Pallas kernels, run_band(): pl.pallas_call(band_kernel, out_shape=jax.ShapeDtypeStruct((HALF, LANES),...  3.72 us
  transfers between devices with their start and end apart: 7, of which 5 were waited for; matrix products, arithmetic and copies ran while one was open for 1% of the time, Pallas kernels for 4%

profile of v5, /device:TPU:0, one launch (start us, length us, event | category | flops | bytes accessed | tf_op | source)
XLA Modules:
  0.0 59.5 jit_solution(15098415809384560229)
XLA Ops:
  1.3 3.9 %points.1 = (f32[16,56,128]{2,1,0:T(8,128)}, f32[57,256]{1,0:T(8,128)}, f32[2,72,256]{2,1,0:T(8,128)}, s32[10,256]{1,0:T(8,128)}) custom-call(s32[16]{0:T(128)} %owner_ref.1, f32[1]{0:T(128)S(6)} %copy.12.damp_ref, f32[72,2,256]{2,1,0:T(2,128)} %bitcast.19, f32[24,2,256]{2,1,0:T(2,128)} %bitcast.21, f32[8,2,256]{2,1,0:T(2,128)} %bitcast.22, ...), custom_call_target="tpu_custom_call" | custom-call | tf_op jit(solution)/shard_map/points/pallas_call | solution.py:718
  5.2 8.0 %all-to-all-start = ((f32[16,56,128]{2,1,0:T(8,128)}), f32[16,56,128]{2,1,0:T(8,128)S(1)}, u32[]{:S(2)}, u32[]{:S(2)}) async-start(f32[16,56,128]{2,1,0:T(8,128)} %get-tuple-element.8), calls=%async_computation | async-start | bytes 917504 | tf_op jit(solution)/shard_map/all_to_all | solution.py:820
  13.2 10.8 %all-to-all-done = f32[16,56,128]{2,1,0:T(8,128)S(1)} async-done(((f32[16,56,128]{2,1,0:T(8,128)}), f32[16,56,128]{2,1,0:T(8,128)S(1)}, u32[]{:S(2)}, u32[]{:S(2)}) %all-to-all-start) | async-done | bytes 458784 | tf_op jit(solution)/shard_map/all_to_all | solution.py:820
  24.0 1.3 %band_give.1 = f32[152,128]{1,0:T(8,128)S(1)} custom-call(s32[1]{0:T(128)S(6)} %sub.3.half_ref, f32[896,128]{1,0:T(8,128)S(1)} %bitcast.16), custom_call_target="tpu_custom_call" | custom-call | flops 400000000 | bytes 10000000 | tf_op jit(solution)/shard_map/band_give/pallas_call | solution.py:746
  25.3 0.1 collective-permute-start
  25.4 2.4 %band_keep.1 = f32[152,128]{1,0:T(8,128)S(1)} custom-call(s32[1]{0:T(128)} %bitcast.half_ref.core_ref, f32[896,128]{1,0:T(8,128)S(1)} %bitcast.17), custom_call_target="tpu_custom_call" | custom-call | flops 400000000 | bytes 10000000 | tf_op jit(solution)/shard_map/band_keep/pallas_call | solution.py:746
  27.8 0.0 collective-permute-done
  27.8 3.3 %collective-permute-start.2 = (f32[152,128]{1,0:T(8,128)S(1)}, f32[152,128]{1,0:T(8,128)S(1)}, u32[]{:S(2)}, u32[]{:S(2)}) collective-permute-start(f32[152,128]{1,0:T(8,128)S(1)} %add.17), channel_id=1, source_target_pairs={{0,64},{16,80},{32,96},{48,112},{64,0},{80,16},{96,32},{112,48},{1... | collective-permute-start | bytes 233480 | tf_op jit(solution)/shard_map/ppermute | solution.py:799
  31.1 1.1 %collective-permute-start.3 = (f32[152,128]{1,0:T(8,128)S(1)}, f32[152,128]{1,0:T(8,128)S(1)}, u32[]{:S(2)}, u32[]{:S(2)}) collective-permute-start(f32[152,128]{1,0:T(8,128)S(1)} %add.17), channel_id=1, source_target_pairs={{0,96},{16,112},{32,64},{48,80},{64,32},{80,48},{96,0},{112,16},{1... | collective-permute-start | bytes 233480 | tf_op jit(solution)/shard_map/ppermute | solution.py:799
  32.2 0.0 collective-permute-start.1
  32.2 1.6 %collective-permute-done.2 = f32[152,128]{1,0:T(8,128)S(1)} collective-permute-done((f32[152,128]{1,0:T(8,128)S(1)}, f32[152,128]{1,0:T(8,128)S(1)}, u32[]{:S(2)}, u32[]{:S(2)}) %collective-permute-start.2) | collective-permute-done | bytes 77856 | tf_op jit(solution)/shard_map/ppermute | solution.py:799
  33.8 2.9 %collective-permute-done.3 = f32[152,128]{1,0:T(8,128)S(1)} collective-permute-done((f32[152,128]{1,0:T(8,128)S(1)}, f32[152,128]{1,0:T(8,128)S(1)}, u32[]{:S(2)}, u32[]{:S(2)}) %collective-permute-start.3) | collective-permute-done | bytes 77856 | tf_op jit(solution)/shard_map/ppermute | solution.py:799
  36.7 0.0 collective-permute-done.1
  36.8 0.3 collective-permute-start.4
  37.0 1.3 %collective-permute-done.4.other_ref = f32[152,128]{1,0:T(8,128)S(1)} collective-permute-done((f32[152,128]{1,0:T(8,128)S(1)}, f32[152,128]{1,0:T(8,128)S(1)}, u32[]{:S(2)}, u32[]{:S(2)}) %collective-permute-start.4) | collective-permute-done | bytes 77856 | tf_op jit(solution)/shard_map/ppermute | solution.py:801
  38.3 8.6 %solve.1 = (f32[9,128]{1,0:T(8,128)S(1)}, f32[16,16,128]{2,1,0:T(8,128)}) custom-call(s32[1]{0:T(128)} %bitcast.half_ref.core_ref, f32[1]{0:T(128)S(6)} %copy.12.damp_ref, f32[152,128]{1,0:T(8,128)S(1)} %add_add_fusion.mine_ref, f32[152,128]{1,0:T(8,128)S(1)} %collective-permute-done.4.other_ref), custom_call_target="tpu_custom_call" | custom-call | tf_op jit(solution)/shard_map/solve/pallas_call | solution.py:763
  46.8 0.0 copy-start
  46.8 0.0 copy-start.1
  46.8 3.6 %all-to-all-start.1 = ((f32[16,16,128]{2,1,0:T(8,128)}), f32[16,16,128]{2,1,0:T(8,128)S(1)}, u32[]{:S(2)}, u32[]{:S(2)}) async-start(f32[16,16,128]{2,1,0:T(8,128)} %get-tuple-element.10), calls=%async_computation.1 | async-start | bytes 262144 | tf_op jit(solution)/shard_map/all_to_all | solution.py:828
  50.5 0.0 copy-start.2
  50.5 0.6 %copy.11 = f32[1,9,128]{2,0,1:T(1,128)} copy(f32[1,9,128]{2,1,0:T(8,128)S(1)} %bitcast.18) | data formatting | bytes 9216
  51.1 7.3 %all-to-all-done.1 = f32[16,16,128]{2,1,0:T(8,128)S(1)} async-done(((f32[16,16,128]{2,1,0:T(8,128)}), f32[16,16,128]{2,1,0:T(8,128)S(1)}, u32[]{:S(2)}, u32[]{:S(2)}) %all-to-all-start.1) | async-done | bytes 131104 | tf_op jit(solution)/shard_map/all_to_all | solution.py:828
  58.4 0.0 copy-done
  58.4 0.0 copy-done.1
  58.5 0.0 copy-done.2
  58.5 1.1 %update.1 = f32[3,256]{1,0:T(4,128)} custom-call(f32[256,128]{1,0:T(8,128)S(1)} %bitcast.15, f32[2,72,256]{2,1,0:T(8,128)S(1)} %copy-done, f32[57,256]{1,0:T(8,128)S(1)} %copy-done.1, s32[10,256]{1,0:T(8,128)S(1)} %copy-done.2), custom_call_target="tpu_custom_call" | custom-call | tf_op jit(solution)/shard_map/update/pallas_call | solution.py:785
  (2 shorter events, 0.0 us)
Async XLA Ops:
  5.2 18.8 %all-to-all-start = ((f32[16,56,128]{2,1,0:T(8,128)}), f32[16,56,128]{2,1,0:T(8,128)S(1)}, u32[]{:S(2)}, u32[]{:S(2)}) async-start(f32[16,56,128]{2,1,0:T(8,128)} %get-tuple-element.8), calls=%async_computation | async-start | bytes 917504 | tf_op jit(solution)/shard_map/all_to_all | solution.py:820
  25.3 2.6 %collective-permute-start = (f32[152,128]{1,0:T(8,128)S(1)}, f32[152,128]{1,0:T(8,128)S(1)}, u32[]{:S(2)}, u32[]{:S(2)}) collective-permute-start(f32[152,128]{1,0:T(8,128)S(1)} %band_give.1), channel_id=1, source_target_pairs={{0,16},{16,0},{32,48},{48,32},{64,80},{80,64},{96,112},{112,96},{1... | collective-permute-start | bytes 233480 | tf_op jit(solution)/shard_map/ppermute | solution.py:823
  27.8 6.0 %collective-permute-start.2 = (f32[152,128]{1,0:T(8,128)S(1)}, f32[152,128]{1,0:T(8,128)S(1)}, u32[]{:S(2)}, u32[]{:S(2)}) collective-permute-start(f32[152,128]{1,0:T(8,128)S(1)} %add.17), channel_id=1, source_target_pairs={{0,64},{16,80},{32,96},{48,112},{64,0},{80,16},{96,32},{112,48},{1... | collective-permute-start | bytes 233480 | tf_op jit(solution)/shard_map/ppermute | solution.py:799
  31.1 5.6 %collective-permute-start.3 = (f32[152,128]{1,0:T(8,128)S(1)}, f32[152,128]{1,0:T(8,128)S(1)}, u32[]{:S(2)}, u32[]{:S(2)}) collective-permute-start(f32[152,128]{1,0:T(8,128)S(1)} %add.17), channel_id=1, source_target_pairs={{0,96},{16,112},{32,64},{48,80},{64,32},{80,48},{96,0},{112,16},{1... | collective-permute-start | bytes 233480 | tf_op jit(solution)/shard_map/ppermute | solution.py:799
  32.2 4.6 %collective-permute-start.1 = (f32[152,128]{1,0:T(8,128)S(1)}, f32[152,128]{1,0:T(8,128)S(1)}, u32[]{:S(2)}, u32[]{:S(2)}) collective-permute-start(f32[152,128]{1,0:T(8,128)S(1)} %add.17), channel_id=1, source_target_pairs={{0,32},{16,48},{32,0},{48,16},{64,96},{80,112},{96,64},{112,80},{1... | collective-permute-start | bytes 233480 | tf_op jit(solution)/shard_map/ppermute | solution.py:799
  36.8 1.5 %collective-permute-start.4 = (f32[152,128]{1,0:T(8,128)S(1)}, f32[152,128]{1,0:T(8,128)S(1)}, u32[]{:S(2)}, u32[]{:S(2)}) collective-permute-start(f32[152,128]{1,0:T(8,128)S(1)} %add_add_fusion.mine_ref), channel_id=1, source_target_pairs={{0,16},{16,0},{32,48},{48,32},{64,80},{80,64},{96,112},{112,96},{1... | collective-permute-start | bytes 233480 | tf_op jit(solution)/shard_map/ppermute | solution.py:801
  46.8 11.6 %copy-start = (f32[2,72,256]{2,1,0:T(8,128)S(1)}, f32[2,72,256]{2,1,0:T(8,128)}, u32[]{:S(2)}) copy-start(f32[2,72,256]{2,1,0:T(8,128)} %get-tuple-element.11.jac_ref) | copy-start | bytes 442372
  46.8 11.6 %copy-start.1 = (f32[57,256]{1,0:T(8,128)S(1)}, f32[57,256]{1,0:T(8,128)}, u32[]{:S(2)}) copy-start(f32[57,256]{1,0:T(8,128)} %get-tuple-element.12.real_ref) | copy-start | bytes 175108
  46.8 11.6 %all-to-all-start.1 = ((f32[16,16,128]{2,1,0:T(8,128)}), f32[16,16,128]{2,1,0:T(8,128)S(1)}, u32[]{:S(2)}, u32[]{:S(2)}) async-start(f32[16,16,128]{2,1,0:T(8,128)} %get-tuple-element.10), calls=%async_computation.1 | async-start | bytes 262144 | tf_op jit(solution)/shard_map/all_to_all | solution.py:828
  50.5 8.0 %copy-start.2 = (s32[10,256]{1,0:T(8,128)S(1)}, s32[10,256]{1,0:T(8,128)}, u32[]{:S(2)}) copy-start(s32[10,256]{1,0:T(8,128)} %get-tuple-element.13.where_ref) | copy-start | bytes 30724

commit v6 on v5

--- a/solution.py
+++ b/solution.py
@@ -446,7 +446,7 @@
 
 
 def solve_kernel(
-    core_ref, damp_ref, mine_ref, other_ref, step_ref, cast_ref, rep, back, dmat, smat, xrow, whole
+    core_ref, damp_ref, mine_ref, other_ref, step_ref, cast_ref, rep, back, xrow, whole
 ):
     lane = iota((8, LANES), 1)
     sub = iota((8, LANES), 0)
@@ -560,34 +560,12 @@
     odd_inverse = factor(UNK, odd_diag, odd_side, (0,))
     advance_wide(odd_side, diag, side, lane, whole, 1, 0)
 
-    def store(diag, side):
-        for a in range(UNK):
-            for v in range(a // 8, 4):
-                dmat[a, 8 * v : 8 * v + 8, :] = diag[a][v]
-            smat[a] = side[a][0]
-
-    def load():
-        diag = [
-            [dmat[a, 8 * v : 8 * v + 8, :] if v >= a // 8 else None for v in range(4)]
-            for a in range(UNK)
-        ]
-        return diag, [[smat[a]] for a in range(UNK)]
-
-    store(diag, side)
-
-    def level(step, carry):
-        stride = lax.shift_left(jnp.int32(1), step)
-        diag, side = load()
-        factor(UNK, diag, side, (0,))
-        work = side
-        diag, side = load()
-        advance_wide(work, diag, side, lane, whole, stride, stride)
-        store(diag, side)
-        return carry
-
-    lax.fori_loop(0, 3, level, jnp.int32(0))
-
-    diag, side = load()
+    for step in range(3):
+        work_diag = [list(line_of) for line_of in diag]
+        work = [list(line_of) for line_of in side]
+        factor(UNK, work_diag, work, (0,))
+        advance_wide(work, diag, side, lane, whole, 2**step, 2**step)
+
     from_left = [lanes_from(side[a][0], few + NODES * (which % 4)) for a in range(UNK)]
     from_right = [lanes_from(side[a][0], few + NODES * (4 + which % 4)) for a in range(UNK)]
     both = [[p + q] for p, q in zip(from_left, from_right)]
@@ -771,8 +749,6 @@
         scratch_shapes=[
             pltpu.VMEM((4, BAND, LANES), f32),
             pltpu.VMEM((3, BAND, LANES), f32),
-            pltpu.VMEM((UNK, 32, LANES), f32),
-            pltpu.VMEM((UNK, 8, LANES), f32),
             pltpu.VMEM((32, LANES), f32),
             pltpu.VMEM((2 * UNK * 32, LANES), f32),
         ],

time: 59.8 us -> 59.5 us (level)
  no operation moved by 1% of the time
where the time goes in v6:
time: 59.5 us; the launch traced here: 59.1 us
  waiting for transfers between devices  23.9 us (40%)
  Pallas kernels  16.9 us (28%)
  starting transfers between devices  16.3 us (27%)
  between operations  1.39 us (2%)
  local copies, waits for them, and re-layouts  0.61 us (1%)
    all_to_all x1, waiting for transfers between devices, per_device(): recv = lax.all_to_all(send, 'cl', split_axis=0, concat_axis=0, tiled=True)  10.8 us
    pallas_call x1, Pallas kernels, run_solve(): pl.pallas_call(solve_kernel, out_shape=(jax.ShapeDtypeStruct((PARAMS, LAN...  8.18 us
    all_to_all x1, starting transfers between devices, per_device(): recv = lax.all_to_all(send, 'cl', split_axis=0, concat_axis=0, tiled=True)  7.97 us
    all_to_all x1, waiting for transfers between devices, per_device(): lax.all_to_all(cast, 'cl', split_axis=0, concat_axis=0, tiled=True)  7.34 us
    ppermute x3, waiting for transfers between devices, sum_over_points(): lax.ppermute(half, 'pt', [(i, i ^ 2 * d) for i in range(ring)])  4.55 us
    ppermute x3, starting transfers between devices, sum_over_points(): lax.ppermute(half, 'pt', [(i, i ^ 2 * d) for i in range(ring)])  4.33 us
    pallas_call x1, Pallas kernels, run_points(): pl.pallas_call(points_kernel, out_shape=(jax.ShapeDtypeStruct((16, PACK,...  3.93 us
    pallas_call x2, Pallas kernels, run_band(): pl.pallas_call(band_kernel, out_shape=jax.ShapeDtypeStruct((HALF, LANES),...  3.72 us
  transfers between devices with their start and end apart: 7, of which 5 were waited for; matrix products, arithmetic and copies ran while one was open for 1% of the time, Pallas kernels for 4%

profile of v6, /device:TPU:0, one launch (start us, length us, event | category | flops | bytes accessed | tf_op | source)
XLA Modules:
  0.0 59.1 jit_solution(1614545879958376209)
XLA Ops:
  1.3 3.9 %points.1 = (f32[16,56,128]{2,1,0:T(8,128)}, f32[57,256]{1,0:T(8,128)}, f32[2,72,256]{2,1,0:T(8,128)}, s32[10,256]{1,0:T(8,128)}) custom-call(s32[16]{0:T(128)} %owner_ref.1, f32[1]{0:T(128)S(6)} %copy.12.damp_ref, f32[72,2,256]{2,1,0:T(2,128)} %bitcast.19, f32[24,2,256]{2,1,0:T(2,128)} %bitcast.21, f32[8,2,256]{2,1,0:T(2,128)} %bitcast.22, ...), custom_call_target="tpu_custom_call" | custom-call | tf_op jit(solution)/shard_map/points/pallas_call | solution.py:696
  5.2 8.0 %all-to-all-start = ((f32[16,56,128]{2,1,0:T(8,128)}), f32[16,56,128]{2,1,0:T(8,128)S(1)}, u32[]{:S(2)}, u32[]{:S(2)}) async-start(f32[16,56,128]{2,1,0:T(8,128)} %get-tuple-element.8), calls=%async_computation | async-start | bytes 917504 | tf_op jit(solution)/shard_map/all_to_all | solution.py:796
  13.2 10.8 %all-to-all-done = f32[16,56,128]{2,1,0:T(8,128)S(1)} async-done(((f32[16,56,128]{2,1,0:T(8,128)}), f32[16,56,128]{2,1,0:T(8,128)S(1)}, u32[]{:S(2)}, u32[]{:S(2)}) %all-to-all-start) | async-done | bytes 458784 | tf_op jit(solution)/shard_map/all_to_all | solution.py:796
  24.0 1.3 %band_give.1 = f32[152,128]{1,0:T(8,128)S(1)} custom-call(s32[1]{0:T(128)S(6)} %sub.3.half_ref, f32[896,128]{1,0:T(8,128)S(1)} %bitcast.16), custom_call_target="tpu_custom_call" | custom-call | flops 400000000 | bytes 10000000 | tf_op jit(solution)/shard_map/band_give/pallas_call | solution.py:724
  25.3 0.1 collective-permute-start
  25.4 2.4 %band_keep.1 = f32[152,128]{1,0:T(8,128)S(1)} custom-call(s32[1]{0:T(128)} %bitcast.half_ref.core_ref, f32[896,128]{1,0:T(8,128)S(1)} %bitcast.17), custom_call_target="tpu_custom_call" | custom-call | flops 400000000 | bytes 10000000 | tf_op jit(solution)/shard_map/band_keep/pallas_call | solution.py:724
  27.8 0.0 collective-permute-done
  27.8 3.3 %collective-permute-start.2 = (f32[152,128]{1,0:T(8,128)S(1)}, f32[152,128]{1,0:T(8,128)S(1)}, u32[]{:S(2)}, u32[]{:S(2)}) collective-permute-start(f32[152,128]{1,0:T(8,128)S(1)} %add.17), channel_id=1, source_target_pairs={{0,64},{16,80},{32,96},{48,112},{64,0},{80,16},{96,32},{112,48},{1... | collective-permute-start | bytes 233480 | tf_op jit(solution)/shard_map/ppermute | solution.py:775
  31.1 1.1 %collective-permute-start.3 = (f32[152,128]{1,0:T(8,128)S(1)}, f32[152,128]{1,0:T(8,128)S(1)}, u32[]{:S(2)}, u32[]{:S(2)}) collective-permute-start(f32[152,128]{1,0:T(8,128)S(1)} %add.17), channel_id=1, source_target_pairs={{0,96},{16,112},{32,64},{48,80},{64,32},{80,48},{96,0},{112,16},{1... | collective-permute-start | bytes 233480 | tf_op jit(solution)/shard_map/ppermute | solution.py:775
  32.2 0.0 collective-permute-start.1
  32.2 1.6 %collective-permute-done.2 = f32[152,128]{1,0:T(8,128)S(1)} collective-permute-done((f32[152,128]{1,0:T(8,128)S(1)}, f32[152,128]{1,0:T(8,128)S(1)}, u32[]{:S(2)}, u32[]{:S(2)}) %collective-permute-start.2) | collective-permute-done | bytes 77856 | tf_op jit(solution)/shard_map/ppermute | solution.py:775
  33.8 2.9 %collective-permute-done.3 = f32[152,128]{1,0:T(8,128)S(1)} collective-permute-done((f32[152,128]{1,0:T(8,128)S(1)}, f32[152,128]{1,0:T(8,128)S(1)}, u32[]{:S(2)}, u32[]{:S(2)}) %collective-permute-start.3) | collective-permute-done | bytes 77856 | tf_op jit(solution)/shard_map/ppermute | solution.py:775
  36.7 0.0 collective-permute-done.1
  36.8 0.3 collective-permute-start.4
  37.0 1.3 %collective-permute-done.4.other_ref = f32[152,128]{1,0:T(8,128)S(1)} collective-permute-done((f32[152,128]{1,0:T(8,128)S(1)}, f32[152,128]{1,0:T(8,128)S(1)}, u32[]{:S(2)}, u32[]{:S(2)}) %collective-permute-start.4) | collective-permute-done | bytes 77856 | tf_op jit(solution)/shard_map/ppermute | solution.py:777
  38.3 8.2 %solve.1 = (f32[9,128]{1,0:T(8,128)S(1)}, f32[16,16,128]{2,1,0:T(8,128)}) custom-call(s32[1]{0:T(128)} %bitcast.half_ref.core_ref, f32[1]{0:T(128)S(6)} %copy.12.damp_ref, f32[152,128]{1,0:T(8,128)S(1)} %add_add_fusion.mine_ref, f32[152,128]{1,0:T(8,128)S(1)} %collective-permute-done.4.other_ref), custom_call_target="tpu_custom_call" | custom-call | tf_op jit(solution)/shard_map/solve/pallas_call | solution.py:741
  46.5 0.0 copy-start
  46.5 0.0 copy-start.1
  46.5 3.6 %all-to-all-start.1 = ((f32[16,16,128]{2,1,0:T(8,128)}), f32[16,16,128]{2,1,0:T(8,128)S(1)}, u32[]{:S(2)}, u32[]{:S(2)}) async-start(f32[16,16,128]{2,1,0:T(8,128)} %get-tuple-element.10), calls=%async_computation.1 | async-start | bytes 262144 | tf_op jit(solution)/shard_map/all_to_all | solution.py:804
  50.1 0.0 copy-start.2
  50.1 0.6 %copy.11 = f32[1,9,128]{2,0,1:T(1,128)} copy(f32[1,9,128]{2,1,0:T(8,128)S(1)} %bitcast.18) | data formatting | bytes 9216
  50.7 7.3 %all-to-all-done.1 = f32[16,16,128]{2,1,0:T(8,128)S(1)} async-done(((f32[16,16,128]{2,1,0:T(8,128)}), f32[16,16,128]{2,1,0:T(8,128)S(1)}, u32[]{:S(2)}, u32[]{:S(2)}) %all-to-all-start.1) | async-done | bytes 131104 | tf_op jit(solution)/shard_map/all_to_all | solution.py:804
  58.1 0.0 copy-done
  58.1 0.0 copy-done.1
  58.1 0.0 copy-done.2
  58.1 1.1 %update.1 = f32[3,256]{1,0:T(4,128)} custom-call(f32[256,128]{1,0:T(8,128)S(1)} %bitcast.15, f32[2,72,256]{2,1,0:T(8,128)S(1)} %copy-done, f32[57,256]{1,0:T(8,128)S(1)} %copy-done.1, s32[10,256]{1,0:T(8,128)S(1)} %copy-done.2), custom_call_target="tpu_custom_call" | custom-call | tf_op jit(solution)/shard_map/update/pallas_call | solution.py:761
  (2 shorter events, 0.0 us)
Async XLA Ops:
  5.2 18.8 %all-to-all-start = ((f32[16,56,128]{2,1,0:T(8,128)}), f32[16,56,128]{2,1,0:T(8,128)S(1)}, u32[]{:S(2)}, u32[]{:S(2)}) async-start(f32[16,56,128]{2,1,0:T(8,128)} %get-tuple-element.8), calls=%async_computation | async-start | bytes 917504 | tf_op jit(solution)/shard_map/all_to_all | solution.py:796
  25.3 2.6 %collective-permute-start = (f32[152,128]{1,0:T(8,128)S(1)}, f32[152,128]{1,0:T(8,128)S(1)}, u32[]{:S(2)}, u32[]{:S(2)}) collective-permute-start(f32[152,128]{1,0:T(8,128)S(1)} %band_give.1), channel_id=1, source_target_pairs={{0,16},{16,0},{32,48},{48,32},{64,80},{80,64},{96,112},{112,96},{1... | collective-permute-start | bytes 233480 | tf_op jit(solution)/shard_map/ppermute | solution.py:799
  27.8 6.0 %collective-permute-start.2 = (f32[152,128]{1,0:T(8,128)S(1)}, f32[152,128]{1,0:T(8,128)S(1)}, u32[]{:S(2)}, u32[]{:S(2)}) collective-permute-start(f32[152,128]{1,0:T(8,128)S(1)} %add.17), channel_id=1, source_target_pairs={{0,64},{16,80},{32,96},{48,112},{64,0},{80,16},{96,32},{112,48},{1... | collective-permute-start | bytes 233480 | tf_op jit(solution)/shard_map/ppermute | solution.py:775
  31.1 5.6 %collective-permute-start.3 = (f32[152,128]{1,0:T(8,128)S(1)}, f32[152,128]{1,0:T(8,128)S(1)}, u32[]{:S(2)}, u32[]{:S(2)}) collective-permute-start(f32[152,128]{1,0:T(8,128)S(1)} %add.17), channel_id=1, source_target_pairs={{0,96},{16,112},{32,64},{48,80},{64,32},{80,48},{96,0},{112,16},{1... | collective-permute-start | bytes 233480 | tf_op jit(solution)/shard_map/ppermute | solution.py:775
  32.2 4.6 %collective-permute-start.1 = (f32[152,128]{1,0:T(8,128)S(1)}, f32[152,128]{1,0:T(8,128)S(1)}, u32[]{:S(2)}, u32[]{:S(2)}) collective-permute-start(f32[152,128]{1,0:T(8,128)S(1)} %add.17), channel_id=1, source_target_pairs={{0,32},{16,48},{32,0},{48,16},{64,96},{80,112},{96,64},{112,80},{1... | collective-permute-start | bytes 233480 | tf_op jit(solution)/shard_map/ppermute | solution.py:775
  36.8 1.5 %collective-permute-start.4 = (f32[152,128]{1,0:T(8,128)S(1)}, f32[152,128]{1,0:T(8,128)S(1)}, u32[]{:S(2)}, u32[]{:S(2)}) collective-permute-start(f32[152,128]{1,0:T(8,128)S(1)} %add_add_fusion.mine_ref), channel_id=1, source_target_pairs={{0,16},{16,0},{32,48},{48,32},{64,80},{80,64},{96,112},{112,96},{1... | collective-permute-start | bytes 233480 | tf_op jit(solution)/shard_map/ppermute | solution.py:777
  46.5 11.6 %copy-start = (f32[2,72,256]{2,1,0:T(8,128)S(1)}, f32[2,72,256]{2,1,0:T(8,128)}, u32[]{:S(2)}) copy-start(f32[2,72,256]{2,1,0:T(8,128)} %get-tuple-element.11.jac_ref) | copy-start | bytes 442372
  46.5 11.6 %copy-start.1 = (f32[57,256]{1,0:T(8,128)S(1)}, f32[57,256]{1,0:T(8,128)}, u32[]{:S(2)}) copy-start(f32[57,256]{1,0:T(8,128)} %get-tuple-element.12.real_ref) | copy-start | bytes 175108
  46.5 11.6 %all-to-all-start.1 = ((f32[16,16,128]{2,1,0:T(8,128)}), f32[16,16,128]{2,1,0:T(8,128)S(1)}, u32[]{:S(2)}, u32[]{:S(2)}) async-start(f32[16,16,128]{2,1,0:T(8,128)} %get-tuple-element.10), calls=%async_computation.1 | async-start | bytes 262144 | tf_op jit(solution)/shard_map/all_to_all | solution.py:804
  50.1 8.0 %copy-start.2 = (s32[10,256]{1,0:T(8,128)S(1)}, s32[10,256]{1,0:T(8,128)}, u32[]{:S(2)}) copy-start(s32[10,256]{1,0:T(8,128)} %get-tuple-element.13.where_ref) | copy-start | bytes 30724
